TPU v7x, 128 devices: a whole 4x4x4 slice. The times are simulated.
128 devices in a mesh: row: 8 (over y_hi, x), feat: 16 (over y_lo, z, core).
Axes of the slice: x: 4, y: 4 (y_hi: 2, y_lo: 2; y = y_hi * 2 + y_lo), z: 4, core: 2. Of those that a mesh axis runs over, the one named last changes fastest.
Arguments:
- design_tiles: bfloat16 [8, 8, 8, 48, 128, 128], P('row', None, None, 'feat'), may hold values from -0.078125 to 0.078125
- block_ids: int32 [8, 8, 8, 48], P(None, None, None, 'feat'), may hold values from 0 to 1023, as said below
- responses: bfloat16 [8, 8, 8, 128, 64], P('row'), may hold values from -6 to 6
- live_groups: int32 [8, 8], replicated, may hold values from 0 to 1, as said below
- start_coef: float32 [131072, 64], P('feat'), may hold values from -6 to 6
Outputs:
- coefficients: float32 [131072, 64], P('feat')
Inputs may be any that keep to these rules, and one draw needn't show every extreme that they name: `block_ids`: the 3 entries of a row block that lie in feat index f's positions are distinct feature blocks of the range f * 64 to (f + 1) * 64 - 1. `live_groups`: A group is all live or all empty; every owner has live groups from exactly half of the 8 sources.
All inputs are finite; a program needn't handle non-finite values.
Results may differ from a plain program's by a relative error of at most 0.002.
Values may be sent and summed in bfloat16 or wider, within the bound.
No kernel may reach another device: no remote copies, remote signals or barrier semaphores. Data moves between devices by JAX's collectives and lax.ppermute only.
A program may use at most 64 MiB of HBM per device.

v0:
```python
import jax
import jax.numpy as jnp
from jax import lax
from jax.sharding import PartitionSpec as P

ITERS = 2


step_size = 0.25
ridge_term = 0.05


def huber_weights(predicted, work_resp, live_flags):
    groups, slot_count, block_rows, columns = predicted.shape
    threshold = 1.4 * columns**0.5
    totals = lax.psum(predicted, "feat")
    residual = work_resp.astype(jnp.float32) - totals
    row_norms = jnp.sqrt(jnp.sum(residual * residual, axis=-1))
    weight = live_flags[:, None, None] * threshold / jnp.maximum(row_norms, threshold)
    scaled = (weight[..., None] * residual).astype(jnp.bfloat16)
    return (scaled, weight.astype(jnp.bfloat16))


def body(design_tiles, block_ids, responses, live_groups, start_coef):
    row_place = lax.axis_index("row")
    feat_place = lax.axis_index("feat")
    block_width = design_tiles.shape[-1]
    columns = start_coef.shape[1]
    local_blocks = start_coef.shape[0] // block_width
    local_ids = block_ids - feat_place * local_blocks
    work_tiles = design_tiles[0]
    work_resp = responses[0]
    work_ids = lax.dynamic_index_in_dim(local_ids, row_place, 0, keepdims=False)
    live_flags = lax.dynamic_index_in_dim(live_groups, row_place, 0, keepdims=False).astype(
        jnp.float32
    )
    onehot = (
        work_ids.reshape(-1)[:, None] == jnp.arange(local_blocks, dtype=jnp.int32)[None, :]
    ).astype(jnp.float32)
    tiles_wide = work_tiles.astype(jnp.float32)
    tile_squares = tiles_wide * tiles_wide
    coefficients = start_coef
    for iteration in range(ITERS):
        coef_bf = coefficients.astype(jnp.bfloat16).reshape(local_blocks, block_width, columns)
        picked = coef_bf[work_ids]
        predicted = jnp.einsum(
            "gskif,gskfc->gsic", work_tiles, picked, preferred_element_type=jnp.float32
        )
        scaled, rounded = huber_weights(predicted, work_resp, live_flags)
        partial_grad = jnp.einsum(
            "gskif,gsic->gskfc", work_tiles, scaled, preferred_element_type=jnp.float32
        )
        partial_curv = jnp.einsum(
            "gskif,gsi->gskf",
            tile_squares,
            rounded.astype(jnp.float32),
            precision=lax.Precision.HIGHEST,
        )
        gradient = jnp.einsum(
            "tb,tfc->bfc",
            onehot,
            partial_grad.reshape(-1, block_width, columns),
            precision=lax.Precision.HIGHEST,
        )
        curvature = jnp.einsum(
            "tb,tf->bf",
            onehot,
            partial_curv.reshape(-1, block_width),
            precision=lax.Precision.HIGHEST,
        )
        gradient, curvature = lax.psum((gradient, curvature), "row")
        coefficients = coefficients + step_size * (
            gradient.reshape(-1, columns) - ridge_term * coefficients
        ) / (curvature.reshape(-1, 1) + ridge_term)
    return coefficients


def solution(mesh):
    in_specs = (
        P("row", None, None, "feat", None, None),
        P(None, None, None, "feat"),
        P("row", None, None, None, None),
        P(),
        P("feat", None),
    )
    out_specs = P("feat", None)
    return jax.shard_map(body, mesh=mesh, in_specs=in_specs, out_specs=out_specs, check_vma=False)
```

profile of v0, /device:TPU:0, one launch (start us, length us, event | category | flops | bytes accessed | tf_op | source)
XLA Modules:
  0.0 509.8 jit_solution(7656828350380415054)
XLA Ops:
  6.5 0.0 all-reduce.5.cloned.1.call-start
  6.5 0.7 compare_select_fusion
  7.2 0.1 copy.14
  7.4 0.1 reshape.107
  7.5 1.9 copy_bitcast_fusion.3
  9.4 2.7 gather_fusion
  12.1 8.0 %fusion.16 = f32[8,8,128,64]{2,3,1,0:T(8,128)} fusion(bf16[8,8,3,128,64]{3,4,2,1,0:T(8,128)(2,1)} %bitcast.118, bf16[1,8,8,3,128,128]{5,4,3,2,1,0:T(8,128)(2,1)} %param.5), kind=kOutput, calls=%fused_computation.29 | convolution fusion | flops 402653184 | bytes 11534336 | tf_op jit(solution)/shard_map/gskif,gskfc->gsic/dot_general | solution.py:46
  20.1 0.0 copy-start
  20.1 0.0 all-reduce.5.cloned.1.call-update
  20.1 0.2 all-reduce.7.cloned.1.call-start
  20.4 0.1 copy.13
  20.5 0.1 eq.15
  20.6 0.7 multiply_bitcast_fusion
  21.3 124.6 %all-reduce.5.cloned.1.call-done = f32[8,8,128,64]{2,3,1,0:T(8,128)} async-done(((f32[8,8,128,64]{2,3,1,0:T(8,128)}), f32[8,8,128,64]{2,3,1,0:T(8,128)}) %all-reduce.5.cloned.1.call-update) | async-done | bytes 2097168 | tf_op jit(solution)/shard_map/psum | solution.py:16
  146.0 0.0 copy-done
  146.0 0.0 copy-start.2
  146.0 2.2 multiply_reduce_fusion.1
  148.2 0.1 convert_bitcast_fusion.3
  148.2 0.0 copy-done.2
  148.2 4.1 fusion.8
  152.3 6.2 %fusion.14 = f32[64,128,64]{1,0,2:T(8,128)S(1)} fusion(f32[192,128,64]{1,2,0:T(8,128)S(1)} %bitcast.115, s32[192]{0:T(256)S(1)} %eq.15), kind=kOutput, calls=%fused_computation.17 | convolution fusion | flops 1207971840 | bytes 8389376 | tf_op jit(solution)/shard_map/tb,tfc->bfc/dot_general | solution.py:59
  158.5 2.5 copy.46
  161.0 0.0 all-reduce.7.cloned.1.call-update
  161.1 0.3 all-reduce.9.cloned.1.call-start
  161.3 7.4 %fusion.1 = f32[8,8,1,3,128]{4,2,3,1,0:T(1,128)S(1)} fusion(bf16[1,8,8,3,128,128]{5,4,3,2,1,0:T(8,128)(2,1)} %param.5, bf16[8,8,128,1,1]{2,1,0,3,4:T(8,128)(2,1)S(1)} %get-tuple-element.7), kind=kOutput, calls=%fused_computation.4 | convolution fusion | flops 44040192 | bytes 6406144 | tf_op jit(solution)/shard_map/gskif,gsi->gskf/dot_general | solution.py:53
  168.8 0.2 fusion.31
  169.0 41.4 %psum.44 = f32[64,128]{1,0:T(8,128)S(1)} all-reduce(f32[64,128]{1,0:T(8,128)S(1)} %fusion.31), channel_id=1, replica_groups=mesh['row'=8,'feat'=16] {'row'}, use_global_device_ids=true, to_apply=%region_3.4 | all-reduce | flops 8192 | bytes 65536 | tf_op jit(solution)/shard_map/psum | solution.py:71
  210.4 44.2 %all-reduce.7.cloned.1.call-done = f32[8192,64]{0,1:T(8,128)} async-done(((f32[8192,64]{0,1:T(8,128)}), f32[8192,64]{0,1:T(8,128)}) %all-reduce.7.cloned.1.call-update) | async-done | bytes 2097168 | tf_op jit(solution)/shard_map/psum | solution.py:71
  254.6 2.7 copy_bitcast_fusion.2
  257.3 2.7 gather_fusion.1
  260.0 8.0 %fusion.19 = f32[8,8,128,64]{2,3,1,0:T(8,128)} fusion(bf16[8,8,3,128,64]{3,4,2,1,0:T(8,128)(2,1)} %bitcast.117, bf16[1,8,8,3,128,128]{5,4,3,2,1,0:T(8,128)(2,1)} %param.5), kind=kOutput, calls=%fused_computation.30 | convolution fusion | flops 402653184 | bytes 11534336 | tf_op jit(solution)/shard_map/gskif,gskfc->gsic/dot_general | solution.py:46
  268.0 0.0 all-reduce.9.cloned.1.call-update
  268.0 0.3 all-reduce.11.cloned.1.call-start
  268.3 122.0 %all-reduce.9.cloned.1.call-done = f32[8,8,128,64]{2,3,1,0:T(8,128)} async-done(((f32[8,8,128,64]{2,3,1,0:T(8,128)}), f32[8,8,128,64]{2,3,1,0:T(8,128)}) %all-reduce.9.cloned.1.call-update) | async-done | bytes 2097168 | tf_op jit(solution)/shard_map/psum | solution.py:16
  390.3 2.2 multiply_reduce_fusion
  392.5 0.1 convert_bitcast_fusion.2
  392.5 0.0 copy-done.3
  392.5 4.1 fusion.3
  396.6 6.2 %fusion.12 = f32[64,128,64]{1,0,2:T(8,128)S(1)} fusion(f32[192,128,64]{1,2,0:T(8,128)S(1)} %bitcast.116, s32[192]{0:T(256)S(1)} %eq.15), kind=kOutput, calls=%fused_computation.15 | convolution fusion | flops 1207971840 | bytes 8389376 | tf_op jit(solution)/shard_map/tb,tfc->bfc/dot_general | solution.py:59
  402.8 2.5 copy.45
  405.3 0.0 all-reduce.11.cloned.1.call-update
  405.4 0.0 copy-start.1
  405.4 7.8 %fusion = f32[8,8,1,3,128]{4,2,3,1,0:T(1,128)S(1)} fusion(bf16[1,8,8,3,128,128]{5,4,3,2,1,0:T(8,128)(2,1)} %param.5, bf16[8,8,128,1,1]{2,1,0,3,4:T(8,128)(2,1)S(1)} %get-tuple-element.5), kind=kOutput, calls=%fused_computation.3 | convolution fusion | flops 44040192 | bytes 6406144 | tf_op jit(solution)/shard_map/gskif,gsi->gskf/dot_general | solution.py:53
  413.3 0.2 fusion.30
  413.5 41.4 %psum.47 = f32[64,128]{1,0:T(8,128)S(1)} all-reduce(f32[64,128]{1,0:T(8,128)S(1)} %fusion.30), channel_id=1, replica_groups=mesh['row'=8,'feat'=16] {'row'}, use_global_device_ids=true, to_apply=%region_7.8 | all-reduce | flops 8192 | bytes 65536 | tf_op jit(solution)/shard_map/psum | solution.py:71
  454.9 44.2 %all-reduce.11.cloned.1.call-done = f32[8192,64]{0,1:T(8,128)} async-done(((f32[8192,64]{0,1:T(8,128)}), f32[8192,64]{0,1:T(8,128)}) %all-reduce.11.cloned.1.call-update) | async-done | bytes 2097168 | tf_op jit(solution)/shard_map/psum | solution.py:71
  499.1 0.0 copy-done.1
  499.1 4.2 divide_add_fusion
  (8 shorter events, 0.2 us)
Async XLA Ops:
  6.5 139.4 %all-reduce.5.cloned.1.call-start = ((), (), s32[]{:S(2)}) async-start(), calls=%async_computation | async-start | bytes 4194304 | tf_op jit(solution)/shard_map/psum | solution.py:16
  20.1 125.9 %copy-start = (bf16[1,8,8,128,64]{3,4,2,1,0:T(8,128)(2,1)S(1)}, bf16[1,8,8,128,64]{3,4,2,1,0:T(8,128)(2,1)}, u32[]{:S(2)}) copy-start(bf16[1,8,8,128,64]{3,4,2,1,0:T(8,128)(2,1)} %param.7) | copy-start | bytes 3145732
  20.1 234.5 %all-reduce.7.cloned.1.call-start = ((), (), s32[]{:S(2)}) async-start(), calls=%async_computation.1 | async-start | bytes 4194304 | tf_op jit(solution)/shard_map/psum | solution.py:71
  146.0 2.3 copy-start.2
  161.1 229.2 %all-reduce.9.cloned.1.call-start = ((), (), s32[]{:S(2)}) async-start(), calls=%async_computation.2 | async-start | bytes 4194304 | tf_op jit(solution)/shard_map/psum | solution.py:16
  268.0 231.1 %all-reduce.11.cloned.1.call-start = ((), (), s32[]{:S(2)}) async-start(), calls=%async_computation.3 | async-start | bytes 4194304 | tf_op jit(solution)/shard_map/psum | solution.py:71
  390.3 2.3 copy-start.3
  405.4 93.7 %copy-start.1 = (f32[8192,64]{0,1:T(8,128)S(1)}, f32[8192,64]{0,1:T(8,128)}, u32[]{:S(2)}) copy-start(f32[8192,64]{0,1:T(8,128)} %param.9) | copy-start | bytes 6291460
Sparse Core Ops, SparseCore 0:
  20.2 125.6 all-reduce.4
  161.2 93.3 all-reduce.6
  268.1 122.1 all-reduce.8
  405.5 93.5 all-reduce.10
where the time goes:
time: 510 us
  waiting for transfers between devices  335 us (66%)
  blocking collectives  82.7 us (16%)
  matrix products  52.1 us (10%)
  other arithmetic  14.8 us (3%)
  between operations  13.2 us (3%)
  local copies, waits for them, and re-layouts  11.2 us (2%)
    psum x2, waiting for transfers between devices, huber_weights(): totals = lax.psum(predicted, 'feat')  247 us
    psum x2, waiting for transfers between devices, body(): gradient, curvature = lax.psum((gradient, curvature), 'row')  88.4 us
    psum x2, blocking collectives, body(): gradient, curvature = lax.psum((gradient, curvature), 'row')  82.7 us
    dot_general x2, matrix products, body(): jnp.einsum('gskif,gskfc->gsic', work_tiles, picked, preferred_element_typ...  15.9 us
    dot_general x2, matrix products, body(): jnp.einsum('gskif,gsi->gskf', tile_squares, rounded.astype(jnp.float32),...  15.2 us
    dot_general x2, matrix products, body(): jnp.einsum('tb,tfc->bfc', onehot, partial_grad.reshape(-1, block_width, c...  12.4 us
  transfers between devices with their start and end apart: 4, of which 4 were waited for; matrix products, arithmetic and copies ran while one was open for 3% of the time, Pallas kernels for 0%

commit v1 on v0

v1 whole, which is shorter than its diff:
```python
import jax
import jax.numpy as jnp
from jax import lax
from jax.experimental import pallas as pl
from jax.experimental.pallas import tpu as pltpu
from jax.sharding import PartitionSpec as P

ITERS = 2
STEP_SIZE = 0.25
RIDGE = 0.05
F32 = jnp.float32
BF16 = jnp.bfloat16
VMEM_LIMIT = 48 * 1024 * 1024

LANES = 128
PAD = 16


def params():
    return pltpu.CompilerParams(vmem_limit_bytes=VMEM_LIMIT)


def coef_blocks(start_t):
    columns, features = start_t.shape
    blocks = features // LANES
    step = 16

    def kernel(start_ref, out_ref):
        for b in range(step):
            out_ref[b] = start_ref[:, b * LANES : (b + 1) * LANES].astype(BF16)

    return pl.pallas_call(
        kernel,
        grid=(blocks // step,),
        in_specs=[pl.BlockSpec((columns, step * LANES), lambda i: (0, i))],
        out_specs=pl.BlockSpec((step, columns, LANES), lambda i: (i, 0, 0)),
        out_shape=jax.ShapeDtypeStruct((blocks, columns, LANES), BF16),
        compiler_params=params(),
    )(start_t)


def predict_half(scalars, ids, tiles, coef, dtype):
    row_blocks, kt, rows, width = tiles.shape
    columns = coef.shape[1]
    half = row_blocks // 2
    step = 8
    steps = half // step

    def kernel(scalars_ref, ids_ref, tiles_ref, coef_ref, out_ref):
        base = (scalars_ref[0] * steps + pl.program_id(0)) * step
        for r in range(step):
            total = None
            for k in range(kt):
                block = ids_ref[(base + r) * kt + k]
                part = lax.dot_general(
                    coef_ref[block],
                    tiles_ref[r, k],
                    (((1,), (1,)), ((), ())),
                    preferred_element_type=F32,
                )
                total = part if total is None else total + part
            out_ref[r] = total.astype(dtype)

    return pl.pallas_call(
        kernel,
        grid_spec=pltpu.PrefetchScalarGridSpec(
            num_scalar_prefetch=2,
            grid=(steps,),
            in_specs=[
                pl.BlockSpec((step, kt, rows, width), lambda i, s, d: (s[0] * steps + i, 0, 0, 0)),
                pl.BlockSpec(coef.shape, lambda i, s, d: (0, 0, 0)),
            ],
            out_specs=pl.BlockSpec((step, columns, rows), lambda i, s, d: (i, 0, 0)),
        ),
        out_shape=jax.ShapeDtypeStruct((half, columns, rows), dtype),
        compiler_params=params(),
    )(scalars, ids, tiles, coef)


def weigh(scalars, parts, resp_t, copies):
    sources, count, columns, rows = parts.shape
    threshold = 1.4 * columns**0.5

    def kernel(scalars_ref, parts_ref, resp_ref, out_ref):
        flag = scalars_ref[1].astype(F32)
        lines = []
        for r in range(count):
            predicted = parts_ref[0, r].astype(F32)
            for s in range(1, sources):
                predicted = predicted + parts_ref[s, r].astype(F32)
            residual = resp_ref[r].astype(F32) - predicted
            norm = jnp.sqrt(jnp.sum(residual * residual, axis=0, keepdims=True))
            weight = flag * threshold / jnp.maximum(norm, threshold)
            scaled = (weight * residual).astype(BF16)
            for c in range(copies):
                out_ref[c, r * columns : (r + 1) * columns, :] = scaled
            lines.append(weight)
        lines.append(jnp.zeros((PAD - count, rows), F32))
        tail = jnp.concatenate(lines, axis=0).astype(BF16)
        for c in range(copies):
            out_ref[c, count * columns :, :] = tail

    height = count * columns + PAD
    return pl.pallas_call(
        kernel,
        grid_spec=pltpu.PrefetchScalarGridSpec(
            num_scalar_prefetch=1,
            grid=(1,),
            in_specs=[
                pl.BlockSpec(parts.shape, lambda i, s: (0, 0, 0, 0)),
                pl.BlockSpec((count, columns, rows), lambda i, s: (s[2], 0, 0)),
            ],
            out_specs=pl.BlockSpec((copies, height, rows), lambda i, s: (0, 0, 0)),
        ),
        out_shape=jax.ShapeDtypeStruct((copies, height, rows), BF16),
        compiler_params=params(),
    )(scalars, parts, resp_t)


def gradient_half(scalars, ids, tiles, scaled, local_blocks, groups, carried=None, before=None, keep_error=False):
    row_blocks, kt, rows, width = tiles.shape
    sources, height, _ = scaled.shape
    count = row_blocks // 2 // sources
    columns = (height - PAD) // count
    per_step = 2
    step = count * per_step
    steps = sources // per_step
    last = before is not None
    owned = local_blocks // groups

    def kernel(scalars_ref, ids_ref, tiles_ref, scaled_ref, *refs):
        refs = list(refs)
        start_ref = refs.pop(0) if last or carried is not None else None
        curv_in = refs.pop(0) if last else None
        if last:
            out_ref = refs.pop(0)
            error_ref = refs.pop(0) if keep_error else None
        grad, curv = refs
        place = pl.program_id(0)
        base = (scalars_ref[0] * steps + place) * step

        @pl.when(place == 0)
        def _():
            if start_ref is not None:
                grad[...] = start_ref[...]
            else:
                grad[...] = jnp.zeros_like(grad)
            if last:
                curv[...] = curv_in[...]
            else:
                curv[...] = jnp.zeros_like(curv)

        for p in range(per_step):
            tail = scaled_ref[p, count * columns :, :].astype(F32)
            for r in range(count):
                weights = jnp.broadcast_to(tail[r : r + 1, :], (rows, rows)).T
                lhs = scaled_ref[p, r * columns : (r + 1) * columns, :]
                at = p * count + r
                for k in range(kt):
                    block = ids_ref[(base + at) * kt + k]
                    tile = tiles_ref[at, k]
                    grad[block] += jnp.dot(lhs, tile, preferred_element_type=F32)
                    wide = tile.astype(F32)
                    square = wide * wide * weights
                    curv[block] += jnp.sum(square.reshape(rows // 8, 8, width), axis=0)

        if last:

            @pl.when(place == steps - 1)
            def _():
                for g in range(groups):
                    lines = []
                    for b in range(owned):
                        at = g * owned + b
                        rounded = grad[at].astype(BF16)
                        out_ref[g, b * columns : (b + 1) * columns, :] = rounded
                        if keep_error:
                            error_ref[at] = grad[at] - rounded.astype(F32)
                        lines.append(jnp.sum(curv[at], axis=0, keepdims=True))
                    lines.append(jnp.zeros((PAD - owned, width), F32))
                    out_ref[g, owned * columns :, :] = jnp.concatenate(lines, axis=0).astype(BF16)

    grad_shape = (local_blocks, columns, width)
    curv_shape = (local_blocks, 8, width)
    whole = lambda shape: pl.BlockSpec(shape, lambda i, s, d: (0,) * len(shape))
    in_specs = [
        pl.BlockSpec((step, kt, rows, width), lambda i, s, d: (s[0] * steps + i, 0, 0, 0)),
        pl.BlockSpec((per_step, height, rows), lambda i, s, d: (i, 0, 0)),
    ]
    extra = before if last else () if carried is None else (carried,)
    in_specs += [whole(x.shape) for x in extra]
    if last:
        out_shape = [jax.ShapeDtypeStruct((groups, owned * columns + PAD, width), BF16)]
        if keep_error:
            out_shape.append(jax.ShapeDtypeStruct(grad_shape, F32))
        out_specs = [whole(x.shape) for x in out_shape]
        scratch = [pltpu.VMEM(grad_shape, F32), pltpu.VMEM(curv_shape, F32)]
    else:
        out_shape = [jax.ShapeDtypeStruct(grad_shape, F32), jax.ShapeDtypeStruct(curv_shape, F32)]
        out_specs = [whole(grad_shape), whole(curv_shape)]
        scratch = []
    return pl.pallas_call(
        kernel,
        grid_spec=pltpu.PrefetchScalarGridSpec(
            num_scalar_prefetch=2,
            grid=(steps,),
            in_specs=in_specs,
            out_specs=out_specs,
            scratch_shapes=scratch,
        ),
        out_shape=out_shape,
        compiler_params=params(),
    )(scalars, ids, tiles, scaled, *extra)


def update(parts, exact, known, copies):
    sources, height, width = parts.shape
    owned, columns, _ = exact.shape

    def kernel(parts_ref, exact_ref, *refs):
        new_ref, sent_ref = refs[-2:]

        def total(lo, hi):
            value = parts_ref[0, lo:hi, :].astype(F32)
            for s in range(1, sources):
                value = value + parts_ref[s, lo:hi, :].astype(F32)
            return value

        curvature = total(owned * columns, height)
        for b in range(owned):
            gradient = total(b * columns, (b + 1) * columns)
            coef = exact_ref[b]
            new = coef + STEP_SIZE * (gradient - RIDGE * coef) / (curvature[b : b + 1] + RIDGE)
            new_ref[b] = new
            if known is not None:
                new = new - refs[0][b].astype(F32)
            for c in range(copies):
                sent_ref[c, b] = new.astype(BF16)

    return pl.pallas_call(
        kernel,
        out_shape=[
            jax.ShapeDtypeStruct(exact.shape, F32),
            jax.ShapeDtypeStruct((copies,) + exact.shape, BF16),
        ],
        compiler_params=params(),
    )(parts, exact, *(() if known is None else (known,)))


def finish(known, change):
    blocks, columns, width = known.shape
    step = 16

    def kernel(known_ref, change_ref, out_ref):
        for b in range(step):
            value = known_ref[b].astype(F32) + change_ref[b].astype(F32)
            out_ref[:, b * width : (b + 1) * width] = value

    return pl.pallas_call(
        kernel,
        grid=(blocks // step,),
        in_specs=[pl.BlockSpec((step, columns, width), lambda i: (i, 0, 0))] * 2,
        out_specs=pl.BlockSpec((columns, step * width), lambda i: (0, i)),
        out_shape=jax.ShapeDtypeStruct((columns, blocks * width), F32),
        compiler_params=params(),
    )(known, change)


def make_body(n_row, n_feat):
    n_yz = n_feat // 2
    chips = [[2 * i + core for i in range(n_yz)] for core in range(2)]
    other_core = [(i, i ^ 1) for i in range(n_feat)]

    def swap_core(x):
        return lax.ppermute(x, "feat", other_core)

    def exchange_feat(x):
        return lax.all_to_all(x, "feat", 0, 0, axis_index_groups=chips, tiled=True)

    def exchange_row(x):
        return lax.all_to_all(x, "row", 0, 0, tiled=True)

    def body(design_tiles, block_ids, responses, live_groups, start_coef):
        row = lax.axis_index("row")
        feat = lax.axis_index("feat")
        core, yz = feat % 2, feat // 2
        _, owners, slots, kt, rows, width = design_tiles.shape
        row_blocks = owners * slots
        features, columns = start_coef.shape
        local_blocks = features // width
        tiles = design_tiles.reshape(row_blocks, kt, rows, width)
        resp_t = responses.reshape(row_blocks, rows, columns).swapaxes(1, 2)
        start_t = start_coef.T
        ids = lax.dynamic_index_in_dim(block_ids, row, 0, keepdims=False).reshape(-1)
        ids = (ids - feat * local_blocks).astype(jnp.int32)
        share = row_blocks // n_feat
        mine = core * n_yz + yz
        live = lax.dynamic_index_in_dim(live_groups, row, 0, keepdims=False)
        flag = live[mine * share // slots]
        here = jnp.stack([core, flag, mine]).astype(jnp.int32)
        there = jnp.stack([1 - core, flag, mine]).astype(jnp.int32)
        owned = local_blocks // n_row
        own = lax.dynamic_slice_in_dim(start_t, row * owned * width, owned * width, 1)
        own = own.reshape(columns, owned, width).swapaxes(0, 1)

        exact, known, own_known, carried = own, coef_blocks(start_t), None, None
        for iteration in range(ITERS):
            ends = iteration == ITERS - 1
            sent = predict_half(there, ids, tiles, known, F32)
            arrived = swap_core(sent)
            kept = predict_half(here, ids, tiles, known, F32)
            pair = (kept + arrived).astype(BF16)
            parts = exchange_feat(pair).reshape(n_yz, share, columns, rows)
            scaled = exchange_feat(weigh(here, parts, resp_t, n_yz))
            scaled_there = swap_core(scaled)
            before = gradient_half(here, ids, tiles, scaled, local_blocks, n_row, carried)
            partial, *error = gradient_half(
                there, ids, tiles, scaled_there, local_blocks, n_row, None, before, not ends
            )
            carried = None if ends else error[0]
            exact, sent = update(exchange_row(partial), exact, own_known, n_row)
            own_known = sent[0]
            gathered = exchange_row(sent).reshape(local_blocks, columns, width)
            if ends:
                return finish(known, gathered).T
            known = gathered

    return body


def solution(mesh):
    in_specs = (
        P("row", None, None, "feat", None, None),
        P(None, None, None, "feat"),
        P("row", None, None, None, None),
        P(),
        P("feat", None),
    )
    return jax.shard_map(
        make_body(mesh.shape["row"], mesh.shape["feat"]),
        mesh=mesh,
        in_specs=in_specs,
        out_specs=P("feat", None),
        check_vma=False,
    )
```

time: 510 us -> 196 us (0.38)
  waiting for transfers between devices: 335 us -> 34.8 us
  matrix products: 52.1 us -> 0 us
  Pallas kernels: 0 us -> 42.8 us
  blocking collectives: 82.7 us -> 97.4 us
  between operations: 13.2 us -> 0.17 us
  other arithmetic: 14.8 us -> 2.56 us
  starting transfers between devices: 0.79 us -> 10.3 us
    psum x4 -> x0, waiting for transfers between devices: 335 us -> none  [the longest x2 247 us: huber_weights(): totals = lax.psum(predicted, 'feat')]
    all_to_all x0 -> x6, blocking collectives: none -> 97.4 us  [the longest x4 57.5 us: exchange_feat(): return lax.all_to_all(x, 'feat', 0, 0, axis_index_groups=chips, tiled=True)]
    psum x2 -> x0, blocking collectives: 82.7 us -> none  [body(): gradient, curvature = lax.psum((gradient, curvature), 'row')]
    dot_general x10 -> x0, matrix products: 52.1 us -> none  [the longest x2 15.9 us: body(): jnp.einsum('gskif,gskfc->gsic', work_tiles, picked, preferred_element_typ...]
    pallas_call x0 -> x14, Pallas kernels: none -> 42.8 us  [the longest x4 19.3 us: gradient_half(): pl.pallas_call(kernel, grid_spec=pltpu.PrefetchScalarGridSpec(num_scalar_...]
    all_to_all x0 -> x2, waiting for transfers between devices: none -> 34.8 us  [exchange_row(): return lax.all_to_all(x, 'row', 0, 0, tiled=True)]
    all_to_all x0 -> x2, starting transfers between devices: none -> 10.2 us  [exchange_row(): return lax.all_to_all(x, 'row', 0, 0, tiled=True)]
    gather x2 -> x0, local copies, waits for them, and re-layouts: 5.46 us -> none  [body(): picked = coef_bf[work_ids]]
  transfers between devices with their start and end apart: 4 -> 6, of which waited for: 4 -> 2; matrix products, arithmetic and copies ran while one was open for 3% -> 1% of each run, Pallas kernels for 0% -> 9%
where the time goes in v1:
time: 196 us; the launch traced here: 195 us
  blocking collectives  97.4 us (50%)
  Pallas kernels  42.8 us (22%)
  waiting for transfers between devices  34.8 us (18%)
  starting transfers between devices  10.3 us (5%)
  local copies, waits for them, and re-layouts  7.39 us (4%)
  other arithmetic  2.56 us (1%)
    all_to_all x4, blocking collectives, exchange_feat(): return lax.all_to_all(x, 'feat', 0, 0, axis_index_groups=chips, tiled=True)  57.5 us
    all_to_all x2, blocking collectives, exchange_row(): return lax.all_to_all(x, 'row', 0, 0, tiled=True)  39.9 us
    all_to_all x2, waiting for transfers between devices, exchange_row(): return lax.all_to_all(x, 'row', 0, 0, tiled=True)  34.8 us
    pallas_call x4, Pallas kernels, gradient_half(): pl.pallas_call(kernel, grid_spec=pltpu.PrefetchScalarGridSpec(num_scalar_...  19.3 us
    pallas_call x4, Pallas kernels, predict_half(): pl.pallas_call(kernel, grid_spec=pltpu.PrefetchScalarGridSpec(num_scalar_...  18.9 us
    all_to_all x2, starting transfers between devices, exchange_row(): return lax.all_to_all(x, 'row', 0, 0, tiled=True)  10.2 us
  transfers between devices with their start and end apart: 6, of which 2 were waited for; matrix products, arithmetic and copies ran while one was open for 1% of the time, Pallas kernels for 9%

profile of v1, /device:TPU:0, one launch (start us, length us, event | category | flops | bytes accessed | tf_op | source)
XLA Modules:
  0.0 195.4 jit_solution(9026111388667851953)
XLA Ops:
  0.0 0.7 dynamic-slice_subtract_fusion
  0.7 0.1 copy.6
  0.8 0.1 sub.23.ids_ref
  1.0 0.0 copy-start.1
  1.0 1.6 copy-done.1
  2.6 0.3 shard_map.55.coef_ref
  2.9 1.4 dynamic_slice.14
  4.3 0.8 add_add_fusion.scalars_ref
  5.0 4.7 %shard_map.57 = f32[32,64,128]{2,1,0:T(8,128)S(1)} custom-call(s32[3]{0:T(128)S(1)} %add_add_fusion.scalars_ref, s32[192]{0:T(256)S(1)} %sub.23.ids_ref, bf16[64,3,128,128]{3,2,1,0:T(8,128)(2,1)} %bitcast.35, bf16[64,64,128]{2,1,0:T(8,128)(2,1)S(1)} %shard_map.55.coef_ref), custom_call_target="tpu_custom_call" | custom-call | tf_op jit(solution)/shard_map/pallas_call | solution.py:64
  9.7 0.0 collective-permute-start
  9.8 0.8 add_add_fusion.1.scalars_ref
  10.5 4.7 %shard_map.56 = f32[32,64,128]{2,1,0:T(8,128)S(1)} custom-call(s32[3]{0:T(128)S(1)} %add_add_fusion.1.scalars_ref, s32[192]{0:T(256)S(1)} %sub.23.ids_ref, bf16[64,3,128,128]{3,2,1,0:T(8,128)(2,1)} %bitcast.36, bf16[64,64,128]{2,1,0:T(8,128)(2,1)S(1)} %shard_map.55.coef_ref), custom_call_target="tpu_custom_call" | custom-call | tf_op jit(solution)/shard_map/pallas_call | solution.py:64
  15.3 0.0 collective-permute-done
  15.3 0.2 add_convert_fusion.1
  15.5 16.9 %all_to_all.40 = bf16[32,64,128]{2,1,0:T(8,128)(2,1)S(1)} all-to-all(bf16[32,64,128]{2,1,0:T(8,128)(2,1)S(1)} %add_convert_fusion.1), channel_id=1, replica_groups={{0,2,4,6,8,10,12,14},{1,3,5,7,9,11,13,15},{16,18,20,22,24,26,28,30},{17..., dimensions={0} | all-to-all | bytes 1048576 | tf_op jit(solution)/shard_map/all_to_all | solution.py:278
  32.3 0.0 copy-done
  32.3 0.7 shard_map.58
  33.0 13.6 %all_to_all.41.scaled_ref = bf16[8,272,128]{2,1,0:T(8,128)(2,1)S(1)} all-to-all(bf16[8,272,128]{2,1,0:T(8,128)(2,1)S(1)} %shard_map.58), channel_id=1, replica_groups={{0,2,4,6,8,10,12,14},{1,3,5,7,9,11,13,15},{16,18,20,22,24,26,28,30},{17..., dimensions={0} | all-to-all | bytes 1114112 | tf_op jit(solution)/shard_map/all_to_all | solution.py:278
  46.6 0.0 collective-permute-start.1
  46.6 4.2 %shard_map.59 = (f32[64,64,128]{2,1,0:T(8,128)S(1)}, f32[64,8,128]{2,1,0:T(8,128)S(1)}) custom-call(s32[3]{0:T(128)S(1)} %add_add_fusion.1.scalars_ref, s32[192]{0:T(256)S(1)} %sub.23.ids_ref, bf16[64,3,128,128]{3,2,1,0:T(8,128)(2,1)} %bitcast.37, bf16[8,272,128]{2,1,0:T(8,128)(2,1)S(1)} %all_to_all.41.scaled_ref), custom_call_target="tpu_custom_call" | custom-call | tf_op jit(solution)/shard_map/pallas_call | solution.py:202
  50.9 0.0 collective-permute-done.1.scaled_ref
  50.9 5.5 %shard_map.60 = (bf16[8,528,128]{2,1,0:T(8,128)(2,1)}, f32[64,64,128]{2,1,0:T(8,128)S(1)}) custom-call(s32[3]{0:T(128)S(1)} %add_add_fusion.scalars_ref, s32[192]{0:T(256)S(1)} %sub.23.ids_ref, bf16[64,3,128,128]{3,2,1,0:T(8,128)(2,1)} %bitcast.38, bf16[8,272,128]{2,1,0:T(8,128)(2,1)S(1)} %collective-permute-done.1.scaled_ref, ...), custom_call_target="tpu_custom_call" | custom-call | tf_op jit(solution)/shard_map/pallas_call | solution.py:202
  56.4 1.3 copy-done.2
  57.7 6.6 %all-to-all-start.2 = ((bf16[8,528,128]{2,1,0:T(8,128)(2,1)}), bf16[8,528,128]{2,1,0:T(8,128)(2,1)S(1)}, u32[]{:S(2)}, u32[]{:S(2)}) async-start(bf16[8,528,128]{2,1,0:T(8,128)(2,1)} %get-tuple-element.16), calls=%async_computation.2 | async-start | bytes 2162688 | tf_op jit(solution)/shard_map/all_to_all | solution.py:281
  64.3 1.0 bitcast_bitcast_fusion.exact_ref
  65.3 17.3 %all-to-all-done.2.parts_ref = bf16[8,528,128]{2,1,0:T(8,128)(2,1)S(1)} async-done(((bf16[8,528,128]{2,1,0:T(8,128)(2,1)}), bf16[8,528,128]{2,1,0:T(8,128)(2,1)S(1)}, u32[]{:S(2)}, u32[]{:S(2)}) %all-to-all-start.2) | async-done | bytes 1081376 | tf_op jit(solution)/shard_map/all_to_all | solution.py:281
  82.5 0.2 shard_map.61
  82.8 1.0 copy-done.4
  83.7 19.8 %all_to_all.42 = bf16[8,8,64,128]{3,2,1,0:T(8,128)(2,1)S(1)} all-to-all(bf16[8,8,64,128]{3,2,1,0:T(8,128)(2,1)S(1)} %get-tuple-element.17), channel_id=1, replica_groups=mesh['row'=8,'feat'=16] {'row'}, dimensions={0} | all-to-all | bytes 2097152 | tf_op jit(solution)/shard_map/all_to_all | solution.py:281
  103.6 4.7 %shard_map.63 = f32[32,64,128]{2,1,0:T(8,128)S(1)} custom-call(s32[3]{0:T(128)S(1)} %add_add_fusion.scalars_ref, s32[192]{0:T(256)S(1)} %sub.23.ids_ref, bf16[64,3,128,128]{3,2,1,0:T(8,128)(2,1)} %bitcast.39, bf16[64,64,128]{2,1,0:T(8,128)(2,1)S(1)} %bitcast.26), custom_call_target="tpu_custom_call" | custom-call | tf_op jit(solution)/shard_map/pallas_call | solution.py:64
  108.3 0.0 collective-permute-start.2
  108.3 4.7 %shard_map.62 = f32[32,64,128]{2,1,0:T(8,128)S(1)} custom-call(s32[3]{0:T(128)S(1)} %add_add_fusion.1.scalars_ref, s32[192]{0:T(256)S(1)} %sub.23.ids_ref, bf16[64,3,128,128]{3,2,1,0:T(8,128)(2,1)} %bitcast.40, bf16[64,64,128]{2,1,0:T(8,128)(2,1)S(1)} %bitcast.27), custom_call_target="tpu_custom_call" | custom-call | tf_op jit(solution)/shard_map/pallas_call | solution.py:64
  113.0 0.0 collective-permute-done.2
  113.1 0.2 add_convert_fusion
  113.2 0.0 copy-start.3
  113.2 13.3 %all_to_all.43 = bf16[32,64,128]{2,1,0:T(8,128)(2,1)S(1)} all-to-all(bf16[32,64,128]{2,1,0:T(8,128)(2,1)S(1)} %add_convert_fusion), channel_id=1, replica_groups={{0,2,4,6,8,10,12,14},{1,3,5,7,9,11,13,15},{16,18,20,22,24,26,28,30},{17..., dimensions={0} | all-to-all | bytes 1048576 | tf_op jit(solution)/shard_map/all_to_all | solution.py:278
  126.5 0.7 shard_map.64
  127.2 13.7 %all_to_all.44.scaled_ref = bf16[8,272,128]{2,1,0:T(8,128)(2,1)S(1)} all-to-all(bf16[8,272,128]{2,1,0:T(8,128)(2,1)S(1)} %shard_map.64), channel_id=1, replica_groups={{0,2,4,6,8,10,12,14},{1,3,5,7,9,11,13,15},{16,18,20,22,24,26,28,30},{17..., dimensions={0} | all-to-all | bytes 1114112 | tf_op jit(solution)/shard_map/all_to_all | solution.py:278
  140.9 0.0 collective-permute-start.3
  140.9 4.2 %shard_map.65 = (f32[64,64,128]{2,1,0:T(8,128)S(1)}, f32[64,8,128]{2,1,0:T(8,128)S(1)}) custom-call(s32[3]{0:T(128)S(1)} %add_add_fusion.1.scalars_ref, s32[192]{0:T(256)S(1)} %sub.23.ids_ref, bf16[64,3,128,128]{3,2,1,0:T(8,128)(2,1)} %bitcast.41, bf16[8,272,128]{2,1,0:T(8,128)(2,1)S(1)} %all_to_all.44.scaled_ref, f32[64,64,128]{2,1,0:T(8,128)S(1)} %copy-done.3), custom_call_target="tpu_custom_call" | custom-call | tf_op jit(solution)/shard_map/pallas_call | solution.py:202
  145.2 0.0 collective-permute-done.3.scaled_ref
  145.2 5.3 %shard_map.66 = bf16[8,528,128]{2,1,0:T(8,128)(2,1)} custom-call(s32[3]{0:T(128)S(1)} %add_add_fusion.scalars_ref, s32[192]{0:T(256)S(1)} %sub.23.ids_ref, bf16[64,3,128,128]{3,2,1,0:T(8,128)(2,1)} %bitcast.42, bf16[8,272,128]{2,1,0:T(8,128)(2,1)S(1)} %collective-permute-done.3.scaled_ref, f32[64,64,128]{2,1,0:T(8,128)S(1)} %get-tuple-element.19.refs_0_, ...), custom_call_target="tpu_custom_call" | custom-call | tf_op jit(solution)/shard_map/pallas_call | solution.py:202
  150.5 3.6 %all-to-all-start.6 = ((bf16[8,528,128]{2,1,0:T(8,128)(2,1)}), bf16[8,528,128]{2,1,0:T(8,128)(2,1)S(1)}, u32[]{:S(2)}, u32[]{:S(2)}) async-start(bf16[8,528,128]{2,1,0:T(8,128)(2,1)} %shard_map.66), calls=%async_computation.6 | async-start | bytes 2162688 | tf_op jit(solution)/shard_map/all_to_all | solution.py:281
  154.1 0.9 slice_bitcast_fusion.refs_0_
  155.0 17.5 %all-to-all-done.6.parts_ref = bf16[8,528,128]{2,1,0:T(8,128)(2,1)S(1)} async-done(((bf16[8,528,128]{2,1,0:T(8,128)(2,1)}), bf16[8,528,128]{2,1,0:T(8,128)(2,1)S(1)}, u32[]{:S(2)}, u32[]{:S(2)}) %all-to-all-start.6) | async-done | bytes 1081376 | tf_op jit(solution)/shard_map/all_to_all | solution.py:281
  172.5 0.9 shard_map.67
  173.5 20.1 %all_to_all.45 = bf16[8,8,64,128]{3,2,1,0:T(8,128)(2,1)S(1)} all-to-all(bf16[8,8,64,128]{3,2,1,0:T(8,128)(2,1)S(1)} %get-tuple-element.22), channel_id=1, replica_groups=mesh['row'=8,'feat'=16] {'row'}, dimensions={0} | all-to-all | bytes 2097152 | tf_op jit(solution)/shard_map/all_to_all | solution.py:281
  193.6 1.9 shard_map.68
  (4 shorter events, 0.0 us)
Async XLA Ops:
  1.0 1.6 copy-start.1
  9.7 5.5 %collective-permute-start = (f32[32,64,128]{2,1,0:T(8,128)S(1)}, f32[32,64,128]{2,1,0:T(8,128)S(1)}, u32[]{:S(2)}, u32[]{:S(2)}) collective-permute-start(f32[32,64,128]{2,1,0:T(8,128)S(1)} %shard_map.57), channel_id=1, source_target_pairs={{0,1},{1,0},{2,3},{3,2},{4,5},{5,4},{6,7},{7,6},{8,9},{9,8},{10,11... | collective-permute-start | bytes 3145736 | tf_op jit(solution)/shard_map/ppermute | solution.py:275
  15.3 17.1 %copy-start = (bf16[1,8,8,128,64]{3,4,2,1,0:T(8,128)(2,1)S(1)}, bf16[1,8,8,128,64]{3,4,2,1,0:T(8,128)(2,1)}, u32[]{:S(2)}) copy-start(bf16[1,8,8,128,64]{3,4,2,1,0:T(8,128)(2,1)} %param.7) | copy-start | bytes 3145732
  46.6 4.2 %collective-permute-start.1 = (bf16[8,272,128]{2,1,0:T(8,128)(2,1)S(1)}, bf16[8,272,128]{2,1,0:T(8,128)(2,1)S(1)}, u32[]{:S(2)}, u32[]{:S(2)}) collective-permute-start(bf16[8,272,128]{2,1,0:T(8,128)(2,1)S(1)} %all_to_all.41.scaled_ref), channel_id=1, source_target_pairs={{0,1},{1,0},{2,3},{3,2},{4,5},{5,4},{6,7},{7,6},{8,9},{9,8},{10,11... | collective-permute-start | bytes 1671176 | tf_op jit(solution)/shard_map/ppermute | solution.py:275
  56.4 1.3 copy-start.2
  57.7 24.9 %all-to-all-start.2 = ((bf16[8,528,128]{2,1,0:T(8,128)(2,1)}), bf16[8,528,128]{2,1,0:T(8,128)(2,1)S(1)}, u32[]{:S(2)}, u32[]{:S(2)}) async-start(bf16[8,528,128]{2,1,0:T(8,128)(2,1)} %get-tuple-element.16), calls=%async_computation.2 | async-start | bytes 2162688 | tf_op jit(solution)/shard_map/all_to_all | solution.py:281
  82.7 1.0 copy-start.4
  108.3 4.8 %collective-permute-start.2 = (f32[32,64,128]{2,1,0:T(8,128)S(1)}, f32[32,64,128]{2,1,0:T(8,128)S(1)}, u32[]{:S(2)}, u32[]{:S(2)}) collective-permute-start(f32[32,64,128]{2,1,0:T(8,128)S(1)} %shard_map.63), channel_id=1, source_target_pairs={{0,1},{1,0},{2,3},{3,2},{4,5},{5,4},{6,7},{7,6},{8,9},{9,8},{10,11... | collective-permute-start | bytes 3145736 | tf_op jit(solution)/shard_map/ppermute | solution.py:275
  113.2 27.7 %copy-start.3 = (f32[64,64,128]{2,1,0:T(8,128)S(1)}, f32[64,64,128]{2,1,0:T(8,128)}, u32[]{:S(2)}) copy-start(f32[64,64,128]{2,1,0:T(8,128)} %copy-done.2) | copy-start | bytes 6291460
  140.9 4.2 %collective-permute-start.3 = (bf16[8,272,128]{2,1,0:T(8,128)(2,1)S(1)}, bf16[8,272,128]{2,1,0:T(8,128)(2,1)S(1)}, u32[]{:S(2)}, u32[]{:S(2)}) collective-permute-start(bf16[8,272,128]{2,1,0:T(8,128)(2,1)S(1)} %all_to_all.44.scaled_ref), channel_id=1, source_target_pairs={{0,1},{1,0},{2,3},{3,2},{4,5},{5,4},{6,7},{7,6},{8,9},{9,8},{10,11... | collective-permute-start | bytes 1671176 | tf_op jit(solution)/shard_map/ppermute | solution.py:275
  150.5 22.0 %all-to-all-start.6 = ((bf16[8,528,128]{2,1,0:T(8,128)(2,1)}), bf16[8,528,128]{2,1,0:T(8,128)(2,1)S(1)}, u32[]{:S(2)}, u32[]{:S(2)}) async-start(bf16[8,528,128]{2,1,0:T(8,128)(2,1)} %shard_map.66), calls=%async_computation.6 | async-start | bytes 2162688 | tf_op jit(solution)/shard_map/all_to_all | solution.py:281

commit v2 on v1

v2 whole, which is shorter than its diff:
```python
import jax
import jax.numpy as jnp
from jax import lax
from jax.experimental import pallas as pl
from jax.experimental.pallas import tpu as pltpu
from jax.sharding import PartitionSpec as P

ITERS = 2
STEP_SIZE = 0.25
RIDGE = 0.05
F32 = jnp.float32
BF16 = jnp.bfloat16
VMEM_LIMIT = 16 * 1024 * 1024

LANES = 128
PAD = 16


def params():
    return pltpu.CompilerParams(vmem_limit_bytes=VMEM_LIMIT)


def whole(count, scalars):
    smem = pl.BlockSpec(memory_space=pltpu.SMEM)
    vmem = pl.BlockSpec(memory_space=pltpu.VMEM)
    return [smem] * scalars + [vmem] * count


def coef_blocks(start_t):
    columns, features = start_t.shape
    blocks = features // LANES

    def kernel(start_ref, out_ref):
        for b in range(blocks):
            out_ref[b] = start_ref[:, b * LANES : (b + 1) * LANES].astype(BF16)

    return pl.pallas_call(
        kernel,
        in_specs=whole(1, 0),
        out_specs=whole(1, 0)[0],
        out_shape=jax.ShapeDtypeStruct((blocks, columns, LANES), BF16),
        compiler_params=params(),
    )(start_t)


def side(scalars_ref, other):
    return 1 - scalars_ref[0] if other else scalars_ref[0]


def predict_half(scalars, ids, tiles, coef, other):
    row_blocks, kt, rows, width = tiles.shape
    columns = coef.shape[1]
    half = row_blocks // 2
    step = 8

    def kernel(scalars_ref, ids_ref, tiles_ref, coef_ref, out_ref):
        base = side(scalars_ref, other) * half

        @pl.loop(0, half // step)
        def _(i):
            for r in range(step):
                at = i * step + r
                row_block = base + at
                picked = [coef_ref[ids_ref[row_block * kt + k]] for k in range(kt)]
                placed = [tiles_ref[row_block, k] for k in range(kt)]
                out_ref[at] = lax.dot_general(
                    jnp.concatenate(picked, axis=1),
                    jnp.concatenate(placed, axis=1),
                    (((1,), (1,)), ((), ())),
                    preferred_element_type=F32,
                )

    return pl.pallas_call(
        kernel,
        in_specs=whole(2, 2),
        out_specs=whole(1, 0)[0],
        out_shape=jax.ShapeDtypeStruct((half, columns, rows), F32),
        compiler_params=params(),
    )(scalars, ids, tiles, coef)


def weigh(scalars, parts, resp_t, copies):
    sources, count, columns, rows = parts.shape
    threshold = 1.4 * columns**0.5
    height = count * columns + PAD

    def kernel(scalars_ref, parts_ref, resp_ref, out_ref):
        flag = scalars_ref[1].astype(F32)
        first = scalars_ref[2] * count
        lines = []
        for r in range(count):
            predicted = parts_ref[0, r].astype(F32)
            for s in range(1, sources):
                predicted = predicted + parts_ref[s, r].astype(F32)
            residual = resp_ref[first + r].astype(F32) - predicted
            norm = jnp.sqrt(jnp.sum(residual * residual, axis=0, keepdims=True))
            weight = flag * threshold / jnp.maximum(norm, threshold)
            scaled = (weight * residual).astype(BF16)
            for c in range(copies):
                out_ref[c, r * columns : (r + 1) * columns, :] = scaled
            lines.append(weight)
        lines.append(jnp.zeros((PAD - count, rows), F32))
        tail = jnp.concatenate(lines, axis=0).astype(BF16)
        for c in range(copies):
            out_ref[c, count * columns :, :] = tail

    return pl.pallas_call(
        kernel,
        in_specs=whole(2, 1),
        out_specs=whole(1, 0)[0],
        out_shape=jax.ShapeDtypeStruct((copies, height, rows), BF16),
        compiler_params=params(),
    )(scalars, parts, resp_t)


def gradient_half(scalars, ids, tiles, scaled, other, local_blocks, groups, before, keep_error):
    row_blocks, kt, rows, width = tiles.shape
    sources, height, _ = scaled.shape
    half = row_blocks // 2
    count = half // sources
    columns = (height - PAD) // count
    owned = local_blocks // groups
    n_before = len(before)

    def kernel(scalars_ref, ids_ref, tiles_ref, scaled_ref, *refs):
        before_refs, refs = refs[:n_before], refs[n_before:]
        if other:
            out_ref = refs[0]
            error_ref = refs[1] if keep_error else None
        grad, curv = refs[-2:]
        base = side(scalars_ref, other) * half
        for ref, start in zip((grad, curv), list(before_refs) + [None] * (2 - n_before)):
            ref[...] = jnp.zeros_like(ref) if start is None else start[...]

        @pl.loop(0, sources)
        def _(p):
            tail = scaled_ref[p, count * columns :, :].astype(F32)
            for r in range(count):
                row_block = base + p * count + r
                weights = jnp.broadcast_to(tail[r : r + 1, :], (rows, rows)).T
                placed = [tiles_ref[row_block, k] for k in range(kt)]
                sums = jnp.dot(
                    scaled_ref[p, r * columns : (r + 1) * columns, :],
                    jnp.concatenate(placed, axis=1),
                    preferred_element_type=F32,
                )
                for k in range(kt):
                    block = ids_ref[row_block * kt + k]
                    grad[block] += sums[:, k * width : (k + 1) * width]
                    wide = placed[k].astype(F32)
                    square = wide * wide * weights
                    curv[block] += jnp.sum(square.reshape(rows // 8, 8, width), axis=0)

        if other:

            @pl.loop(0, groups)
            def _(g):
                lines = []
                for b in range(owned):
                    at = g * owned + b
                    rounded = grad[at].astype(BF16)
                    out_ref[g, b * columns : (b + 1) * columns, :] = rounded
                    if keep_error:
                        error_ref[at] = grad[at] - rounded.astype(F32)
                    lines.append(jnp.sum(curv[at], axis=0, keepdims=True))
                lines.append(jnp.zeros((PAD - owned, width), F32))
                out_ref[g, owned * columns :, :] = jnp.concatenate(lines, axis=0).astype(BF16)

    grad_shape = (local_blocks, columns, width)
    curv_shape = (local_blocks, 8, width)
    out_shape, scratch = [], []
    if other:
        out_shape.append(jax.ShapeDtypeStruct((groups, owned * columns + PAD, width), BF16))
        if keep_error:
            out_shape.append(jax.ShapeDtypeStruct(grad_shape, F32))
        scratch = [pltpu.VMEM(grad_shape, F32), pltpu.VMEM(curv_shape, F32)]
    else:
        out_shape = [jax.ShapeDtypeStruct(grad_shape, F32), jax.ShapeDtypeStruct(curv_shape, F32)]
    return pl.pallas_call(
        kernel,
        in_specs=whole(2 + n_before, 2),
        out_specs=whole(len(out_shape), 0),
        out_shape=out_shape,
        scratch_shapes=scratch,
        compiler_params=params(),
    )(scalars, ids, tiles, scaled, *before)


def update(scalars, parts, exact, known, copies, owned):
    sources, height, width = parts.shape
    columns = (height - PAD) // owned
    shape = (owned, columns, width)
    first = known is None

    def kernel(scalars_ref, parts_ref, exact_ref, *refs):
        sent_ref = refs[-1]

        def total(lo, hi):
            value = parts_ref[0, lo:hi, :].astype(F32)
            for s in range(1, sources):
                value = value + parts_ref[s, lo:hi, :].astype(F32)
            return value

        curvature = total(owned * columns, height)
        for b in range(owned):
            gradient = total(b * columns, (b + 1) * columns)
            if first:
                at = pl.multiple_of((scalars_ref[3] * owned + b) * width, width)
                coef = exact_ref[:, pl.ds(at, width)]
            else:
                coef = exact_ref[b]
            new = coef + STEP_SIZE * (gradient - RIDGE * coef) / (curvature[b : b + 1] + RIDGE)
            if first:
                refs[0][b] = new
            else:
                new = new - refs[0][0, b].astype(F32)
            for c in range(copies):
                sent_ref[c, b] = new.astype(BF16)

    out_shape = [jax.ShapeDtypeStruct((copies,) + shape, BF16)]
    if first:
        out_shape.insert(0, jax.ShapeDtypeStruct(shape, F32))
    return pl.pallas_call(
        kernel,
        in_specs=whole(2 + (not first), 1),
        out_specs=whole(len(out_shape), 0),
        out_shape=out_shape,
        compiler_params=params(),
    )(scalars, parts, exact, *(() if first else (known,)))


def finish(known, change):
    blocks, columns, width = known.shape
    step = 16

    def kernel(known_ref, change_ref, out_ref):
        for b in range(step):
            value = known_ref[b].astype(F32) + change_ref[b].astype(F32)
            out_ref[:, b * width : (b + 1) * width] = value

    return pl.pallas_call(
        kernel,
        grid=(blocks // step,),
        in_specs=[pl.BlockSpec((step, columns, width), lambda i: (i, 0, 0))] * 2,
        out_specs=pl.BlockSpec((columns, step * width), lambda i: (0, i)),
        out_shape=jax.ShapeDtypeStruct((columns, blocks * width), F32),
        compiler_params=params(),
    )(known, change)


def make_body(n_row, n_feat):
    n_yz = n_feat // 2
    chips = [[2 * i + core for i in range(n_yz)] for core in range(2)]
    other_core = [(i, i ^ 1) for i in range(n_feat)]

    def swap_core(x):
        return lax.ppermute(x, "feat", other_core)

    def exchange_feat(x):
        return lax.all_to_all(x, "feat", 0, 0, axis_index_groups=chips, tiled=True)

    def exchange_row(x):
        return lax.all_to_all(x, "row", 0, 0, tiled=True)

    def body(design_tiles, block_ids, responses, live_groups, start_coef):
        row = lax.axis_index("row")
        feat = lax.axis_index("feat")
        core, yz = feat % 2, feat // 2
        _, owners, slots, kt, rows, width = design_tiles.shape
        row_blocks = owners * slots
        features, columns = start_coef.shape
        local_blocks = features // width
        tiles = design_tiles.reshape(row_blocks, kt, rows, width)
        resp_t = responses.reshape(row_blocks, rows, columns).swapaxes(1, 2)
        start_t = start_coef.T
        ids = lax.dynamic_index_in_dim(block_ids, row, 0, keepdims=False).reshape(-1)
        ids = (ids - feat * local_blocks).astype(jnp.int32)
        share = row_blocks // n_feat
        mine = core * n_yz + yz
        live = lax.dynamic_index_in_dim(live_groups, row, 0, keepdims=False)
        flag = live[mine * share // slots]
        scalars = jnp.stack([core, flag, mine, row]).astype(jnp.int32)
        owned = local_blocks // n_row

        known, exact, sent, carried = coef_blocks(start_t), start_t, None, ()
        for iteration in range(ITERS):
            ends = iteration == ITERS - 1
            arrived = swap_core(predict_half(scalars, ids, tiles, known, True))
            kept = predict_half(scalars, ids, tiles, known, False)
            pair = (kept + arrived).astype(BF16)
            parts = exchange_feat(pair).reshape(n_yz, share, columns, rows)
            scaled = exchange_feat(weigh(scalars, parts, resp_t, n_yz))
            scaled_there = swap_core(scaled)
            before = gradient_half(
                scalars, ids, tiles, scaled, False, local_blocks, n_row, carried, False
            )
            partial, *carried = gradient_half(
                scalars, ids, tiles, scaled_there, True, local_blocks, n_row, before, not ends
            )
            *new, sent = update(scalars, exchange_row(partial), exact, sent, n_row, owned)
            gathered = exchange_row(sent).reshape(local_blocks, columns, width)
            if ends:
                return finish(known, gathered).T
            known, exact = gathered, new[0]

    return body


def solution(mesh):
    in_specs = (
        P("row", None, None, "feat", None, None),
        P(None, None, None, "feat"),
        P("row", None, None, None, None),
        P(),
        P("feat", None),
    )
    return jax.shard_map(
        make_body(mesh.shape["row"], mesh.shape["feat"]),
        mesh=mesh,
        in_specs=in_specs,
        out_specs=P("feat", None),
        check_vma=False,
    )
```

time: 196 us -> 176 us (0.90)
  blocking collectives: 97.4 us -> 142 us
  waiting for transfers between devices: 34.8 us -> 0.43 us
  Pallas kernels: 42.8 us -> 25.2 us
  starting transfers between devices: 10.3 us -> 0.18 us
    all_to_all x2 -> x4, blocking collectives: 39.9 us -> 85.2 us  [exchange_row(): return lax.all_to_all(x, 'row', 0, 0, tiled=True)]
    all_to_all x2 -> x0, waiting for transfers between devices: 34.8 us -> none  [exchange_row(): return lax.all_to_all(x, 'row', 0, 0, tiled=True)]
    pallas_call x13, Pallas kernels: 40.9 us -> 23.4 us  [the longest x4 10.8 us: gradient_half(): pl.pallas_call(kernel, in_specs=whole(2 + n_before, 2), out_specs=whole(l...]
    all_to_all x2 -> x0, starting transfers between devices: 10.2 us -> none  [exchange_row(): return lax.all_to_all(x, 'row', 0, 0, tiled=True)]
    unnamed x10 -> x12, local copies, waits for them, and re-layouts: 3.89 us -> 4.4 us
  transfers between devices with their start and end apart: 6 -> 4, of which waited for: 2 -> 2; matrix products, arithmetic and copies ran while one was open for 1% -> 0% of each run, Pallas kernels for 9% -> 6%
where the time goes in v2:
time: 176 us
  blocking collectives  142 us (81%)
  Pallas kernels  25.2 us (14%)
  local copies, waits for them, and re-layouts  5.9 us (3%)
    all_to_all x4, blocking collectives, exchange_row(): return lax.all_to_all(x, 'row', 0, 0, tiled=True)  85.2 us
    all_to_all x4, blocking collectives, exchange_feat(): return lax.all_to_all(x, 'feat', 0, 0, axis_index_groups=chips, tiled=True)  56.9 us
    pallas_call x4, Pallas kernels, gradient_half(): pl.pallas_call(kernel, in_specs=whole(2 + n_before, 2), out_specs=whole(l...  10.8 us
    pallas_call x4, Pallas kernels, predict_half(): pl.pallas_call(kernel, in_specs=whole(2, 2), out_specs=whole(1, 0)[0], ou...  9.66 us
    unnamed x12, local copies, waits for them, and re-layouts  4.4 us
  transfers between devices with their start and end apart: 4, of which 2 were waited for; matrix products, arithmetic and copies ran while one was open for 0% of the time, Pallas kernels for 6%

profile of v2, /device:TPU:0, one launch (start us, length us, event | category | flops | bytes accessed | tf_op | source)
XLA Modules:
  0.0 175.7 jit_solution(13728849290088271723)
XLA Ops:
  0.0 0.7 dynamic-slice_subtract_fusion
  0.7 0.1 copy.6
  0.8 0.1 sub.19.ids_ref
  1.0 0.0 copy-start.1
  1.0 1.6 copy-done.1
  2.6 0.1 shard_map.55.coef_ref
  2.7 1.2 dynamic_slice.11
  3.9 0.6 pad_add_fusion.scalars_ref
  4.5 0.0 copy-start
  4.5 2.8 %copy-done = bf16[1,8,8,3,128,128]{5,4,3,2,1,0:T(8,128)(2,1)S(1)} copy-done((bf16[1,8,8,3,128,128]{5,4,3,2,1,0:T(8,128)(2,1)S(1)}, bf16[1,8,8,3,128,128]{5,4,3,2,1,0:T(8,128)(2,1)}, u32[]{:S(2)}) %copy-start) | copy-done | bytes 6291480
  7.3 2.4 %shard_map.57 = f32[32,64,128]{2,1,0:T(8,128)S(1)} custom-call(s32[4]{0:T(128)S(1)} %pad_add_fusion.scalars_ref, s32[192]{0:T(256)S(1)} %sub.19.ids_ref, bf16[64,3,128,128]{3,2,1,0:T(8,128)(2,1)S(1)} %bitcast.16, bf16[64,64,128]{2,1,0:T(8,128)(2,1)S(1)} %shard_map.55.coef_ref), custom_call_target="tpu_custom_call" | custom-call | tf_op jit(solution)/shard_map/pallas_call | solution.py:73
  9.8 0.0 slice-start.1
  9.8 0.1 collective-permute-start
  9.9 2.4 %shard_map.56 = f32[32,64,128]{2,1,0:T(8,128)S(1)} custom-call(s32[4]{0:T(128)S(1)} %pad_add_fusion.scalars_ref, s32[192]{0:T(256)S(1)} %sub.19.ids_ref, bf16[64,3,128,128]{3,2,1,0:T(8,128)(2,1)S(1)} %bitcast.17, bf16[64,64,128]{2,1,0:T(8,128)(2,1)S(1)} %shard_map.55.coef_ref), custom_call_target="tpu_custom_call" | custom-call | tf_op jit(solution)/shard_map/pallas_call | solution.py:73
  12.3 0.0 copy-start.3
  12.3 0.2 collective-permute-done
  12.5 0.2 add_convert_fusion.1
  12.7 16.7 %all_to_all.40 = bf16[32,64,128]{2,1,0:T(8,128)(2,1)S(1)} all-to-all(bf16[32,64,128]{2,1,0:T(8,128)(2,1)S(1)} %add_convert_fusion.1), channel_id=1, replica_groups={{0,2,4,6,8,10,12,14},{1,3,5,7,9,11,13,15},{16,18,20,22,24,26,28,30},{17..., dimensions={0} | all-to-all | bytes 1048576 | tf_op jit(solution)/shard_map/all_to_all | solution.py:260
  29.4 0.0 copy-done.3
  29.4 0.7 shard_map.58
  30.1 13.6 %all_to_all.41.scaled_ref = bf16[8,272,128]{2,1,0:T(8,128)(2,1)S(1)} all-to-all(bf16[8,272,128]{2,1,0:T(8,128)(2,1)S(1)} %shard_map.58), channel_id=1, replica_groups={{0,2,4,6,8,10,12,14},{1,3,5,7,9,11,13,15},{16,18,20,22,24,26,28,30},{17..., dimensions={0} | all-to-all | bytes 1114112 | tf_op jit(solution)/shard_map/all_to_all | solution.py:260
  43.6 0.0 collective-permute-start.1
  43.7 0.0 slice-done
  43.7 0.0 slice-done.1
  43.7 2.6 %shard_map.59 = (f32[64,64,128]{2,1,0:T(8,128)S(1)}, f32[64,8,128]{2,1,0:T(8,128)S(1)}) custom-call(s32[4]{0:T(128)S(1)} %pad_add_fusion.scalars_ref, s32[192]{0:T(256)S(1)} %sub.19.ids_ref, bf16[64,3,128,128]{3,2,1,0:T(8,128)(2,1)S(1)} %bitcast.20, bf16[8,272,128]{2,1,0:T(8,128)(2,1)S(1)} %all_to_all.41.scaled_ref), custom_call_target="tpu_custom_call" | custom-call | tf_op jit(solution)/shard_map/pallas_call | solution.py:179
  46.2 0.0 collective-permute-done.1.scaled_ref
  46.3 2.9 %shard_map.60 = (bf16[8,528,128]{2,1,0:T(8,128)(2,1)S(1)}, f32[64,64,128]{2,1,0:T(8,128)S(1)}) custom-call(s32[4]{0:T(128)S(1)} %pad_add_fusion.scalars_ref, s32[192]{0:T(256)S(1)} %sub.19.ids_ref, bf16[64,3,128,128]{3,2,1,0:T(8,128)(2,1)S(1)} %bitcast.21, bf16[8,272,128]{2,1,0:T(8,128)(2,1)S(1)} %collective-permute-done.1.scaled_ref, ...), custom_call_target="tpu_custom_call" | custom-call | tf_op jit(solution)/shard_map/pallas_call | solution.py:179
  49.1 0.0 copy-start.2
  49.1 25.0 %all_to_all.42.parts_ref = bf16[8,528,128]{2,1,0:T(8,128)(2,1)S(1)} all-to-all(bf16[8,528,128]{2,1,0:T(8,128)(2,1)S(1)} %get-tuple-element.15), channel_id=1, replica_groups=mesh['row'=8,'feat'=16] {'row'}, dimensions={0} | all-to-all | bytes 2162688 | tf_op jit(solution)/shard_map/all_to_all | solution.py:263
  74.1 0.0 copy-done.2
  74.1 0.7 shard_map.61
  74.9 19.5 %all_to_all.43 = bf16[8,8,64,128]{3,2,1,0:T(8,128)(2,1)S(1)} all-to-all(bf16[8,8,64,128]{3,2,1,0:T(8,128)(2,1)S(1)} %get-tuple-element.16.refs_0_), channel_id=1, replica_groups=mesh['row'=8,'feat'=16] {'row'}, dimensions={0} | all-to-all | bytes 2097152 | tf_op jit(solution)/shard_map/all_to_all | solution.py:263
  94.4 2.4 %shard_map.63 = f32[32,64,128]{2,1,0:T(8,128)S(1)} custom-call(s32[4]{0:T(128)S(1)} %pad_add_fusion.scalars_ref, s32[192]{0:T(256)S(1)} %sub.19.ids_ref, bf16[64,3,128,128]{3,2,1,0:T(8,128)(2,1)S(1)} %bitcast.22, bf16[64,64,128]{2,1,0:T(8,128)(2,1)S(1)} %bitcast.26), custom_call_target="tpu_custom_call" | custom-call | tf_op jit(solution)/shard_map/pallas_call | solution.py:73
  96.8 0.1 collective-permute-start.2
  96.9 2.4 %shard_map.62 = f32[32,64,128]{2,1,0:T(8,128)S(1)} custom-call(s32[4]{0:T(128)S(1)} %pad_add_fusion.scalars_ref, s32[192]{0:T(256)S(1)} %sub.19.ids_ref, bf16[64,3,128,128]{3,2,1,0:T(8,128)(2,1)S(1)} %bitcast.23, bf16[64,64,128]{2,1,0:T(8,128)(2,1)S(1)} %bitcast.27), custom_call_target="tpu_custom_call" | custom-call | tf_op jit(solution)/shard_map/pallas_call | solution.py:73
  99.3 0.2 collective-permute-done.2
  99.6 0.2 add_convert_fusion
  99.7 13.0 %all_to_all.44 = bf16[32,64,128]{2,1,0:T(8,128)(2,1)S(1)} all-to-all(bf16[32,64,128]{2,1,0:T(8,128)(2,1)S(1)} %add_convert_fusion), channel_id=1, replica_groups={{0,2,4,6,8,10,12,14},{1,3,5,7,9,11,13,15},{16,18,20,22,24,26,28,30},{17..., dimensions={0} | all-to-all | bytes 1048576 | tf_op jit(solution)/shard_map/all_to_all | solution.py:260
  112.7 0.7 shard_map.64
  113.4 13.7 %all_to_all.45.scaled_ref = bf16[8,272,128]{2,1,0:T(8,128)(2,1)S(1)} all-to-all(bf16[8,272,128]{2,1,0:T(8,128)(2,1)S(1)} %shard_map.64), channel_id=1, replica_groups={{0,2,4,6,8,10,12,14},{1,3,5,7,9,11,13,15},{16,18,20,22,24,26,28,30},{17..., dimensions={0} | all-to-all | bytes 1114112 | tf_op jit(solution)/shard_map/all_to_all | solution.py:260
  127.1 0.0 collective-permute-start.3
  127.1 2.6 %shard_map.65 = (f32[64,64,128]{2,1,0:T(8,128)S(1)}, f32[64,8,128]{2,1,0:T(8,128)S(1)}) custom-call(s32[4]{0:T(128)S(1)} %pad_add_fusion.scalars_ref, s32[192]{0:T(256)S(1)} %sub.19.ids_ref, bf16[64,3,128,128]{3,2,1,0:T(8,128)(2,1)S(1)} %bitcast.24, bf16[8,272,128]{2,1,0:T(8,128)(2,1)S(1)} %all_to_all.45.scaled_ref, f32[64,64,128]{2,1,0:T(8,128)S(1)} %get-tuple-element.17.refs_0_), custom_call_target="tpu_custom_call" | custom-call | tf_op jit(solution)/shard_map/pallas_call | solution.py:179
  129.6 0.0 collective-permute-done.3.scaled_ref
  129.6 2.8 %shard_map.66 = bf16[8,528,128]{2,1,0:T(8,128)(2,1)S(1)} custom-call(s32[4]{0:T(128)S(1)} %pad_add_fusion.scalars_ref, s32[192]{0:T(256)S(1)} %sub.19.ids_ref, bf16[64,3,128,128]{3,2,1,0:T(8,128)(2,1)S(1)} %bitcast.25, bf16[8,272,128]{2,1,0:T(8,128)(2,1)S(1)} %collective-permute-done.3.scaled_ref, f32[64,64,128]{2,1,0:T(8,128)S(1)} %get-tuple-element.18.refs_0_, ...), custom_call_target="tpu_custom_call" | custom-call | tf_op jit(solution)/shard_map/pallas_call | solution.py:179
  132.4 21.1 %all_to_all.46.parts_ref = bf16[8,528,128]{2,1,0:T(8,128)(2,1)S(1)} all-to-all(bf16[8,528,128]{2,1,0:T(8,128)(2,1)S(1)} %shard_map.66), channel_id=1, replica_groups=mesh['row'=8,'feat'=16] {'row'}, dimensions={0} | all-to-all | bytes 2162688 | tf_op jit(solution)/shard_map/all_to_all | solution.py:263
  153.5 0.7 shard_map.67
  154.3 19.6 %all_to_all.47 = bf16[8,8,64,128]{3,2,1,0:T(8,128)(2,1)S(1)} all-to-all(bf16[8,8,64,128]{3,2,1,0:T(8,128)(2,1)S(1)} %shard_map.67), channel_id=1, replica_groups=mesh['row'=8,'feat'=16] {'row'}, dimensions={0} | all-to-all | bytes 2097152 | tf_op jit(solution)/shard_map/all_to_all | solution.py:263
  173.9 1.9 %shard_map.68 = f32[64,8192]{1,0:T(8,128)} custom-call(bf16[64,64,128]{2,1,0:T(8,128)(2,1)S(1)} %bitcast.28, bf16[64,64,128]{2,1,0:T(8,128)(2,1)S(1)} %bitcast.33), custom_call_target="tpu_custom_call" | custom-call | tf_op jit(solution)/shard_map/pallas_call | solution.py:241
  (2 shorter events, 0.0 us)
Async XLA Ops:
  1.0 1.6 copy-start.1
  4.5 2.8 %copy-start = (bf16[1,8,8,3,128,128]{5,4,3,2,1,0:T(8,128)(2,1)S(1)}, bf16[1,8,8,3,128,128]{5,4,3,2,1,0:T(8,128)(2,1)}, u32[]{:S(2)}) copy-start(bf16[1,8,8,3,128,128]{5,4,3,2,1,0:T(8,128)(2,1)} %param.5) | copy-start | bytes 18874372
  7.3 36.3 %slice-start = ((s8[6291456]{0:T(1024)(128)(4,1)}), s8[4194304]{0:T(1024)(128)(4,1)S(1)}, s32[]{:S(2)}) async-start(s8[6291456]{0:T(1024)(128)(4,1)} %bitcast.18), calls=%async_computation.8 | async-start | bytes 8388608
  9.8 33.9 %slice-start.1 = ((s8[6291456]{0:T(1024)(128)(4,1)}), s8[2097152]{0:T(1024)(128)(4,1)S(1)}, s32[]{:S(2)}) async-start(s8[6291456]{0:T(1024)(128)(4,1)} %bitcast.18), calls=%async_computation.9 | async-start | bytes 4194304
  9.8 2.7 %collective-permute-start = (f32[32,64,128]{2,1,0:T(8,128)S(1)}, f32[32,64,128]{2,1,0:T(8,128)S(1)}, u32[]{:S(2)}, u32[]{:S(2)}) collective-permute-start(f32[32,64,128]{2,1,0:T(8,128)S(1)} %shard_map.57), channel_id=1, source_target_pairs={{0,1},{1,0},{2,3},{3,2},{4,5},{5,4},{6,7},{7,6},{8,9},{9,8},{10,11... | collective-permute-start | bytes 3145736 | tf_op jit(solution)/shard_map/ppermute | solution.py:257
  12.3 17.1 %copy-start.3 = (bf16[1,8,8,128,64]{3,4,2,1,0:T(8,128)(2,1)S(1)}, bf16[1,8,8,128,64]{3,4,2,1,0:T(8,128)(2,1)}, u32[]{:S(2)}) copy-start(bf16[1,8,8,128,64]{3,4,2,1,0:T(8,128)(2,1)} %param.7) | copy-start | bytes 3145732
  43.6 2.6 %collective-permute-start.1 = (bf16[8,272,128]{2,1,0:T(8,128)(2,1)S(1)}, bf16[8,272,128]{2,1,0:T(8,128)(2,1)S(1)}, u32[]{:S(2)}, u32[]{:S(2)}) collective-permute-start(bf16[8,272,128]{2,1,0:T(8,128)(2,1)S(1)} %all_to_all.41.scaled_ref), channel_id=1, source_target_pairs={{0,1},{1,0},{2,3},{3,2},{4,5},{5,4},{6,7},{7,6},{8,9},{9,8},{10,11... | collective-permute-start | bytes 1671176 | tf_op jit(solution)/shard_map/ppermute | solution.py:257
  49.1 25.0 %copy-start.2 = (f32[8192,64]{0,1:T(8,128)S(1)}, f32[8192,64]{0,1:T(8,128)}, u32[]{:S(2)}) copy-start(f32[8192,64]{0,1:T(8,128)} %param.9) | copy-start | bytes 6291460
  96.8 2.7 %collective-permute-start.2 = (f32[32,64,128]{2,1,0:T(8,128)S(1)}, f32[32,64,128]{2,1,0:T(8,128)S(1)}, u32[]{:S(2)}, u32[]{:S(2)}) collective-permute-start(f32[32,64,128]{2,1,0:T(8,128)S(1)} %shard_map.63), channel_id=1, source_target_pairs={{0,1},{1,0},{2,3},{3,2},{4,5},{5,4},{6,7},{7,6},{8,9},{9,8},{10,11... | collective-permute-start | bytes 3145736 | tf_op jit(solution)/shard_map/ppermute | solution.py:257
  127.1 2.6 %collective-permute-start.3 = (bf16[8,272,128]{2,1,0:T(8,128)(2,1)S(1)}, bf16[8,272,128]{2,1,0:T(8,128)(2,1)S(1)}, u32[]{:S(2)}, u32[]{:S(2)}) collective-permute-start(bf16[8,272,128]{2,1,0:T(8,128)(2,1)S(1)} %all_to_all.45.scaled_ref), channel_id=1, source_target_pairs={{0,1},{1,0},{2,3},{3,2},{4,5},{5,4},{6,7},{7,6},{8,9},{9,8},{10,11... | collective-permute-start | bytes 1671176 | tf_op jit(solution)/shard_map/ppermute | solution.py:257

commit v3 on v2

--- a/solution.py
+++ b/solution.py
@@ -11,13 +11,14 @@
 F32 = jnp.float32
 BF16 = jnp.bfloat16
 VMEM_LIMIT = 16 * 1024 * 1024
+FIRST_LIMIT = 50 * 1024 * 1024
 
 LANES = 128
 PAD = 16
 
 
-def params():
-    return pltpu.CompilerParams(vmem_limit_bytes=VMEM_LIMIT)
+def params(limit=VMEM_LIMIT):
+    return pltpu.CompilerParams(vmem_limit_bytes=limit)
 
 
 def whole(count, scalars):
@@ -26,67 +27,122 @@
     return [smem] * scalars + [vmem] * count
 
 
-def coef_blocks(start_t):
+def place():
+    feat = lax.axis_index("feat")
+    return lax.axis_index("row"), feat % 2, feat // 2
+
+
+def side(other):
+    core = lax.axis_index("feat") % 2
+    return 1 - core if other else core
+
+
+def predict_block(ids_ref, tiles_ref, coef_ref, at, row_block, kt):
+    picked = [coef_ref[ids_ref[row_block * kt + k]] for k in range(kt)]
+    placed = [tiles_ref[at, k] for k in range(kt)]
+    return lax.dot_general(
+        jnp.concatenate(picked, axis=1),
+        jnp.concatenate(placed, axis=1),
+        (((1,), (1,)), ((), ())),
+        preferred_element_type=F32,
+    )
+
+
+def predict_stream(ids, tiles, other, start_t, coef=None):
+    row_blocks, kt, rows, width = tiles.shape
     columns, features = start_t.shape
-    blocks = features // LANES
-
-    def kernel(start_ref, out_ref):
-        for b in range(blocks):
-            out_ref[b] = start_ref[:, b * LANES : (b + 1) * LANES].astype(BF16)
-
-    return pl.pallas_call(
-        kernel,
-        in_specs=whole(1, 0),
-        out_specs=whole(1, 0)[0],
-        out_shape=jax.ShapeDtypeStruct((blocks, columns, LANES), BF16),
-        compiler_params=params(),
-    )(start_t)
-
-
-def side(scalars_ref, other):
-    return 1 - scalars_ref[0] if other else scalars_ref[0]
-
-
-def predict_half(scalars, ids, tiles, coef, other):
+    blocks = features // width
+    half = row_blocks // 2
+    step = 8
+    pieces = half // step
+    coef_pieces = 4
+    share = features // coef_pieces
+    makes = coef is None
+
+    def kernel(ids_ref, tiles_hbm, source_ref, out_ref, *refs):
+        if makes:
+            coef_ref, held, tile_sem, start_ref, start_sem = refs
+        else:
+            coef_ref, (held, tile_sem) = source_ref, refs
+        base = side(other) * half
+        starts, copies = [], []
+        if makes:
+            for p in range(coef_pieces):
+                at = pl.ds(p * share, share)
+                starts.append(
+                    pltpu.make_async_copy(source_ref.at[:, at], start_ref.at[:, at], start_sem.at[p])
+                )
+        for p in range(pieces):
+            copies.append(
+                pltpu.make_async_copy(
+                    tiles_hbm.at[pl.ds(base + p * step, step)],
+                    held.at[pl.ds(p * step, step)],
+                    tile_sem.at[p],
+                )
+            )
+        for copy in starts + copies:
+            copy.start()
+        for p in range(len(starts)):
+            starts[p].wait()
+            for b in range(p * blocks // coef_pieces, (p + 1) * blocks // coef_pieces):
+                coef_ref[b] = start_ref[:, b * width : (b + 1) * width].astype(BF16)
+        for p in range(pieces):
+            copies[p].wait()
+            for r in range(step):
+                at = p * step + r
+                out_ref[at] = predict_block(ids_ref, held, coef_ref, at, base + at, kt)
+
+    hbm = pl.BlockSpec(memory_space=pltpu.HBM)
+    out_shape = [jax.ShapeDtypeStruct((half, columns, rows), F32)]
+    scratch = [pltpu.VMEM((half, kt, rows, width), BF16), pltpu.SemaphoreType.DMA((pieces,))]
+    if makes:
+        out_shape.append(jax.ShapeDtypeStruct((blocks, columns, width), BF16))
+        scratch += [pltpu.VMEM(start_t.shape, F32), pltpu.SemaphoreType.DMA((coef_pieces,))]
+    return pl.pallas_call(
+        kernel,
+        in_specs=whole(0, 1) + [hbm] + ([hbm] if makes else whole(1, 0)),
+        out_specs=whole(len(out_shape), 0),
+        out_shape=out_shape,
+        scratch_shapes=scratch,
+        compiler_params=params(FIRST_LIMIT),
+    )(ids, tiles, start_t if makes else coef)
+
+
+def predict_half(ids, tiles, coef, other):
     row_blocks, kt, rows, width = tiles.shape
     columns = coef.shape[1]
     half = row_blocks // 2
     step = 8
 
-    def kernel(scalars_ref, ids_ref, tiles_ref, coef_ref, out_ref):
-        base = side(scalars_ref, other) * half
+    def kernel(ids_ref, tiles_ref, coef_ref, out_ref):
+        base = side(other) * half
 
         @pl.loop(0, half // step)
         def _(i):
             for r in range(step):
                 at = i * step + r
-                row_block = base + at
-                picked = [coef_ref[ids_ref[row_block * kt + k]] for k in range(kt)]
-                placed = [tiles_ref[row_block, k] for k in range(kt)]
-                out_ref[at] = lax.dot_general(
-                    jnp.concatenate(picked, axis=1),
-                    jnp.concatenate(placed, axis=1),
-                    (((1,), (1,)), ((), ())),
-                    preferred_element_type=F32,
-                )
-
-    return pl.pallas_call(
-        kernel,
-        in_specs=whole(2, 2),
+                out_ref[at] = predict_block(ids_ref, tiles_ref, coef_ref, base + at, base + at, kt)
+
+    return pl.pallas_call(
+        kernel,
+        in_specs=whole(2, 1),
         out_specs=whole(1, 0)[0],
         out_shape=jax.ShapeDtypeStruct((half, columns, rows), F32),
         compiler_params=params(),
-    )(scalars, ids, tiles, coef)
-
-
-def weigh(scalars, parts, resp_t, copies):
+    )(ids, tiles, coef)
+
+
+def weigh(n_feat, live, parts, resp_t, copies):
     sources, count, columns, rows = parts.shape
     threshold = 1.4 * columns**0.5
     height = count * columns + PAD
 
-    def kernel(scalars_ref, parts_ref, resp_ref, out_ref):
-        flag = scalars_ref[1].astype(F32)
-        first = scalars_ref[2] * count
+    slots = resp_t.shape[0] // live.shape[1]
+
+    def kernel(live_ref, parts_ref, resp_ref, out_ref):
+        row, core, chip = place()
+        first = (core * (n_feat // 2) + chip) * count
+        flag = live_ref[row, first // slots].astype(F32)
         lines = []
         for r in range(count):
             predicted = parts_ref[0, r].astype(F32)
@@ -110,10 +166,10 @@
         out_specs=whole(1, 0)[0],
         out_shape=jax.ShapeDtypeStruct((copies, height, rows), BF16),
         compiler_params=params(),
-    )(scalars, parts, resp_t)
-
-
-def gradient_half(scalars, ids, tiles, scaled, other, local_blocks, groups, before, keep_error):
+    )(live, parts, resp_t)
+
+
+def gradient_half(ids, tiles, scaled, other, local_blocks, groups, before, keep_error):
     row_blocks, kt, rows, width = tiles.shape
     sources, height, _ = scaled.shape
     half = row_blocks // 2
@@ -122,13 +178,13 @@
     owned = local_blocks // groups
     n_before = len(before)
 
-    def kernel(scalars_ref, ids_ref, tiles_ref, scaled_ref, *refs):
+    def kernel(ids_ref, tiles_ref, scaled_ref, *refs):
         before_refs, refs = refs[:n_before], refs[n_before:]
         if other:
             out_ref = refs[0]
             error_ref = refs[1] if keep_error else None
         grad, curv = refs[-2:]
-        base = side(scalars_ref, other) * half
+        base = side(other) * half
         for ref, start in zip((grad, curv), list(before_refs) + [None] * (2 - n_before)):
             ref[...] = jnp.zeros_like(ref) if start is None else start[...]
 
@@ -178,21 +234,21 @@
         out_shape = [jax.ShapeDtypeStruct(grad_shape, F32), jax.ShapeDtypeStruct(curv_shape, F32)]
     return pl.pallas_call(
         kernel,
-        in_specs=whole(2 + n_before, 2),
+        in_specs=whole(2 + n_before, 1),
         out_specs=whole(len(out_shape), 0),
         out_shape=out_shape,
         scratch_shapes=scratch,
         compiler_params=params(),
-    )(scalars, ids, tiles, scaled, *before)
-
-
-def update(scalars, parts, exact, known, copies, owned):
+    )(ids, tiles, scaled, *before)
+
+
+def update(parts, exact, known, copies, owned):
     sources, height, width = parts.shape
     columns = (height - PAD) // owned
     shape = (owned, columns, width)
     first = known is None
 
-    def kernel(scalars_ref, parts_ref, exact_ref, *refs):
+    def kernel(parts_ref, exact_ref, *refs):
         sent_ref = refs[-1]
 
         def total(lo, hi):
@@ -205,7 +261,7 @@
         for b in range(owned):
             gradient = total(b * columns, (b + 1) * columns)
             if first:
-                at = pl.multiple_of((scalars_ref[3] * owned + b) * width, width)
+                at = pl.multiple_of((lax.axis_index("row") * owned + b) * width, width)
                 coef = exact_ref[:, pl.ds(at, width)]
             else:
                 coef = exact_ref[b]
@@ -222,28 +278,36 @@
         out_shape.insert(0, jax.ShapeDtypeStruct(shape, F32))
     return pl.pallas_call(
         kernel,
-        in_specs=whole(2 + (not first), 1),
+        in_specs=whole(2 + (not first), 0),
         out_specs=whole(len(out_shape), 0),
         out_shape=out_shape,
         compiler_params=params(),
-    )(scalars, parts, exact, *(() if first else (known,)))
+    )(parts, exact, *(() if first else (known,)))
 
 
 def finish(known, change):
     blocks, columns, width = known.shape
-    step = 16
-
-    def kernel(known_ref, change_ref, out_ref):
-        for b in range(step):
-            value = known_ref[b].astype(F32) + change_ref[b].astype(F32)
-            out_ref[:, b * width : (b + 1) * width] = value
-
-    return pl.pallas_call(
-        kernel,
-        grid=(blocks // step,),
-        in_specs=[pl.BlockSpec((step, columns, width), lambda i: (i, 0, 0))] * 2,
-        out_specs=pl.BlockSpec((columns, step * width), lambda i: (0, i)),
-        out_shape=jax.ShapeDtypeStruct((columns, blocks * width), F32),
+    pieces = 4
+    step = blocks // pieces
+
+    def kernel(known_ref, change_ref, out_hbm, held, sem):
+        copies = []
+        for p in range(pieces):
+            for b in range(p * step, (p + 1) * step):
+                held[:, b * width : (b + 1) * width] = known_ref[b].astype(F32) + change_ref[b].astype(F32)
+            at = pl.ds(p * step * width, step * width)
+            copies.append(pltpu.make_async_copy(held.at[:, at], out_hbm.at[:, at], sem.at[p]))
+            copies[p].start()
+        for copy in copies:
+            copy.wait()
+
+    shape = (columns, blocks * width)
+    return pl.pallas_call(
+        kernel,
+        in_specs=whole(2, 0),
+        out_specs=pl.BlockSpec(memory_space=pltpu.HBM),
+        out_shape=jax.ShapeDtypeStruct(shape, F32),
+        scratch_shapes=[pltpu.VMEM(shape, F32), pltpu.SemaphoreType.DMA((pieces,))],
         compiler_params=params(),
     )(known, change)
 
@@ -265,7 +329,6 @@
     def body(design_tiles, block_ids, responses, live_groups, start_coef):
         row = lax.axis_index("row")
         feat = lax.axis_index("feat")
-        core, yz = feat % 2, feat // 2
         _, owners, slots, kt, rows, width = design_tiles.shape
         row_blocks = owners * slots
         features, columns = start_coef.shape
@@ -276,28 +339,30 @@
         ids = lax.dynamic_index_in_dim(block_ids, row, 0, keepdims=False).reshape(-1)
         ids = (ids - feat * local_blocks).astype(jnp.int32)
         share = row_blocks // n_feat
-        mine = core * n_yz + yz
-        live = lax.dynamic_index_in_dim(live_groups, row, 0, keepdims=False)
-        flag = live[mine * share // slots]
-        scalars = jnp.stack([core, flag, mine, row]).astype(jnp.int32)
         owned = local_blocks // n_row
 
-        known, exact, sent, carried = coef_blocks(start_t), start_t, None, ()
+        known = None
+        exact, sent, carried = start_t, None, ()
         for iteration in range(ITERS):
             ends = iteration == ITERS - 1
-            arrived = swap_core(predict_half(scalars, ids, tiles, known, True))
-            kept = predict_half(scalars, ids, tiles, known, False)
+            if iteration == 0:
+                ahead, known = predict_stream(ids, tiles, True, start_t)
+                arrived = swap_core(ahead)
+                [kept] = predict_stream(ids, tiles, False, start_t, known)
+            else:
+                arrived = swap_core(predict_half(ids, tiles, known, True))
+                kept = predict_half(ids, tiles, known, False)
             pair = (kept + arrived).astype(BF16)
             parts = exchange_feat(pair).reshape(n_yz, share, columns, rows)
-            scaled = exchange_feat(weigh(scalars, parts, resp_t, n_yz))
+            scaled = exchange_feat(weigh(n_feat, live_groups, parts, resp_t, n_yz))
             scaled_there = swap_core(scaled)
             before = gradient_half(
-                scalars, ids, tiles, scaled, False, local_blocks, n_row, carried, False
+                ids, tiles, scaled, False, local_blocks, n_row, carried, False
             )
             partial, *carried = gradient_half(
-                scalars, ids, tiles, scaled_there, True, local_blocks, n_row, before, not ends
+                ids, tiles, scaled_there, True, local_blocks, n_row, before, not ends
             )
-            *new, sent = update(scalars, exchange_row(partial), exact, sent, n_row, owned)
+            *new, sent = update(exchange_row(partial), exact, sent, n_row, owned)
             gathered = exchange_row(sent).reshape(local_blocks, columns, width)
             if ends:
                 return finish(known, gathered).T

time: 176 us -> 172 us (0.977)
  local copies, waits for them, and re-layouts: 5.9 us -> 0.29 us
  Pallas kernels: 25.2 us -> 27.2 us
    unnamed x12 -> x10, local copies, waits for them, and re-layouts: 4.4 us -> 0.03 us
    pallas_call x12 -> x11, Pallas kernels: 23.9 us -> 25.7 us  [the longest x4 10.8 us: gradient_half(): pl.pallas_call(kernel, in_specs=whole(2 + n_before, 1), out_specs=whole(l...]
  transfers between devices with their start and end apart: 4 -> 4, of which waited for: 2 -> 1; matrix products, arithmetic and copies ran while one was open for 0% -> 0% of each run, Pallas kernels for 6% -> 7%
where the time goes in v3:
time: 172 us; the launch traced here: 171 us
  blocking collectives  142 us (83%)
  Pallas kernels  27.2 us (16%)
    all_to_all x4, blocking collectives, exchange_row(): return lax.all_to_all(x, 'row', 0, 0, tiled=True)  85.2 us
    all_to_all x4, blocking collectives, exchange_feat(): return lax.all_to_all(x, 'feat', 0, 0, axis_index_groups=chips, tiled=True)  57.1 us
    pallas_call x4, Pallas kernels, gradient_half(): pl.pallas_call(kernel, in_specs=whole(2 + n_before, 1), out_specs=whole(l...  10.8 us
    pallas_call x2, Pallas kernels, predict_stream(): pl.pallas_call(kernel, in_specs=whole(0, 1) + [hbm] + ([hbm] if makes els...  8.25 us
    pallas_call x2, Pallas kernels, predict_half(): pl.pallas_call(kernel, in_specs=whole(2, 1), out_specs=whole(1, 0)[0], ou...  4.86 us
  transfers between devices with their start and end apart: 4, of which 1 were waited for; matrix products, arithmetic and copies ran while one was open for 0% of the time, Pallas kernels for 7%

profile of v3, /device:TPU:0, one launch (start us, length us, event | category | flops | bytes accessed | tf_op | source)
XLA Modules:
  0.0 171.4 jit_solution(18402352056474480826)
XLA Ops:
  0.0 0.7 dynamic-slice_subtract_fusion
  0.7 0.1 copy.6
  0.8 0.1 sub.10.ids_ref
  1.0 4.3 %shard_map.55 = (f32[32,64,128]{2,1,0:T(8,128)S(1)}, bf16[64,64,128]{2,1,0:T(8,128)(2,1)S(1)}) custom-call(s32[192]{0:T(256)S(1)} %sub.10.ids_ref, bf16[64,3,128,128]{3,2,1,0:T(8,128)(2,1)} %bitcast.12, f32[64,8192]{1,0:T(8,128)} %bitcast.25), custom_call_target="tpu_custom_call" | custom-call | tf_op jit(solution)/shard_map/pallas_call | solution.py:101
  5.3 0.1 collective-permute-start
  5.4 0.0 slice-start
  5.4 0.0 slice-start.1
  5.4 3.9 %shard_map.56 = f32[32,64,128]{2,1,0:T(8,128)S(1)} custom-call(s32[192]{0:T(256)S(1)} %sub.10.ids_ref, bf16[64,3,128,128]{3,2,1,0:T(8,128)(2,1)} %bitcast.13, bf16[64,64,128]{2,1,0:T(8,128)(2,1)S(1)} %get-tuple-element.15.source_ref), custom_call_target="tpu_custom_call" | custom-call | tf_op jit(solution)/shard_map/pallas_call | solution.py:101
  9.4 0.0 copy-start.1
  9.4 0.0 copy-start.2
  9.4 0.0 collective-permute-done
  9.4 0.2 add_convert_fusion.1
  9.6 16.9 %all_to_all.40 = bf16[32,64,128]{2,1,0:T(8,128)(2,1)S(1)} all-to-all(bf16[32,64,128]{2,1,0:T(8,128)(2,1)S(1)} %add_convert_fusion.1), channel_id=1, replica_groups={{0,2,4,6,8,10,12,14},{1,3,5,7,9,11,13,15},{16,18,20,22,24,26,28,30},{17..., dimensions={0} | all-to-all | bytes 1048576 | tf_op jit(solution)/shard_map/all_to_all | solution.py:324
  26.4 0.0 copy-done.1
  26.4 0.0 copy-done.2
  26.4 0.7 shard_map.57
  27.2 13.6 %all_to_all.41.scaled_ref = bf16[8,272,128]{2,1,0:T(8,128)(2,1)S(1)} all-to-all(bf16[8,272,128]{2,1,0:T(8,128)(2,1)S(1)} %shard_map.57), channel_id=1, replica_groups={{0,2,4,6,8,10,12,14},{1,3,5,7,9,11,13,15},{16,18,20,22,24,26,28,30},{17..., dimensions={0} | all-to-all | bytes 1114112 | tf_op jit(solution)/shard_map/all_to_all | solution.py:324
  40.8 0.0 collective-permute-start.1
  40.8 0.0 slice-done
  40.8 0.0 slice-done.1
  40.8 2.6 %shard_map.58 = (f32[64,64,128]{2,1,0:T(8,128)S(1)}, f32[64,8,128]{2,1,0:T(8,128)S(1)}) custom-call(s32[192]{0:T(256)S(1)} %sub.10.ids_ref, bf16[64,3,128,128]{3,2,1,0:T(8,128)(2,1)S(1)} %bitcast.16, bf16[8,272,128]{2,1,0:T(8,128)(2,1)S(1)} %all_to_all.41.scaled_ref), custom_call_target="tpu_custom_call" | custom-call | tf_op jit(solution)/shard_map/pallas_call | solution.py:235
  43.4 0.0 collective-permute-done.1.scaled_ref
  43.4 2.9 %shard_map.59 = (bf16[8,528,128]{2,1,0:T(8,128)(2,1)S(1)}, f32[64,64,128]{2,1,0:T(8,128)S(1)}) custom-call(s32[192]{0:T(256)S(1)} %sub.10.ids_ref, bf16[64,3,128,128]{3,2,1,0:T(8,128)(2,1)S(1)} %bitcast.17, bf16[8,272,128]{2,1,0:T(8,128)(2,1)S(1)} %collective-permute-done.1.scaled_ref, f32[64,64,128]{2,1,0:T(8,128)S(1)} %get-tuple-element.17.refs_0_, ...), custom_call_target="tpu_custom_call" | custom-call | tf_op jit(solution)/shard_map/pallas_call | solution.py:235
  46.3 0.0 copy-start
  46.3 25.0 %all_to_all.42.parts_ref = bf16[8,528,128]{2,1,0:T(8,128)(2,1)S(1)} all-to-all(bf16[8,528,128]{2,1,0:T(8,128)(2,1)S(1)} %get-tuple-element.19), channel_id=1, replica_groups=mesh['row'=8,'feat'=16] {'row'}, dimensions={0} | all-to-all | bytes 2162688 | tf_op jit(solution)/shard_map/all_to_all | solution.py:327
  71.3 0.0 copy-done
  71.3 0.2 shard_map.60
  71.5 19.5 %all_to_all.43 = bf16[8,8,64,128]{3,2,1,0:T(8,128)(2,1)S(1)} all-to-all(bf16[8,8,64,128]{3,2,1,0:T(8,128)(2,1)S(1)} %get-tuple-element.20.refs_0_), channel_id=1, replica_groups=mesh['row'=8,'feat'=16] {'row'}, dimensions={0} | all-to-all | bytes 2097152 | tf_op jit(solution)/shard_map/all_to_all | solution.py:327
  91.0 2.4 %shard_map.62 = f32[32,64,128]{2,1,0:T(8,128)S(1)} custom-call(s32[192]{0:T(256)S(1)} %sub.10.ids_ref, bf16[64,3,128,128]{3,2,1,0:T(8,128)(2,1)S(1)} %bitcast.18, bf16[64,64,128]{2,1,0:T(8,128)(2,1)S(1)} %bitcast.22), custom_call_target="tpu_custom_call" | custom-call | tf_op jit(solution)/shard_map/pallas_call | solution.py:126
  93.4 0.1 collective-permute-start.2
  93.5 2.4 %shard_map.61 = f32[32,64,128]{2,1,0:T(8,128)S(1)} custom-call(s32[192]{0:T(256)S(1)} %sub.10.ids_ref, bf16[64,3,128,128]{3,2,1,0:T(8,128)(2,1)S(1)} %bitcast.19, bf16[64,64,128]{2,1,0:T(8,128)(2,1)S(1)} %bitcast.23), custom_call_target="tpu_custom_call" | custom-call | tf_op jit(solution)/shard_map/pallas_call | solution.py:126
  96.0 0.2 collective-permute-done.2
  96.2 0.2 add_convert_fusion
  96.4 13.0 %all_to_all.44 = bf16[32,64,128]{2,1,0:T(8,128)(2,1)S(1)} all-to-all(bf16[32,64,128]{2,1,0:T(8,128)(2,1)S(1)} %add_convert_fusion), channel_id=1, replica_groups={{0,2,4,6,8,10,12,14},{1,3,5,7,9,11,13,15},{16,18,20,22,24,26,28,30},{17..., dimensions={0} | all-to-all | bytes 1048576 | tf_op jit(solution)/shard_map/all_to_all | solution.py:324
  109.3 0.7 shard_map.63
  110.0 13.7 %all_to_all.45.scaled_ref = bf16[8,272,128]{2,1,0:T(8,128)(2,1)S(1)} all-to-all(bf16[8,272,128]{2,1,0:T(8,128)(2,1)S(1)} %shard_map.63), channel_id=1, replica_groups={{0,2,4,6,8,10,12,14},{1,3,5,7,9,11,13,15},{16,18,20,22,24,26,28,30},{17..., dimensions={0} | all-to-all | bytes 1114112 | tf_op jit(solution)/shard_map/all_to_all | solution.py:324
  123.8 0.0 collective-permute-start.3
  123.8 2.6 %shard_map.64 = (f32[64,64,128]{2,1,0:T(8,128)S(1)}, f32[64,8,128]{2,1,0:T(8,128)S(1)}) custom-call(s32[192]{0:T(256)S(1)} %sub.10.ids_ref, bf16[64,3,128,128]{3,2,1,0:T(8,128)(2,1)S(1)} %bitcast.20, bf16[8,272,128]{2,1,0:T(8,128)(2,1)S(1)} %all_to_all.45.scaled_ref, f32[64,64,128]{2,1,0:T(8,128)S(1)} %get-tuple-element.21.refs_0_), custom_call_target="tpu_custom_call" | custom-call | tf_op jit(solution)/shard_map/pallas_call | solution.py:235
  126.3 0.0 collective-permute-done.3.scaled_ref
  126.3 2.8 %shard_map.65 = bf16[8,528,128]{2,1,0:T(8,128)(2,1)S(1)} custom-call(s32[192]{0:T(256)S(1)} %sub.10.ids_ref, bf16[64,3,128,128]{3,2,1,0:T(8,128)(2,1)S(1)} %bitcast.21, bf16[8,272,128]{2,1,0:T(8,128)(2,1)S(1)} %collective-permute-done.3.scaled_ref, f32[64,64,128]{2,1,0:T(8,128)S(1)} %get-tuple-element.22.refs_0_, f32[64,8,128]{2,1,0:T(8,128)S(1)} %get-tuple-element.23.refs_1_), custom_call_target="tpu_custom_call" | custom-call | tf_op jit(solution)/shard_map/pallas_call | solution.py:235
  129.1 21.1 %all_to_all.46.parts_ref = bf16[8,528,128]{2,1,0:T(8,128)(2,1)S(1)} all-to-all(bf16[8,528,128]{2,1,0:T(8,128)(2,1)S(1)} %shard_map.65), channel_id=1, replica_groups=mesh['row'=8,'feat'=16] {'row'}, dimensions={0} | all-to-all | bytes 2162688 | tf_op jit(solution)/shard_map/all_to_all | solution.py:327
  150.2 0.2 shard_map.66
  150.5 19.6 %all_to_all.47 = bf16[8,8,64,128]{3,2,1,0:T(8,128)(2,1)S(1)} all-to-all(bf16[8,8,64,128]{3,2,1,0:T(8,128)(2,1)S(1)} %shard_map.66), channel_id=1, replica_groups=mesh['row'=8,'feat'=16] {'row'}, dimensions={0} | all-to-all | bytes 2097152 | tf_op jit(solution)/shard_map/all_to_all | solution.py:327
  170.0 1.4 shard_map.67
  (1 shorter events, 0.0 us)
Async XLA Ops:
  5.3 4.1 %collective-permute-start = (f32[32,64,128]{2,1,0:T(8,128)S(1)}, f32[32,64,128]{2,1,0:T(8,128)S(1)}, u32[]{:S(2)}, u32[]{:S(2)}) collective-permute-start(f32[32,64,128]{2,1,0:T(8,128)S(1)} %get-tuple-element.16), channel_id=1, source_target_pairs={{0,1},{1,0},{2,3},{3,2},{4,5},{5,4},{6,7},{7,6},{8,9},{9,8},{10,11... | collective-permute-start | bytes 3145736 | tf_op jit(solution)/shard_map/ppermute | solution.py:321
  5.4 35.4 %slice-start = ((s8[6291456]{0:T(1024)(128)(4,1)}), s8[4194304]{0:T(1024)(128)(4,1)S(1)}, s32[]{:S(2)}) async-start(s8[6291456]{0:T(1024)(128)(4,1)} %bitcast.14), calls=%async_computation.8 | async-start | bytes 8388608
  5.4 35.4 %slice-start.1 = ((s8[6291456]{0:T(1024)(128)(4,1)}), s8[2097152]{0:T(1024)(128)(4,1)S(1)}, s32[]{:S(2)}) async-start(s8[6291456]{0:T(1024)(128)(4,1)} %bitcast.14), calls=%async_computation.9 | async-start | bytes 4194304
  9.4 17.1 %copy-start.1 = (bf16[1,8,8,128,64]{3,4,2,1,0:T(8,128)(2,1)S(1)}, bf16[1,8,8,128,64]{3,4,2,1,0:T(8,128)(2,1)}, u32[]{:S(2)}) copy-start(bf16[1,8,8,128,64]{3,4,2,1,0:T(8,128)(2,1)} %param.7) | copy-start | bytes 3145732
  9.4 17.1 %copy-start.2 = (s32[8,8]{1,0:T(8,128)S(1)}, s32[8,8]{1,0:T(8,128)}, u32[]{:S(2)}) copy-start(s32[8,8]{1,0:T(8,128)} %live_ref.3) | copy-start | bytes 772
  40.8 2.6 %collective-permute-start.1 = (bf16[8,272,128]{2,1,0:T(8,128)(2,1)S(1)}, bf16[8,272,128]{2,1,0:T(8,128)(2,1)S(1)}, u32[]{:S(2)}, u32[]{:S(2)}) collective-permute-start(bf16[8,272,128]{2,1,0:T(8,128)(2,1)S(1)} %all_to_all.41.scaled_ref), channel_id=1, source_target_pairs={{0,1},{1,0},{2,3},{3,2},{4,5},{5,4},{6,7},{7,6},{8,9},{9,8},{10,11... | collective-permute-start | bytes 1671176 | tf_op jit(solution)/shard_map/ppermute | solution.py:321
  46.3 25.0 %copy-start = (f32[8192,64]{0,1:T(8,128)S(1)}, f32[8192,64]{0,1:T(8,128)}, u32[]{:S(2)}) copy-start(f32[8192,64]{0,1:T(8,128)} %param.9) | copy-start | bytes 6291460
  93.4 2.7 %collective-permute-start.2 = (f32[32,64,128]{2,1,0:T(8,128)S(1)}, f32[32,64,128]{2,1,0:T(8,128)S(1)}, u32[]{:S(2)}, u32[]{:S(2)}) collective-permute-start(f32[32,64,128]{2,1,0:T(8,128)S(1)} %shard_map.62), channel_id=1, source_target_pairs={{0,1},{1,0},{2,3},{3,2},{4,5},{5,4},{6,7},{7,6},{8,9},{9,8},{10,11... | collective-permute-start | bytes 3145736 | tf_op jit(solution)/shard_map/ppermute | solution.py:321
  123.8 2.6 %collective-permute-start.3 = (bf16[8,272,128]{2,1,0:T(8,128)(2,1)S(1)}, bf16[8,272,128]{2,1,0:T(8,128)(2,1)S(1)}, u32[]{:S(2)}, u32[]{:S(2)}) collective-permute-start(bf16[8,272,128]{2,1,0:T(8,128)(2,1)S(1)} %all_to_all.45.scaled_ref), channel_id=1, source_target_pairs={{0,1},{1,0},{2,3},{3,2},{4,5},{5,4},{6,7},{7,6},{8,9},{9,8},{10,11... | collective-permute-start | bytes 1671176 | tf_op jit(solution)/shard_map/ppermute | solution.py:321

commit v4 on v3

--- a/solution.py
+++ b/solution.py
@@ -37,18 +37,24 @@
     return 1 - core if other else core
 
 
-def predict_block(ids_ref, tiles_ref, coef_ref, at, row_block, kt):
-    picked = [coef_ref[ids_ref[row_block * kt + k]] for k in range(kt)]
-    placed = [tiles_ref[at, k] for k in range(kt)]
-    return lax.dot_general(
-        jnp.concatenate(picked, axis=1),
-        jnp.concatenate(placed, axis=1),
+def predict_pair(ids_ref, tiles_ref, coef_ref, out_ref, put, at, row_block, kt):
+    picked, placed = [], []
+    for r in range(2):
+        first = (row_block + r) * kt
+        picked.append(jnp.concatenate([coef_ref[ids_ref[first + k]] for k in range(kt)], axis=1))
+        placed.append(jnp.concatenate([tiles_ref[at + r, k] for k in range(kt)], axis=1))
+    both = lax.dot_general(
+        jnp.concatenate(picked, axis=0),
+        jnp.concatenate(placed, axis=0),
         (((1,), (1,)), ((), ())),
         preferred_element_type=F32,
     )
-
-
-def predict_stream(ids, tiles, other, start_t, coef=None):
+    columns, rows = picked[0].shape[0], placed[0].shape[0]
+    out_ref[put] = both[:columns, :rows]
+    out_ref[put + 1] = both[columns:, rows:]
+
+
+def predict_first(ids, tiles, start_t):
     row_blocks, kt, rows, width = tiles.shape
     columns, features = start_t.shape
     blocks = features // width
@@ -57,21 +63,15 @@
     pieces = half // step
     coef_pieces = 4
     share = features // coef_pieces
-    makes = coef is None
-
-    def kernel(ids_ref, tiles_hbm, source_ref, out_ref, *refs):
-        if makes:
-            coef_ref, held, tile_sem, start_ref, start_sem = refs
-        else:
-            coef_ref, (held, tile_sem) = source_ref, refs
-        base = side(other) * half
+
+    def kernel(ids_ref, tiles_hbm, start_hbm, out_ref, coef_ref, held, tile_sem, start_ref, start_sem):
+        base = side(True) * half
         starts, copies = [], []
-        if makes:
-            for p in range(coef_pieces):
-                at = pl.ds(p * share, share)
-                starts.append(
-                    pltpu.make_async_copy(source_ref.at[:, at], start_ref.at[:, at], start_sem.at[p])
-                )
+        for p in range(coef_pieces):
+            at = pl.ds(p * share, share)
+            starts.append(
+                pltpu.make_async_copy(start_hbm.at[:, at], start_ref.at[:, at], start_sem.at[p])
+            )
         for p in range(pieces):
             copies.append(
                 pltpu.make_async_copy(
@@ -82,46 +82,49 @@
             )
         for copy in starts + copies:
             copy.start()
-        for p in range(len(starts)):
+        for p in range(coef_pieces):
             starts[p].wait()
             for b in range(p * blocks // coef_pieces, (p + 1) * blocks // coef_pieces):
                 coef_ref[b] = start_ref[:, b * width : (b + 1) * width].astype(BF16)
         for p in range(pieces):
             copies[p].wait()
-            for r in range(step):
+            for r in range(0, step, 2):
                 at = p * step + r
-                out_ref[at] = predict_block(ids_ref, held, coef_ref, at, base + at, kt)
+                predict_pair(ids_ref, held, coef_ref, out_ref, at, at, base + at, kt)
 
     hbm = pl.BlockSpec(memory_space=pltpu.HBM)
-    out_shape = [jax.ShapeDtypeStruct((half, columns, rows), F32)]
-    scratch = [pltpu.VMEM((half, kt, rows, width), BF16), pltpu.SemaphoreType.DMA((pieces,))]
-    if makes:
-        out_shape.append(jax.ShapeDtypeStruct((blocks, columns, width), BF16))
-        scratch += [pltpu.VMEM(start_t.shape, F32), pltpu.SemaphoreType.DMA((coef_pieces,))]
-    return pl.pallas_call(
-        kernel,
-        in_specs=whole(0, 1) + [hbm] + ([hbm] if makes else whole(1, 0)),
-        out_specs=whole(len(out_shape), 0),
-        out_shape=out_shape,
-        scratch_shapes=scratch,
+    return pl.pallas_call(
+        kernel,
+        in_specs=whole(0, 1) + [hbm, hbm],
+        out_specs=whole(2, 0),
+        out_shape=[
+            jax.ShapeDtypeStruct((half, columns, rows), F32),
+            jax.ShapeDtypeStruct((blocks, columns, width), BF16),
+        ],
+        scratch_shapes=[
+            pltpu.VMEM((half, kt, rows, width), BF16),
+            pltpu.SemaphoreType.DMA((pieces,)),
+            pltpu.VMEM(start_t.shape, F32),
+            pltpu.SemaphoreType.DMA((coef_pieces,)),
+        ],
         compiler_params=params(FIRST_LIMIT),
-    )(ids, tiles, start_t if makes else coef)
+    )(ids, tiles, start_t)
 
 
 def predict_half(ids, tiles, coef, other):
     row_blocks, kt, rows, width = tiles.shape
     columns = coef.shape[1]
     half = row_blocks // 2
-    step = 8
+    step = 16
 
     def kernel(ids_ref, tiles_ref, coef_ref, out_ref):
         base = side(other) * half
 
         @pl.loop(0, half // step)
         def _(i):
-            for r in range(step):
+            for r in range(0, step, 2):
                 at = i * step + r
-                out_ref[at] = predict_block(ids_ref, tiles_ref, coef_ref, base + at, base + at, kt)
+                predict_pair(ids_ref, tiles_ref, coef_ref, out_ref, at, base + at, base + at, kt)
 
     return pl.pallas_call(
         kernel,
@@ -177,19 +180,15 @@
     columns = (height - PAD) // count
     owned = local_blocks // groups
     n_before = len(before)
+    turn = 2
 
     def kernel(ids_ref, tiles_ref, scaled_ref, *refs):
-        before_refs, refs = refs[:n_before], refs[n_before:]
-        if other:
-            out_ref = refs[0]
-            error_ref = refs[1] if keep_error else None
-        grad, curv = refs[-2:]
+        grad, curv, *out = refs[n_before:]
         base = side(other) * half
-        for ref, start in zip((grad, curv), list(before_refs) + [None] * (2 - n_before)):
-            ref[...] = jnp.zeros_like(ref) if start is None else start[...]
-
-        @pl.loop(0, sources)
-        def _(p):
+        for ref in (grad, curv)[n_before:]:
+            ref[...] = jnp.zeros_like(ref)
+
+        def add(p):
             tail = scaled_ref[p, count * columns :, :].astype(F32)
             for r in range(count):
                 row_block = base + p * count + r
@@ -207,6 +206,11 @@
                     square = wide * wide * weights
                     curv[block] += jnp.sum(square.reshape(rows // 8, 8, width), axis=0)
 
+        @pl.loop(0, sources // turn)
+        def _(i):
+            for t in range(turn):
+                add(i * turn + t)
+
         if other:
 
             @pl.loop(0, groups)
@@ -215,29 +219,25 @@
                 for b in range(owned):
                     at = g * owned + b
                     rounded = grad[at].astype(BF16)
-                    out_ref[g, b * columns : (b + 1) * columns, :] = rounded
+                    out[0][g, b * columns : (b + 1) * columns, :] = rounded
                     if keep_error:
-                        error_ref[at] = grad[at] - rounded.astype(F32)
+                        grad[at] -= rounded.astype(F32)
                     lines.append(jnp.sum(curv[at], axis=0, keepdims=True))
                 lines.append(jnp.zeros((PAD - owned, width), F32))
-                out_ref[g, owned * columns :, :] = jnp.concatenate(lines, axis=0).astype(BF16)
-
-    grad_shape = (local_blocks, columns, width)
-    curv_shape = (local_blocks, 8, width)
-    out_shape, scratch = [], []
+                out[0][g, owned * columns :, :] = jnp.concatenate(lines, axis=0).astype(BF16)
+
+    out_shape = [
+        jax.ShapeDtypeStruct((local_blocks, columns, width), F32),
+        jax.ShapeDtypeStruct((local_blocks, 8, width), F32),
+    ]
     if other:
         out_shape.append(jax.ShapeDtypeStruct((groups, owned * columns + PAD, width), BF16))
-        if keep_error:
-            out_shape.append(jax.ShapeDtypeStruct(grad_shape, F32))
-        scratch = [pltpu.VMEM(grad_shape, F32), pltpu.VMEM(curv_shape, F32)]
-    else:
-        out_shape = [jax.ShapeDtypeStruct(grad_shape, F32), jax.ShapeDtypeStruct(curv_shape, F32)]
     return pl.pallas_call(
         kernel,
         in_specs=whole(2 + n_before, 1),
         out_specs=whole(len(out_shape), 0),
         out_shape=out_shape,
-        scratch_shapes=scratch,
+        input_output_aliases={3 + i: i for i in range(n_before)},
         compiler_params=params(),
     )(ids, tiles, scaled, *before)
 
@@ -346,12 +346,11 @@
         for iteration in range(ITERS):
             ends = iteration == ITERS - 1
             if iteration == 0:
-                ahead, known = predict_stream(ids, tiles, True, start_t)
-                arrived = swap_core(ahead)
-                [kept] = predict_stream(ids, tiles, False, start_t, known)
+                ahead, known = predict_first(ids, tiles, start_t)
             else:
-                arrived = swap_core(predict_half(ids, tiles, known, True))
-                kept = predict_half(ids, tiles, known, False)
+                ahead = predict_half(ids, tiles, known, True)
+            arrived = swap_core(ahead)
+            kept = predict_half(ids, tiles, known, False)
             pair = (kept + arrived).astype(BF16)
             parts = exchange_feat(pair).reshape(n_yz, share, columns, rows)
             scaled = exchange_feat(weigh(n_feat, live_groups, parts, resp_t, n_yz))
@@ -359,9 +358,10 @@
             before = gradient_half(
                 ids, tiles, scaled, False, local_blocks, n_row, carried, False
             )
-            partial, *carried = gradient_half(
+            error, _, partial = gradient_half(
                 ids, tiles, scaled_there, True, local_blocks, n_row, before, not ends
             )
+            carried = (error,)
             *new, sent = update(exchange_row(partial), exact, sent, n_row, owned)
             gathered = exchange_row(sent).reshape(local_blocks, columns, width)
             if ends:

time: 172 us -> 166 us (0.965)
  Pallas kernels: 27.2 us -> 21.4 us
    pallas_call x2 -> x1, Pallas kernels: 8.25 us -> 4.14 us  [predict_first(): pl.pallas_call(kernel, in_specs=whole(0, 1) + [hbm, hbm], out_specs=whole...]
    pallas_call x4, Pallas kernels: 10.8 us -> 8.55 us  [gradient_half(): pl.pallas_call(kernel, in_specs=whole(2 + n_before, 1), out_specs=whole(l...]
    pallas_call x2 -> x3, Pallas kernels: 4.86 us -> 5.45 us  [predict_half(): pl.pallas_call(kernel, in_specs=whole(2, 1), out_specs=whole(1, 0)[0], ou...]
  transfers between devices with their start and end apart: 4 -> 4, of which waited for: 1 -> 2; matrix products, arithmetic and copies ran while one was open for 0% -> 0% of each run, Pallas kernels for 7% -> 5%
where the time goes in v4:
time: 166 us
  blocking collectives  141 us (85%)
  Pallas kernels  21.4 us (13%)
    all_to_all x4, blocking collectives, exchange_row(): return lax.all_to_all(x, 'row', 0, 0, tiled=True)  85.2 us
    all_to_all x4, blocking collectives, exchange_feat(): return lax.all_to_all(x, 'feat', 0, 0, axis_index_groups=chips, tiled=True)  55.8 us
    pallas_call x4, Pallas kernels, gradient_half(): pl.pallas_call(kernel, in_specs=whole(2 + n_before, 1), out_specs=whole(l...  8.55 us
    pallas_call x3, Pallas kernels, predict_half(): pl.pallas_call(kernel, in_specs=whole(2, 1), out_specs=whole(1, 0)[0], ou...  5.45 us
    pallas_call x1, Pallas kernels, predict_first(): pl.pallas_call(kernel, in_specs=whole(0, 1) + [hbm, hbm], out_specs=whole...  4.14 us
  transfers between devices with their start and end apart: 4, of which 2 were waited for; matrix products, arithmetic and copies ran while one was open for 0% of the time, Pallas kernels for 5%

profile of v4, /device:TPU:0, one launch (start us, length us, event | category | flops | bytes accessed | tf_op | source)
XLA Modules:
  0.0 165.7 jit_solution(10744985111641017394)
XLA Ops:
  0.0 0.7 dynamic-slice_subtract_fusion
  0.7 0.1 copy.11
  0.8 0.1 sub.10.ids_ref
  1.0 0.0 copy-start
  1.0 4.1 %shard_map.55 = (f32[32,64,128]{2,1,0:T(8,128)S(1)}, bf16[64,64,128]{2,1,0:T(8,128)(2,1)S(1)}) custom-call(s32[192]{0:T(256)S(1)} %sub.10.ids_ref, bf16[64,3,128,128]{3,2,1,0:T(8,128)(2,1)} %bitcast.12, f32[64,8192]{1,0:T(8,128)} %bitcast.23), custom_call_target="tpu_custom_call" | custom-call | tf_op jit(solution)/shard_map/pallas_call | solution.py:96
  5.1 0.1 collective-permute-start
  5.2 0.1 copy-done
  5.3 1.8 %shard_map.56 = f32[32,64,128]{2,1,0:T(8,128)S(1)} custom-call(s32[192]{0:T(256)S(1)} %sub.10.ids_ref, bf16[64,3,128,128]{3,2,1,0:T(8,128)(2,1)S(1)} %bitcast.13, bf16[64,64,128]{2,1,0:T(8,128)(2,1)S(1)} %get-tuple-element.16.coef_ref), custom_call_target="tpu_custom_call" | custom-call | tf_op jit(solution)/shard_map/pallas_call | solution.py:129
  7.1 0.0 copy-start.2
  7.2 0.0 copy-start.3
  7.2 0.7 collective-permute-done
  7.9 0.2 add_convert_fusion.1
  8.1 16.5 %all_to_all.40 = bf16[32,64,128]{2,1,0:T(8,128)(2,1)S(1)} all-to-all(bf16[32,64,128]{2,1,0:T(8,128)(2,1)S(1)} %add_convert_fusion.1), channel_id=1, replica_groups={{0,2,4,6,8,10,12,14},{1,3,5,7,9,11,13,15},{16,18,20,22,24,26,28,30},{17..., dimensions={0} | all-to-all | bytes 1048576 | tf_op jit(solution)/shard_map/all_to_all | solution.py:324
  24.6 0.0 copy-done.2
  24.6 0.0 copy-done.3
  24.6 0.7 shard_map.57
  25.3 12.8 %all_to_all.41.scaled_ref = bf16[8,272,128]{2,1,0:T(8,128)(2,1)S(1)} all-to-all(bf16[8,272,128]{2,1,0:T(8,128)(2,1)S(1)} %shard_map.57), channel_id=1, replica_groups={{0,2,4,6,8,10,12,14},{1,3,5,7,9,11,13,15},{16,18,20,22,24,26,28,30},{17..., dimensions={0} | all-to-all | bytes 1114112 | tf_op jit(solution)/shard_map/all_to_all | solution.py:324
  38.1 0.0 collective-permute-start.1
  38.1 2.1 %shard_map.58 = (f32[64,64,128]{2,1,0:T(8,128)S(1)}, f32[64,8,128]{2,1,0:T(8,128)S(1)}) custom-call(s32[192]{0:T(256)S(1)} %sub.10.ids_ref, bf16[64,3,128,128]{3,2,1,0:T(8,128)(2,1)S(1)} %bitcast.14, bf16[8,272,128]{2,1,0:T(8,128)(2,1)S(1)} %all_to_all.41.scaled_ref), custom_call_target="tpu_custom_call" | custom-call | tf_op jit(solution)/shard_map/pallas_call | solution.py:235
  40.3 0.0 collective-permute-done.1.scaled_ref
  40.3 2.3 %shard_map.59 = (f32[64,64,128]{2,1,0:T(8,128)S(1)}, f32[64,8,128]{2,1,0:T(8,128)S(1)}, bf16[8,528,128]{2,1,0:T(8,128)(2,1)S(1)}) custom-call(s32[192]{0:T(256)S(1)} %sub.10.ids_ref, bf16[64,3,128,128]{3,2,1,0:T(8,128)(2,1)S(1)} %bitcast.15, ...), custom_call_target="tpu_custom_call", output_to_operand_aliasing={{0}: (3, {}), {1}: (4, {})} | custom-call | tf_op jit(solution)/shard_map/pallas_call | solution.py:235
  42.6 0.0 copy-start.1
  42.6 25.0 %all_to_all.42.parts_ref = bf16[8,528,128]{2,1,0:T(8,128)(2,1)S(1)} all-to-all(bf16[8,528,128]{2,1,0:T(8,128)(2,1)S(1)} %get-tuple-element.20), channel_id=1, replica_groups=mesh['row'=8,'feat'=16] {'row'}, dimensions={0} | all-to-all | bytes 2162688 | tf_op jit(solution)/shard_map/all_to_all | solution.py:327
  67.6 0.0 copy-done.1
  67.6 0.2 shard_map.60
  67.8 19.5 %all_to_all.43 = bf16[8,8,64,128]{3,2,1,0:T(8,128)(2,1)S(1)} all-to-all(bf16[8,8,64,128]{3,2,1,0:T(8,128)(2,1)S(1)} %get-tuple-element.21.refs_0_), channel_id=1, replica_groups=mesh['row'=8,'feat'=16] {'row'}, dimensions={0} | all-to-all | bytes 2097152 | tf_op jit(solution)/shard_map/all_to_all | solution.py:327
  87.3 1.8 %shard_map.62 = f32[32,64,128]{2,1,0:T(8,128)S(1)} custom-call(s32[192]{0:T(256)S(1)} %sub.10.ids_ref, bf16[64,3,128,128]{3,2,1,0:T(8,128)(2,1)S(1)} %bitcast.16, bf16[64,64,128]{2,1,0:T(8,128)(2,1)S(1)} %bitcast.20), custom_call_target="tpu_custom_call" | custom-call | tf_op jit(solution)/shard_map/pallas_call | solution.py:129
  89.2 0.1 collective-permute-start.2
  89.3 1.8 %shard_map.61 = f32[32,64,128]{2,1,0:T(8,128)S(1)} custom-call(s32[192]{0:T(256)S(1)} %sub.10.ids_ref, bf16[64,3,128,128]{3,2,1,0:T(8,128)(2,1)S(1)} %bitcast.17, bf16[64,64,128]{2,1,0:T(8,128)(2,1)S(1)} %bitcast.21), custom_call_target="tpu_custom_call" | custom-call | tf_op jit(solution)/shard_map/pallas_call | solution.py:129
  91.1 0.8 collective-permute-done.2
  91.9 0.2 add_convert_fusion
  92.1 12.9 %all_to_all.44 = bf16[32,64,128]{2,1,0:T(8,128)(2,1)S(1)} all-to-all(bf16[32,64,128]{2,1,0:T(8,128)(2,1)S(1)} %add_convert_fusion), channel_id=1, replica_groups={{0,2,4,6,8,10,12,14},{1,3,5,7,9,11,13,15},{16,18,20,22,24,26,28,30},{17..., dimensions={0} | all-to-all | bytes 1048576 | tf_op jit(solution)/shard_map/all_to_all | solution.py:324
  105.0 0.7 shard_map.63
  105.7 13.5 %all_to_all.45.scaled_ref = bf16[8,272,128]{2,1,0:T(8,128)(2,1)S(1)} all-to-all(bf16[8,272,128]{2,1,0:T(8,128)(2,1)S(1)} %shard_map.63), channel_id=1, replica_groups={{0,2,4,6,8,10,12,14},{1,3,5,7,9,11,13,15},{16,18,20,22,24,26,28,30},{17..., dimensions={0} | all-to-all | bytes 1114112 | tf_op jit(solution)/shard_map/all_to_all | solution.py:324
  119.3 0.0 collective-permute-start.3
  119.3 2.0 %shard_map.64 = (f32[64,64,128]{2,1,0:T(8,128)S(1)}, f32[64,8,128]{2,1,0:T(8,128)S(1)}) custom-call(s32[192]{0:T(256)S(1)} %sub.10.ids_ref, bf16[64,3,128,128]{3,2,1,0:T(8,128)(2,1)S(1)} %bitcast.18, bf16[8,272,128]{2,1,0:T(8,128)(2,1)S(1)} %all_to_all.45.scaled_ref, f32[64,64,128]{2,1,0:T(8,128)S(1)} %get-tuple-element.22.refs_0_), custom_call_target="tpu_custom_call", output_to_operand_aliasing={{0}: (3, {})} | custom-call | tf_op jit(solution)/shard_map/pallas_call | solution.py:235
  121.2 0.0 collective-permute-done.3.scaled_ref
  121.2 2.2 %shard_map.65 = (f32[64,64,128]{2,1,0:T(8,128)S(1)}, f32[64,8,128]{2,1,0:T(8,128)S(1)}, bf16[8,528,128]{2,1,0:T(8,128)(2,1)S(1)}) custom-call(s32[192]{0:T(256)S(1)} %sub.10.ids_ref, bf16[64,3,128,128]{3,2,1,0:T(8,128)(2,1)S(1)} %bitcast.19, ...), custom_call_target="tpu_custom_call", output_to_operand_aliasing={{0}: (3, {}), {1}: (4, {})} | custom-call | tf_op jit(solution)/shard_map/pallas_call | solution.py:235
  123.4 21.1 %all_to_all.46.parts_ref = bf16[8,528,128]{2,1,0:T(8,128)(2,1)S(1)} all-to-all(bf16[8,528,128]{2,1,0:T(8,128)(2,1)S(1)} %get-tuple-element.25), channel_id=1, replica_groups=mesh['row'=8,'feat'=16] {'row'}, dimensions={0} | all-to-all | bytes 2162688 | tf_op jit(solution)/shard_map/all_to_all | solution.py:327
  144.6 0.2 shard_map.66
  144.8 19.6 %all_to_all.47 = bf16[8,8,64,128]{3,2,1,0:T(8,128)(2,1)S(1)} all-to-all(bf16[8,8,64,128]{3,2,1,0:T(8,128)(2,1)S(1)} %shard_map.66), channel_id=1, replica_groups=mesh['row'=8,'feat'=16] {'row'}, dimensions={0} | all-to-all | bytes 2097152 | tf_op jit(solution)/shard_map/all_to_all | solution.py:327
  164.3 1.4 shard_map.67
Async XLA Ops:
  1.0 4.4 %copy-start = (bf16[1,8,8,3,128,128]{5,4,3,2,1,0:T(8,128)(2,1)S(1)}, bf16[1,8,8,3,128,128]{5,4,3,2,1,0:T(8,128)(2,1)}, u32[]{:S(2)}) copy-start(bf16[1,8,8,3,128,128]{5,4,3,2,1,0:T(8,128)(2,1)} %param.5) | copy-start | bytes 18874372
  5.1 2.7 %collective-permute-start = (f32[32,64,128]{2,1,0:T(8,128)S(1)}, f32[32,64,128]{2,1,0:T(8,128)S(1)}, u32[]{:S(2)}, u32[]{:S(2)}) collective-permute-start(f32[32,64,128]{2,1,0:T(8,128)S(1)} %get-tuple-element.17), channel_id=1, source_target_pairs={{0,1},{1,0},{2,3},{3,2},{4,5},{5,4},{6,7},{7,6},{8,9},{9,8},{10,11... | collective-permute-start | bytes 3145736 | tf_op jit(solution)/shard_map/ppermute | solution.py:321
  7.1 17.4 %copy-start.2 = (bf16[1,8,8,128,64]{3,4,2,1,0:T(8,128)(2,1)S(1)}, bf16[1,8,8,128,64]{3,4,2,1,0:T(8,128)(2,1)}, u32[]{:S(2)}) copy-start(bf16[1,8,8,128,64]{3,4,2,1,0:T(8,128)(2,1)} %param.7) | copy-start | bytes 3145732
  7.2 17.4 %copy-start.3 = (s32[8,8]{1,0:T(8,128)S(1)}, s32[8,8]{1,0:T(8,128)}, u32[]{:S(2)}) copy-start(s32[8,8]{1,0:T(8,128)} %live_ref.3) | copy-start | bytes 772
  38.1 2.1 %collective-permute-start.1 = (bf16[8,272,128]{2,1,0:T(8,128)(2,1)S(1)}, bf16[8,272,128]{2,1,0:T(8,128)(2,1)S(1)}, u32[]{:S(2)}, u32[]{:S(2)}) collective-permute-start(bf16[8,272,128]{2,1,0:T(8,128)(2,1)S(1)} %all_to_all.41.scaled_ref), channel_id=1, source_target_pairs={{0,1},{1,0},{2,3},{3,2},{4,5},{5,4},{6,7},{7,6},{8,9},{9,8},{10,11... | collective-permute-start | bytes 1671176 | tf_op jit(solution)/shard_map/ppermute | solution.py:321
  42.6 25.0 %copy-start.1 = (f32[8192,64]{0,1:T(8,128)S(1)}, f32[8192,64]{0,1:T(8,128)}, u32[]{:S(2)}) copy-start(f32[8192,64]{0,1:T(8,128)} %param.9) | copy-start | bytes 6291460
  89.2 2.7 %collective-permute-start.2 = (f32[32,64,128]{2,1,0:T(8,128)S(1)}, f32[32,64,128]{2,1,0:T(8,128)S(1)}, u32[]{:S(2)}, u32[]{:S(2)}) collective-permute-start(f32[32,64,128]{2,1,0:T(8,128)S(1)} %shard_map.62), channel_id=1, source_target_pairs={{0,1},{1,0},{2,3},{3,2},{4,5},{5,4},{6,7},{7,6},{8,9},{9,8},{10,11... | collective-permute-start | bytes 3145736 | tf_op jit(solution)/shard_map/ppermute | solution.py:321
  119.3 2.0 %collective-permute-start.3 = (bf16[8,272,128]{2,1,0:T(8,128)(2,1)S(1)}, bf16[8,272,128]{2,1,0:T(8,128)(2,1)S(1)}, u32[]{:S(2)}, u32[]{:S(2)}) collective-permute-start(bf16[8,272,128]{2,1,0:T(8,128)(2,1)S(1)} %all_to_all.45.scaled_ref), channel_id=1, source_target_pairs={{0,1},{1,0},{2,3},{3,2},{4,5},{5,4},{6,7},{7,6},{8,9},{9,8},{10,11... | collective-permute-start | bytes 1671176 | tf_op jit(solution)/shard_map/ppermute | solution.py:321

commit v5 on v4

--- a/solution.py
+++ b/solution.py
@@ -27,9 +27,9 @@
     return [smem] * scalars + [vmem] * count
 
 
-def place():
+def place(n_feat):
     feat = lax.axis_index("feat")
-    return lax.axis_index("row"), feat % 2, feat // 2
+    return lax.axis_index("row"), lax.rem(feat, 2), lax.div(feat, 2)
 
 
 def side(other):
@@ -54,7 +54,7 @@
     out_ref[put + 1] = both[columns:, rows:]
 
 
-def predict_first(ids, tiles, start_t):
+def predict_first(ids, tiles, start_t, owned):
     row_blocks, kt, rows, width = tiles.shape
     columns, features = start_t.shape
     blocks = features // width
@@ -64,9 +64,11 @@
     coef_pieces = 4
     share = features // coef_pieces
 
-    def kernel(ids_ref, tiles_hbm, start_hbm, out_ref, coef_ref, held, tile_sem, start_ref, start_sem):
+    def kernel(ids_vmem, tiles_hbm, start_hbm, out_ref, coef_ref, own_ref, *scratch):
+        held, tile_sem, start_ref, start_sem, ids_ref, ids_sem = scratch
         base = side(True) * half
         starts, copies = [], []
+        ids_copy = pltpu.make_async_copy(ids_vmem, ids_ref, ids_sem)
         for p in range(coef_pieces):
             at = pl.ds(p * share, share)
             starts.append(
@@ -80,12 +82,16 @@
                     tile_sem.at[p],
                 )
             )
-        for copy in starts + copies:
+        for copy in starts + [ids_copy] + copies:
             copy.start()
         for p in range(coef_pieces):
             starts[p].wait()
             for b in range(p * blocks // coef_pieces, (p + 1) * blocks // coef_pieces):
                 coef_ref[b] = start_ref[:, b * width : (b + 1) * width].astype(BF16)
+        for b in range(owned):
+            at = pl.multiple_of((lax.axis_index("row") * owned + b) * width, width)
+            own_ref[b] = start_ref[:, pl.ds(at, width)]
+        ids_copy.wait()
         for p in range(pieces):
             copies[p].wait()
             for r in range(0, step, 2):
@@ -95,17 +101,20 @@
     hbm = pl.BlockSpec(memory_space=pltpu.HBM)
     return pl.pallas_call(
         kernel,
-        in_specs=whole(0, 1) + [hbm, hbm],
-        out_specs=whole(2, 0),
+        in_specs=whole(1, 0) + [hbm, hbm],
+        out_specs=whole(3, 0),
         out_shape=[
             jax.ShapeDtypeStruct((half, columns, rows), F32),
             jax.ShapeDtypeStruct((blocks, columns, width), BF16),
+            jax.ShapeDtypeStruct((owned, columns, width), F32),
         ],
         scratch_shapes=[
             pltpu.VMEM((half, kt, rows, width), BF16),
             pltpu.SemaphoreType.DMA((pieces,)),
             pltpu.VMEM(start_t.shape, F32),
             pltpu.SemaphoreType.DMA((coef_pieces,)),
+            pltpu.SMEM(ids.shape, jnp.int32),
+            pltpu.SemaphoreType.DMA(()),
         ],
         compiler_params=params(FIRST_LIMIT),
     )(ids, tiles, start_t)
@@ -143,9 +152,12 @@
     slots = resp_t.shape[0] // live.shape[1]
 
     def kernel(live_ref, parts_ref, resp_ref, out_ref):
-        row, core, chip = place()
+        row, core, chip = place(n_feat)
         first = (core * (n_feat // 2) + chip) * count
-        flag = live_ref[row, first // slots].astype(F32)
+        at = lax.broadcasted_iota(jnp.int32, live.shape, 0) == row
+        at &= lax.broadcasted_iota(jnp.int32, live.shape, 1) == first // slots
+        flag = jnp.sum(jnp.where(at, live_ref[...].astype(F32), 0.0), axis=0, keepdims=True)
+        flag = jnp.sum(flag, axis=1, keepdims=True)
         lines = []
         for r in range(count):
             predicted = parts_ref[0, r].astype(F32)
@@ -165,7 +177,7 @@
 
     return pl.pallas_call(
         kernel,
-        in_specs=whole(2, 1),
+        in_specs=whole(3, 0),
         out_specs=whole(1, 0)[0],
         out_shape=jax.ShapeDtypeStruct((copies, height, rows), BF16),
         compiler_params=params(),
@@ -260,11 +272,7 @@
         curvature = total(owned * columns, height)
         for b in range(owned):
             gradient = total(b * columns, (b + 1) * columns)
-            if first:
-                at = pl.multiple_of((lax.axis_index("row") * owned + b) * width, width)
-                coef = exact_ref[:, pl.ds(at, width)]
-            else:
-                coef = exact_ref[b]
+            coef = exact_ref[b]
             new = coef + STEP_SIZE * (gradient - RIDGE * coef) / (curvature[b : b + 1] + RIDGE)
             if first:
                 refs[0][b] = new
@@ -287,7 +295,7 @@
 
 def finish(known, change):
     blocks, columns, width = known.shape
-    pieces = 4
+    pieces = 8
     step = blocks // pieces
 
     def kernel(known_ref, change_ref, out_hbm, held, sem):
@@ -341,12 +349,11 @@
         share = row_blocks // n_feat
         owned = local_blocks // n_row
 
-        known = None
-        exact, sent, carried = start_t, None, ()
+        sent, carried = None, ()
         for iteration in range(ITERS):
             ends = iteration == ITERS - 1
             if iteration == 0:
-                ahead, known = predict_first(ids, tiles, start_t)
+                ahead, known, exact = predict_first(ids, tiles, start_t, owned)
             else:
                 ahead = predict_half(ids, tiles, known, True)
             arrived = swap_core(ahead)

time: 166 us -> 164 us (0.988)
  Pallas kernels: 21.4 us -> 19.6 us
    pallas_call x3, Pallas kernels: 5.59 us -> 3.82 us  [the longest x1 3.54 us: predict_first(): pl.pallas_call(kernel, in_specs=whole(1, 0) + [hbm, hbm], out_specs=whole...]
where the time goes in v5:
time: 164 us; the launch traced here: 163 us
  blocking collectives  140 us (85%)
  Pallas kernels  19.6 us (12%)
    all_to_all x4, blocking collectives, exchange_row(): return lax.all_to_all(x, 'row', 0, 0, tiled=True)  85 us
    all_to_all x4, blocking collectives, exchange_feat(): return lax.all_to_all(x, 'feat', 0, 0, axis_index_groups=chips, tiled=True)  55.1 us
    pallas_call x4, Pallas kernels, gradient_half(): pl.pallas_call(kernel, in_specs=whole(2 + n_before, 1), out_specs=whole(l...  8.55 us
    pallas_call x3, Pallas kernels, predict_half(): pl.pallas_call(kernel, in_specs=whole(2, 1), out_specs=whole(1, 0)[0], ou...  5.45 us
    pallas_call x1, Pallas kernels, predict_first(): pl.pallas_call(kernel, in_specs=whole(1, 0) + [hbm, hbm], out_specs=whole...  3.54 us
  transfers between devices with their start and end apart: 4, of which 2 were waited for; matrix products, arithmetic and copies ran while one was open for 0% of the time, Pallas kernels for 5%

profile of v5, /device:TPU:0, one launch (start us, length us, event | category | flops | bytes accessed | tf_op | source)
XLA Modules:
  0.0 163.1 jit_solution(15568390702043467036)
XLA Ops:
  0.0 0.7 dynamic-slice_subtract_fusion
  0.7 0.1 copy.11
  0.8 0.1 sub.10.ids_vmem.ids_ref
  1.0 0.0 copy-start
  1.0 3.5 %shard_map.55 = (f32[32,64,128]{2,1,0:T(8,128)S(1)}, bf16[64,64,128]{2,1,0:T(8,128)(2,1)S(1)}, f32[8,64,128]{2,1,0:T(8,128)S(1)}) custom-call(s32[192]{0:T(256)S(1)} %sub.10.ids_vmem.ids_ref, bf16[64,3,128,128]{3,2,1,0:T(8,128)(2,1)} %bitcast.12, f32[64,8192]{1,0:T(8,128)} %bitcast.28), custom_call_target="tpu_custom_call" | custom-call | tf_op jit(solution)/shard_map/pallas_call | solution.py:102
  4.5 0.1 collective-permute-start
  4.6 0.7 copy-done
  5.3 1.8 %shard_map.56 = f32[32,64,128]{2,1,0:T(8,128)S(1)} custom-call(s32[192]{0:T(256)S(1)} %sub.10.ids_vmem.ids_ref, bf16[64,3,128,128]{3,2,1,0:T(8,128)(2,1)S(1)} %bitcast.13, bf16[64,64,128]{2,1,0:T(8,128)(2,1)S(1)} %get-tuple-element.17.coef_ref), custom_call_target="tpu_custom_call" | custom-call | tf_op jit(solution)/shard_map/pallas_call | solution.py:138
  7.1 0.0 copy-start.1
  7.2 0.0 copy-start.2
  7.2 0.1 collective-permute-done
  7.3 0.2 add_convert_fusion.1
  7.5 16.6 %all_to_all.40 = bf16[32,64,128]{2,1,0:T(8,128)(2,1)S(1)} all-to-all(bf16[32,64,128]{2,1,0:T(8,128)(2,1)S(1)} %add_convert_fusion.1), channel_id=1, replica_groups={{0,2,4,6,8,10,12,14},{1,3,5,7,9,11,13,15},{16,18,20,22,24,26,28,30},{17..., dimensions={0} | all-to-all | bytes 1048576 | tf_op jit(solution)/shard_map/all_to_all | solution.py:332
  24.0 0.0 copy-done.1
  24.0 0.0 copy-done.2
  24.0 0.1 shard_map.57
  24.2 12.1 %all_to_all.41.scaled_ref = bf16[8,272,128]{2,1,0:T(8,128)(2,1)S(1)} all-to-all(bf16[8,272,128]{2,1,0:T(8,128)(2,1)S(1)} %shard_map.57), channel_id=1, replica_groups={{0,2,4,6,8,10,12,14},{1,3,5,7,9,11,13,15},{16,18,20,22,24,26,28,30},{17..., dimensions={0} | all-to-all | bytes 1114112 | tf_op jit(solution)/shard_map/all_to_all | solution.py:332
  36.3 0.0 collective-permute-start.1
  36.3 2.1 %shard_map.58 = (f32[64,64,128]{2,1,0:T(8,128)S(1)}, f32[64,8,128]{2,1,0:T(8,128)S(1)}) custom-call(s32[192]{0:T(256)S(1)} %sub.10.ids_vmem.ids_ref, bf16[64,3,128,128]{3,2,1,0:T(8,128)(2,1)S(1)} %bitcast.14, bf16[8,272,128]{2,1,0:T(8,128)(2,1)S(1)} %all_to_all.41.scaled_ref), custom_call_target="tpu_custom_call" | custom-call | tf_op jit(solution)/shard_map/pallas_call | solution.py:247
  38.4 0.0 collective-permute-done.1.scaled_ref
  38.5 2.3 %shard_map.59 = (f32[64,64,128]{2,1,0:T(8,128)S(1)}, f32[64,8,128]{2,1,0:T(8,128)S(1)}, bf16[8,528,128]{2,1,0:T(8,128)(2,1)S(1)}) custom-call(s32[192]{0:T(256)S(1)} %sub.10.ids_vmem.ids_ref, bf16[64,3,128,128]{3,2,1,0:T(8,128)(2,1)S(1)} %bitcast.15, ...), custom_call_target="tpu_custom_call", output_to_operand_aliasing={{0}: (3, {}), {1}: (4, {})} | custom-call | tf_op jit(solution)/shard_map/pallas_call | solution.py:247
  40.7 24.8 %all_to_all.42.parts_ref = bf16[8,528,128]{2,1,0:T(8,128)(2,1)S(1)} all-to-all(bf16[8,528,128]{2,1,0:T(8,128)(2,1)S(1)} %get-tuple-element.21), channel_id=1, replica_groups=mesh['row'=8,'feat'=16] {'row'}, dimensions={0} | all-to-all | bytes 2162688 | tf_op jit(solution)/shard_map/all_to_all | solution.py:335
  65.6 0.2 shard_map.60
  65.8 19.5 %all_to_all.43 = bf16[8,8,64,128]{3,2,1,0:T(8,128)(2,1)S(1)} all-to-all(bf16[8,8,64,128]{3,2,1,0:T(8,128)(2,1)S(1)} %get-tuple-element.23.refs_0_), channel_id=1, replica_groups=mesh['row'=8,'feat'=16] {'row'}, dimensions={0} | all-to-all | bytes 2097152 | tf_op jit(solution)/shard_map/all_to_all | solution.py:335
  85.3 1.8 %shard_map.62 = f32[32,64,128]{2,1,0:T(8,128)S(1)} custom-call(s32[192]{0:T(256)S(1)} %sub.10.ids_vmem.ids_ref, bf16[64,3,128,128]{3,2,1,0:T(8,128)(2,1)S(1)} %bitcast.16, bf16[64,64,128]{2,1,0:T(8,128)(2,1)S(1)} %bitcast.20), custom_call_target="tpu_custom_call" | custom-call | tf_op jit(solution)/shard_map/pallas_call | solution.py:138
  87.1 0.1 collective-permute-start.2
  87.2 1.8 %shard_map.61 = f32[32,64,128]{2,1,0:T(8,128)S(1)} custom-call(s32[192]{0:T(256)S(1)} %sub.10.ids_vmem.ids_ref, bf16[64,3,128,128]{3,2,1,0:T(8,128)(2,1)S(1)} %bitcast.17, bf16[64,64,128]{2,1,0:T(8,128)(2,1)S(1)} %bitcast.21), custom_call_target="tpu_custom_call" | custom-call | tf_op jit(solution)/shard_map/pallas_call | solution.py:138
  89.1 0.8 collective-permute-done.2
  89.9 0.2 add_convert_fusion
  90.1 12.9 %all_to_all.44 = bf16[32,64,128]{2,1,0:T(8,128)(2,1)S(1)} all-to-all(bf16[32,64,128]{2,1,0:T(8,128)(2,1)S(1)} %add_convert_fusion), channel_id=1, replica_groups={{0,2,4,6,8,10,12,14},{1,3,5,7,9,11,13,15},{16,18,20,22,24,26,28,30},{17..., dimensions={0} | all-to-all | bytes 1048576 | tf_op jit(solution)/shard_map/all_to_all | solution.py:332
  103.0 0.1 shard_map.63
  103.1 13.5 %all_to_all.45.scaled_ref = bf16[8,272,128]{2,1,0:T(8,128)(2,1)S(1)} all-to-all(bf16[8,272,128]{2,1,0:T(8,128)(2,1)S(1)} %shard_map.63), channel_id=1, replica_groups={{0,2,4,6,8,10,12,14},{1,3,5,7,9,11,13,15},{16,18,20,22,24,26,28,30},{17..., dimensions={0} | all-to-all | bytes 1114112 | tf_op jit(solution)/shard_map/all_to_all | solution.py:332
  116.6 0.0 collective-permute-start.3
  116.7 2.0 %shard_map.64 = (f32[64,64,128]{2,1,0:T(8,128)S(1)}, f32[64,8,128]{2,1,0:T(8,128)S(1)}) custom-call(s32[192]{0:T(256)S(1)} %sub.10.ids_vmem.ids_ref, bf16[64,3,128,128]{3,2,1,0:T(8,128)(2,1)S(1)} %bitcast.18, bf16[8,272,128]{2,1,0:T(8,128)(2,1)S(1)} %all_to_all.45.scaled_ref, ...), custom_call_target="tpu_custom_call", output_to_operand_aliasing={{0}: (3, {})} | custom-call | tf_op jit(solution)/shard_map/pallas_call | solution.py:247
  118.6 0.0 collective-permute-done.3.scaled_ref
  118.6 2.2 %shard_map.65 = (f32[64,64,128]{2,1,0:T(8,128)S(1)}, f32[64,8,128]{2,1,0:T(8,128)S(1)}, bf16[8,528,128]{2,1,0:T(8,128)(2,1)S(1)}) custom-call(s32[192]{0:T(256)S(1)} %sub.10.ids_vmem.ids_ref, bf16[64,3,128,128]{3,2,1,0:T(8,128)(2,1)S(1)} %bitcast.19, ...), custom_call_target="tpu_custom_call", output_to_operand_aliasing={{0}: (3, {}), {1}: (4, {})} | custom-call | tf_op jit(solution)/shard_map/pallas_call | solution.py:247
  120.8 21.1 %all_to_all.46.parts_ref = bf16[8,528,128]{2,1,0:T(8,128)(2,1)S(1)} all-to-all(bf16[8,528,128]{2,1,0:T(8,128)(2,1)S(1)} %get-tuple-element.27), channel_id=1, replica_groups=mesh['row'=8,'feat'=16] {'row'}, dimensions={0} | all-to-all | bytes 2162688 | tf_op jit(solution)/shard_map/all_to_all | solution.py:335
  141.9 0.2 shard_map.66
  142.1 19.6 %all_to_all.47 = bf16[8,8,64,128]{3,2,1,0:T(8,128)(2,1)S(1)} all-to-all(bf16[8,8,64,128]{3,2,1,0:T(8,128)(2,1)S(1)} %shard_map.66), channel_id=1, replica_groups=mesh['row'=8,'feat'=16] {'row'}, dimensions={0} | all-to-all | bytes 2097152 | tf_op jit(solution)/shard_map/all_to_all | solution.py:335
  161.7 1.4 shard_map.67
Async XLA Ops:
  1.0 4.4 %copy-start = (bf16[1,8,8,3,128,128]{5,4,3,2,1,0:T(8,128)(2,1)S(1)}, bf16[1,8,8,3,128,128]{5,4,3,2,1,0:T(8,128)(2,1)}, u32[]{:S(2)}) copy-start(bf16[1,8,8,3,128,128]{5,4,3,2,1,0:T(8,128)(2,1)} %param.5) | copy-start | bytes 18874372
  4.5 2.7 %collective-permute-start = (f32[32,64,128]{2,1,0:T(8,128)S(1)}, f32[32,64,128]{2,1,0:T(8,128)S(1)}, u32[]{:S(2)}, u32[]{:S(2)}) collective-permute-start(f32[32,64,128]{2,1,0:T(8,128)S(1)} %get-tuple-element.18), channel_id=1, source_target_pairs={{0,1},{1,0},{2,3},{3,2},{4,5},{5,4},{6,7},{7,6},{8,9},{9,8},{10,11... | collective-permute-start | bytes 3145736 | tf_op jit(solution)/shard_map/ppermute | solution.py:329
  7.1 16.9 %copy-start.1 = (bf16[1,8,8,128,64]{3,4,2,1,0:T(8,128)(2,1)S(1)}, bf16[1,8,8,128,64]{3,4,2,1,0:T(8,128)(2,1)}, u32[]{:S(2)}) copy-start(bf16[1,8,8,128,64]{3,4,2,1,0:T(8,128)(2,1)} %param.7) | copy-start | bytes 3145732
  7.2 16.9 %copy-start.2 = (s32[8,8]{1,0:T(8,128)S(1)}, s32[8,8]{1,0:T(8,128)}, u32[]{:S(2)}) copy-start(s32[8,8]{1,0:T(8,128)} %live_ref.3) | copy-start | bytes 772
  36.3 2.1 %collective-permute-start.1 = (bf16[8,272,128]{2,1,0:T(8,128)(2,1)S(1)}, bf16[8,272,128]{2,1,0:T(8,128)(2,1)S(1)}, u32[]{:S(2)}, u32[]{:S(2)}) collective-permute-start(bf16[8,272,128]{2,1,0:T(8,128)(2,1)S(1)} %all_to_all.41.scaled_ref), channel_id=1, source_target_pairs={{0,1},{1,0},{2,3},{3,2},{4,5},{5,4},{6,7},{7,6},{8,9},{9,8},{10,11... | collective-permute-start | bytes 1671176 | tf_op jit(solution)/shard_map/ppermute | solution.py:329
  87.1 2.7 %collective-permute-start.2 = (f32[32,64,128]{2,1,0:T(8,128)S(1)}, f32[32,64,128]{2,1,0:T(8,128)S(1)}, u32[]{:S(2)}, u32[]{:S(2)}) collective-permute-start(f32[32,64,128]{2,1,0:T(8,128)S(1)} %shard_map.62), channel_id=1, source_target_pairs={{0,1},{1,0},{2,3},{3,2},{4,5},{5,4},{6,7},{7,6},{8,9},{9,8},{10,11... | collective-permute-start | bytes 3145736 | tf_op jit(solution)/shard_map/ppermute | solution.py:329
  116.6 2.0 %collective-permute-start.3 = (bf16[8,272,128]{2,1,0:T(8,128)(2,1)S(1)}, bf16[8,272,128]{2,1,0:T(8,128)(2,1)S(1)}, u32[]{:S(2)}, u32[]{:S(2)}) collective-permute-start(bf16[8,272,128]{2,1,0:T(8,128)(2,1)S(1)} %all_to_all.45.scaled_ref), channel_id=1, source_target_pairs={{0,1},{1,0},{2,3},{3,2},{4,5},{5,4},{6,7},{7,6},{8,9},{9,8},{10,11... | collective-permute-start | bytes 1671176 | tf_op jit(solution)/shard_map/ppermute | solution.py:329

commit v6 on v5

--- a/solution.py
+++ b/solution.py
@@ -37,11 +37,15 @@
     return 1 - core if other else core
 
 
-def predict_pair(ids_ref, tiles_ref, coef_ref, out_ref, put, at, row_block, kt):
+def blocks_of(ids_ref, other, kt):
+    line = ids_ref[pl.ds(side(other), 1), :]
+    return lambda row_block, k: line[0, row_block * kt + k]
+
+
+def predict_pair(block_of, tiles_ref, coef_ref, out_ref, put, at, kt):
     picked, placed = [], []
     for r in range(2):
-        first = (row_block + r) * kt
-        picked.append(jnp.concatenate([coef_ref[ids_ref[first + k]] for k in range(kt)], axis=1))
+        picked.append(jnp.concatenate([coef_ref[block_of(put + r, k)] for k in range(kt)], axis=1))
         placed.append(jnp.concatenate([tiles_ref[at + r, k] for k in range(kt)], axis=1))
     both = lax.dot_general(
         jnp.concatenate(picked, axis=0),
@@ -64,11 +68,11 @@
     coef_pieces = 4
     share = features // coef_pieces
 
-    def kernel(ids_vmem, tiles_hbm, start_hbm, out_ref, coef_ref, own_ref, *scratch):
-        held, tile_sem, start_ref, start_sem, ids_ref, ids_sem = scratch
+    def kernel(ids_ref, tiles_hbm, start_hbm, out_ref, coef_ref, own_ref, *scratch):
+        held, tile_sem, start_ref, start_sem = scratch
         base = side(True) * half
+        block_of = blocks_of(ids_ref, True, kt)
         starts, copies = [], []
-        ids_copy = pltpu.make_async_copy(ids_vmem, ids_ref, ids_sem)
         for p in range(coef_pieces):
             at = pl.ds(p * share, share)
             starts.append(
@@ -82,7 +86,7 @@
                     tile_sem.at[p],
                 )
             )
-        for copy in starts + [ids_copy] + copies:
+        for copy in starts + copies:
             copy.start()
         for p in range(coef_pieces):
             starts[p].wait()
@@ -91,12 +95,11 @@
         for b in range(owned):
             at = pl.multiple_of((lax.axis_index("row") * owned + b) * width, width)
             own_ref[b] = start_ref[:, pl.ds(at, width)]
-        ids_copy.wait()
         for p in range(pieces):
             copies[p].wait()
             for r in range(0, step, 2):
                 at = p * step + r
-                predict_pair(ids_ref, held, coef_ref, out_ref, at, at, base + at, kt)
+                predict_pair(block_of, held, coef_ref, out_ref, at, at, kt)
 
     hbm = pl.BlockSpec(memory_space=pltpu.HBM)
     return pl.pallas_call(
@@ -113,8 +116,6 @@
             pltpu.SemaphoreType.DMA((pieces,)),
             pltpu.VMEM(start_t.shape, F32),
             pltpu.SemaphoreType.DMA((coef_pieces,)),
-            pltpu.SMEM(ids.shape, jnp.int32),
-            pltpu.SemaphoreType.DMA(()),
         ],
         compiler_params=params(FIRST_LIMIT),
     )(ids, tiles, start_t)
@@ -124,20 +125,16 @@
     row_blocks, kt, rows, width = tiles.shape
     columns = coef.shape[1]
     half = row_blocks // 2
-    step = 16
 
     def kernel(ids_ref, tiles_ref, coef_ref, out_ref):
         base = side(other) * half
-
-        @pl.loop(0, half // step)
-        def _(i):
-            for r in range(0, step, 2):
-                at = i * step + r
-                predict_pair(ids_ref, tiles_ref, coef_ref, out_ref, at, base + at, base + at, kt)
-
-    return pl.pallas_call(
-        kernel,
-        in_specs=whole(2, 1),
+        block_of = blocks_of(ids_ref, other, kt)
+        for r in range(0, half, 2):
+            predict_pair(block_of, tiles_ref, coef_ref, out_ref, r, base + r, kt)
+
+    return pl.pallas_call(
+        kernel,
+        in_specs=whole(3, 0),
         out_specs=whole(1, 0)[0],
         out_shape=jax.ShapeDtypeStruct((half, columns, rows), F32),
         compiler_params=params(),
@@ -192,11 +189,11 @@
     columns = (height - PAD) // count
     owned = local_blocks // groups
     n_before = len(before)
-    turn = 2
 
     def kernel(ids_ref, tiles_ref, scaled_ref, *refs):
         grad, curv, *out = refs[n_before:]
         base = side(other) * half
+        block_of = blocks_of(ids_ref, other, kt)
         for ref in (grad, curv)[n_before:]:
             ref[...] = jnp.zeros_like(ref)
 
@@ -212,16 +209,14 @@
                     preferred_element_type=F32,
                 )
                 for k in range(kt):
-                    block = ids_ref[row_block * kt + k]
+                    block = block_of(p * count + r, k)
                     grad[block] += sums[:, k * width : (k + 1) * width]
                     wide = placed[k].astype(F32)
                     square = wide * wide * weights
                     curv[block] += jnp.sum(square.reshape(rows // 8, 8, width), axis=0)
 
-        @pl.loop(0, sources // turn)
-        def _(i):
-            for t in range(turn):
-                add(i * turn + t)
+        for p in range(sources):
+            add(p)
 
         if other:
 
@@ -246,7 +241,7 @@
         out_shape.append(jax.ShapeDtypeStruct((groups, owned * columns + PAD, width), BF16))
     return pl.pallas_call(
         kernel,
-        in_specs=whole(2 + n_before, 1),
+        in_specs=whole(3 + n_before, 0),
         out_specs=whole(len(out_shape), 0),
         out_shape=out_shape,
         input_output_aliases={3 + i: i for i in range(n_before)},
@@ -345,7 +340,8 @@
         resp_t = responses.reshape(row_blocks, rows, columns).swapaxes(1, 2)
         start_t = start_coef.T
         ids = lax.dynamic_index_in_dim(block_ids, row, 0, keepdims=False).reshape(-1)
-        ids = (ids - feat * local_blocks).astype(jnp.int32)
+        ids = (ids - feat * local_blocks).astype(jnp.int32).reshape(2, -1)
+        ids = jnp.pad(ids, ((0, 0), (0, -ids.shape[1] % LANES)))
         share = row_blocks // n_feat
         owned = local_blocks // n_row
 

time: 164 us -> 162 us (0.988)
  Pallas kernels: 19.6 us -> 16.4 us
  waiting for transfers between devices: 0.93 us -> 3.66 us
    pallas_call x7, Pallas kernels: 14 us -> 10 us  [the longest x4 6.4 us: gradient_half(): pl.pallas_call(kernel, in_specs=whole(3 + n_before, 0), out_specs=whole(l...]
    ppermute x4, waiting for transfers between devices: 0.93 us -> 3.66 us  [swap_core(): return lax.ppermute(x, 'feat', other_core)]
  transfers between devices with their start and end apart: 4 -> 4, of which waited for: 2 -> 4; matrix products, arithmetic and copies ran while one was open for 0% -> 0% of each run, Pallas kernels for 5% -> 3%
where the time goes in v6:
time: 162 us
  blocking collectives  140 us (86%)
  Pallas kernels  16.4 us (10%)
  waiting for transfers between devices  3.66 us (2%)
    all_to_all x4, blocking collectives, exchange_row(): return lax.all_to_all(x, 'row', 0, 0, tiled=True)  84.3 us
    all_to_all x4, blocking collectives, exchange_feat(): return lax.all_to_all(x, 'feat', 0, 0, axis_index_groups=chips, tiled=True)  55.8 us
    pallas_call x4, Pallas kernels, gradient_half(): pl.pallas_call(kernel, in_specs=whole(3 + n_before, 0), out_specs=whole(l...  6.4 us
    pallas_call x1, Pallas kernels, predict_first(): pl.pallas_call(kernel, in_specs=whole(1, 0) + [hbm, hbm], out_specs=whole...  4.23 us
    ppermute x4, waiting for transfers between devices, swap_core(): return lax.ppermute(x, 'feat', other_core)  3.66 us
    pallas_call x3, Pallas kernels, predict_half(): pl.pallas_call(kernel, in_specs=whole(3, 0), out_specs=whole(1, 0)[0], ou...  3.64 us
  transfers between devices with their start and end apart: 4, of which 4 were waited for; matrix products, arithmetic and copies ran while one was open for 0% of the time, Pallas kernels for 3%

profile of v6, /device:TPU:0, one launch (start us, length us, event | category | flops | bytes accessed | tf_op | source)
XLA Modules:
  0.0 161.7 jit_solution(11990537358865587213)
XLA Ops:
  0.0 0.7 dynamic-slice_subtract_fusion
  0.7 0.1 copy.12
  0.8 0.1 sub.12
  1.0 0.0 copy-start
  1.0 4.2 %shard_map.55 = (f32[32,64,128]{2,1,0:T(8,128)S(1)}, bf16[64,64,128]{2,1,0:T(8,128)(2,1)S(1)}, f32[8,64,128]{2,1,0:T(8,128)S(1)}) custom-call(s32[2,128]{1,0:T(2,128)S(1)} %pad.4.ids_ref, bf16[64,3,128,128]{3,2,1,0:T(8,128)(2,1)} %bitcast.12, f32[64,8192]{1,0:T(8,128)} %bitcast.28), custom_call_target="tpu_custom_call" | custom-call | tf_op jit(solution)/shard_map/pallas_call | solution.py:105
  5.2 0.1 collective-permute-start
  5.3 0.0 copy-done
  5.3 1.2 shard_map.56
  6.5 0.0 copy-start.1
  6.5 0.0 copy-start.2
  6.6 1.4 collective-permute-done
  7.9 0.2 add_convert_fusion.1
  8.1 16.5 %all_to_all.40 = bf16[32,64,128]{2,1,0:T(8,128)(2,1)S(1)} all-to-all(bf16[32,64,128]{2,1,0:T(8,128)(2,1)S(1)} %add_convert_fusion.1), channel_id=1, replica_groups={{0,2,4,6,8,10,12,14},{1,3,5,7,9,11,13,15},{16,18,20,22,24,26,28,30},{17..., dimensions={0} | all-to-all | bytes 1048576 | tf_op jit(solution)/shard_map/all_to_all | solution.py:327
  24.7 0.0 copy-done.1
  24.7 0.0 copy-done.2
  24.7 0.1 shard_map.57
  24.8 12.8 %all_to_all.41.scaled_ref = bf16[8,272,128]{2,1,0:T(8,128)(2,1)S(1)} all-to-all(bf16[8,272,128]{2,1,0:T(8,128)(2,1)S(1)} %shard_map.57), channel_id=1, replica_groups={{0,2,4,6,8,10,12,14},{1,3,5,7,9,11,13,15},{16,18,20,22,24,26,28,30},{17..., dimensions={0} | all-to-all | bytes 1114112 | tf_op jit(solution)/shard_map/all_to_all | solution.py:327
  37.6 0.0 collective-permute-start.1
  37.6 1.6 shard_map.58
  39.2 0.4 collective-permute-done.1.scaled_ref
  39.6 1.7 %shard_map.59 = (f32[64,64,128]{2,1,0:T(8,128)S(1)}, f32[64,8,128]{2,1,0:T(8,128)S(1)}, bf16[8,528,128]{2,1,0:T(8,128)(2,1)S(1)}) custom-call(s32[2,128]{1,0:T(2,128)S(1)} %pad.4.ids_ref, bf16[64,3,128,128]{3,2,1,0:T(8,128)(2,1)S(1)} %bitcast.15, ...), custom_call_target="tpu_custom_call", output_to_operand_aliasing={{0}: (3, {}), {1}: (4, {})} | custom-call | tf_op jit(solution)/shard_map/pallas_call | solution.py:242
  41.3 24.5 %all_to_all.42.parts_ref = bf16[8,528,128]{2,1,0:T(8,128)(2,1)S(1)} all-to-all(bf16[8,528,128]{2,1,0:T(8,128)(2,1)S(1)} %get-tuple-element.21), channel_id=1, replica_groups=mesh['row'=8,'feat'=16] {'row'}, dimensions={0} | all-to-all | bytes 2162688 | tf_op jit(solution)/shard_map/all_to_all | solution.py:330
  65.8 0.2 shard_map.60
  66.0 19.5 %all_to_all.43 = bf16[8,8,64,128]{3,2,1,0:T(8,128)(2,1)S(1)} all-to-all(bf16[8,8,64,128]{3,2,1,0:T(8,128)(2,1)S(1)} %get-tuple-element.23.refs_0_), channel_id=1, replica_groups=mesh['row'=8,'feat'=16] {'row'}, dimensions={0} | all-to-all | bytes 2097152 | tf_op jit(solution)/shard_map/all_to_all | solution.py:330
  85.5 1.2 shard_map.62
  86.7 0.1 collective-permute-start.2
  86.8 1.2 shard_map.61
  88.1 1.4 collective-permute-done.2
  89.5 0.2 add_convert_fusion
  89.7 12.9 %all_to_all.44 = bf16[32,64,128]{2,1,0:T(8,128)(2,1)S(1)} all-to-all(bf16[32,64,128]{2,1,0:T(8,128)(2,1)S(1)} %add_convert_fusion), channel_id=1, replica_groups={{0,2,4,6,8,10,12,14},{1,3,5,7,9,11,13,15},{16,18,20,22,24,26,28,30},{17..., dimensions={0} | all-to-all | bytes 1048576 | tf_op jit(solution)/shard_map/all_to_all | solution.py:327
  102.6 0.1 shard_map.63
  102.7 13.5 %all_to_all.45.scaled_ref = bf16[8,272,128]{2,1,0:T(8,128)(2,1)S(1)} all-to-all(bf16[8,272,128]{2,1,0:T(8,128)(2,1)S(1)} %shard_map.63), channel_id=1, replica_groups={{0,2,4,6,8,10,12,14},{1,3,5,7,9,11,13,15},{16,18,20,22,24,26,28,30},{17..., dimensions={0} | all-to-all | bytes 1114112 | tf_op jit(solution)/shard_map/all_to_all | solution.py:327
  116.2 0.0 collective-permute-start.3
  116.2 1.5 shard_map.64
  117.7 0.5 collective-permute-done.3.scaled_ref
  118.2 1.6 %shard_map.65 = (f32[64,64,128]{2,1,0:T(8,128)S(1)}, f32[64,8,128]{2,1,0:T(8,128)S(1)}, bf16[8,528,128]{2,1,0:T(8,128)(2,1)S(1)}) custom-call(s32[2,128]{1,0:T(2,128)S(1)} %pad.4.ids_ref, bf16[64,3,128,128]{3,2,1,0:T(8,128)(2,1)S(1)} %bitcast.19, ...), custom_call_target="tpu_custom_call", output_to_operand_aliasing={{0}: (3, {}), {1}: (4, {})} | custom-call | tf_op jit(solution)/shard_map/pallas_call | solution.py:242
  119.8 20.7 %all_to_all.46.parts_ref = bf16[8,528,128]{2,1,0:T(8,128)(2,1)S(1)} all-to-all(bf16[8,528,128]{2,1,0:T(8,128)(2,1)S(1)} %get-tuple-element.27), channel_id=1, replica_groups=mesh['row'=8,'feat'=16] {'row'}, dimensions={0} | all-to-all | bytes 2162688 | tf_op jit(solution)/shard_map/all_to_all | solution.py:330
  140.6 0.2 shard_map.66
  140.8 19.5 %all_to_all.47 = bf16[8,8,64,128]{3,2,1,0:T(8,128)(2,1)S(1)} all-to-all(bf16[8,8,64,128]{3,2,1,0:T(8,128)(2,1)S(1)} %shard_map.66), channel_id=1, replica_groups=mesh['row'=8,'feat'=16] {'row'}, dimensions={0} | all-to-all | bytes 2097152 | tf_op jit(solution)/shard_map/all_to_all | solution.py:330
  160.3 1.4 shard_map.67
  (1 shorter events, 0.0 us)
Async XLA Ops:
  1.0 4.4 %copy-start = (bf16[1,8,8,3,128,128]{5,4,3,2,1,0:T(8,128)(2,1)S(1)}, bf16[1,8,8,3,128,128]{5,4,3,2,1,0:T(8,128)(2,1)}, u32[]{:S(2)}) copy-start(bf16[1,8,8,3,128,128]{5,4,3,2,1,0:T(8,128)(2,1)} %param.5) | copy-start | bytes 18874372
  5.2 2.7 %collective-permute-start = (f32[32,64,128]{2,1,0:T(8,128)S(1)}, f32[32,64,128]{2,1,0:T(8,128)S(1)}, u32[]{:S(2)}, u32[]{:S(2)}) collective-permute-start(f32[32,64,128]{2,1,0:T(8,128)S(1)} %get-tuple-element.18), channel_id=1, source_target_pairs={{0,1},{1,0},{2,3},{3,2},{4,5},{5,4},{6,7},{7,6},{8,9},{9,8},{10,11... | collective-permute-start | bytes 3145736 | tf_op jit(solution)/shard_map/ppermute | solution.py:324
  6.5 18.1 %copy-start.1 = (bf16[1,8,8,128,64]{3,4,2,1,0:T(8,128)(2,1)S(1)}, bf16[1,8,8,128,64]{3,4,2,1,0:T(8,128)(2,1)}, u32[]{:S(2)}) copy-start(bf16[1,8,8,128,64]{3,4,2,1,0:T(8,128)(2,1)} %param.7) | copy-start | bytes 3145732
  6.5 18.1 %copy-start.2 = (s32[8,8]{1,0:T(8,128)S(1)}, s32[8,8]{1,0:T(8,128)}, u32[]{:S(2)}) copy-start(s32[8,8]{1,0:T(8,128)} %live_ref.3) | copy-start | bytes 772
  37.6 2.0 %collective-permute-start.1 = (bf16[8,272,128]{2,1,0:T(8,128)(2,1)S(1)}, bf16[8,272,128]{2,1,0:T(8,128)(2,1)S(1)}, u32[]{:S(2)}, u32[]{:S(2)}) collective-permute-start(bf16[8,272,128]{2,1,0:T(8,128)(2,1)S(1)} %all_to_all.41.scaled_ref), channel_id=1, source_target_pairs={{0,1},{1,0},{2,3},{3,2},{4,5},{5,4},{6,7},{7,6},{8,9},{9,8},{10,11... | collective-permute-start | bytes 1671176 | tf_op jit(solution)/shard_map/ppermute | solution.py:324
  86.7 2.7 %collective-permute-start.2 = (f32[32,64,128]{2,1,0:T(8,128)S(1)}, f32[32,64,128]{2,1,0:T(8,128)S(1)}, u32[]{:S(2)}, u32[]{:S(2)}) collective-permute-start(f32[32,64,128]{2,1,0:T(8,128)S(1)} %shard_map.62), channel_id=1, source_target_pairs={{0,1},{1,0},{2,3},{3,2},{4,5},{5,4},{6,7},{7,6},{8,9},{9,8},{10,11... | collective-permute-start | bytes 3145736 | tf_op jit(solution)/shard_map/ppermute | solution.py:324
  116.2 2.0 %collective-permute-start.3 = (bf16[8,272,128]{2,1,0:T(8,128)(2,1)S(1)}, bf16[8,272,128]{2,1,0:T(8,128)(2,1)S(1)}, u32[]{:S(2)}, u32[]{:S(2)}) collective-permute-start(bf16[8,272,128]{2,1,0:T(8,128)(2,1)S(1)} %all_to_all.45.scaled_ref), channel_id=1, source_target_pairs={{0,1},{1,0},{2,3},{3,2},{4,5},{5,4},{6,7},{7,6},{8,9},{9,8},{10,11... | collective-permute-start | bytes 1671176 | tf_op jit(solution)/shard_map/ppermute | solution.py:324

commit v7 on v6

--- a/solution.py
+++ b/solution.py
@@ -11,7 +11,7 @@
 F32 = jnp.float32
 BF16 = jnp.bfloat16
 VMEM_LIMIT = 16 * 1024 * 1024
-FIRST_LIMIT = 50 * 1024 * 1024
+FIRST_LIMIT = 51 * 1024 * 1024
 
 LANES = 128
 PAD = 16
@@ -54,11 +54,11 @@
         preferred_element_type=F32,
     )
     columns, rows = picked[0].shape[0], placed[0].shape[0]
-    out_ref[put] = both[:columns, :rows]
-    out_ref[put + 1] = both[columns:, rows:]
-
-
-def predict_first(ids, tiles, start_t, owned):
+    out_ref[put] = both[:columns, :rows].astype(out_ref.dtype)
+    out_ref[put + 1] = both[columns:, rows:].astype(out_ref.dtype)
+
+
+def predict_first(ids, tiles, start_t, owned, dtype):
     row_blocks, kt, rows, width = tiles.shape
     columns, features = start_t.shape
     blocks = features // width
@@ -68,10 +68,12 @@
     coef_pieces = 4
     share = features // coef_pieces
 
-    def kernel(ids_ref, tiles_hbm, start_hbm, out_ref, coef_ref, own_ref, *scratch):
-        held, tile_sem, start_ref, start_sem = scratch
-        base = side(True) * half
-        block_of = blocks_of(ids_ref, True, kt)
+    def kernel(ids_vmem, tiles_hbm, start_hbm, out_ref, coef_ref, own_ref, *scratch):
+        held, tile_sem, start_ref, start_sem, ids_ref, ids_sem = scratch
+        other = side(True)
+        base = other * half
+        block_of = lambda row_block, k: ids_ref[other, row_block * kt + k]
+        ids_copy = pltpu.make_async_copy(ids_vmem, ids_ref, ids_sem)
         starts, copies = [], []
         for p in range(coef_pieces):
             at = pl.ds(p * share, share)
@@ -86,7 +88,7 @@
                     tile_sem.at[p],
                 )
             )
-        for copy in starts + copies:
+        for copy in starts + [ids_copy] + copies:
             copy.start()
         for p in range(coef_pieces):
             starts[p].wait()
@@ -95,6 +97,7 @@
         for b in range(owned):
             at = pl.multiple_of((lax.axis_index("row") * owned + b) * width, width)
             own_ref[b] = start_ref[:, pl.ds(at, width)]
+        ids_copy.wait()
         for p in range(pieces):
             copies[p].wait()
             for r in range(0, step, 2):
@@ -107,7 +110,7 @@
         in_specs=whole(1, 0) + [hbm, hbm],
         out_specs=whole(3, 0),
         out_shape=[
-            jax.ShapeDtypeStruct((half, columns, rows), F32),
+            jax.ShapeDtypeStruct((half, columns, rows), dtype),
             jax.ShapeDtypeStruct((blocks, columns, width), BF16),
             jax.ShapeDtypeStruct((owned, columns, width), F32),
         ],
@@ -116,6 +119,8 @@
             pltpu.SemaphoreType.DMA((pieces,)),
             pltpu.VMEM(start_t.shape, F32),
             pltpu.SemaphoreType.DMA((coef_pieces,)),
+            pltpu.SMEM(ids.shape, jnp.int32),
+            pltpu.SemaphoreType.DMA(()),
         ],
         compiler_params=params(FIRST_LIMIT),
     )(ids, tiles, start_t)
@@ -349,12 +354,12 @@
         for iteration in range(ITERS):
             ends = iteration == ITERS - 1
             if iteration == 0:
-                ahead, known, exact = predict_first(ids, tiles, start_t, owned)
+                ahead, known, exact = predict_first(ids, tiles, start_t, owned, BF16)
             else:
                 ahead = predict_half(ids, tiles, known, True)
             arrived = swap_core(ahead)
             kept = predict_half(ids, tiles, known, False)
-            pair = (kept + arrived).astype(BF16)
+            pair = (kept + arrived.astype(F32)).astype(BF16)
             parts = exchange_feat(pair).reshape(n_yz, share, columns, rows)
             scaled = exchange_feat(weigh(n_feat, live_groups, parts, resp_t, n_yz))
             scaled_there = swap_core(scaled)

time: 162 us -> 160 us (0.988)
  transfers between devices with their start and end apart: 4 -> 4, of which waited for: 4 -> 3; matrix products, arithmetic and copies ran while one was open for 0% -> 0% of each run, Pallas kernels for 3% -> 3%
where the time goes in v7:
time: 160 us
  blocking collectives  139 us (87%)
  Pallas kernels  15.7 us (10%)
  waiting for transfers between devices  2.27 us (1%)
    all_to_all x4, blocking collectives, exchange_row(): return lax.all_to_all(x, 'row', 0, 0, tiled=True)  84.3 us
    all_to_all x4, blocking collectives, exchange_feat(): return lax.all_to_all(x, 'feat', 0, 0, axis_index_groups=chips, tiled=True)  55 us
    pallas_call x4, Pallas kernels, gradient_half(): pl.pallas_call(kernel, in_specs=whole(3 + n_before, 0), out_specs=whole(l...  6.42 us
    pallas_call x3, Pallas kernels, predict_half(): pl.pallas_call(kernel, in_specs=whole(3, 0), out_specs=whole(1, 0)[0], ou...  3.64 us
    pallas_call x1, Pallas kernels, predict_first(): pl.pallas_call(kernel, in_specs=whole(1, 0) + [hbm, hbm], out_specs=whole...  3.54 us
  transfers between devices with their start and end apart: 4, of which 3 were waited for; matrix products, arithmetic and copies ran while one was open for 0% of the time, Pallas kernels for 3%

profile of v7, /device:TPU:0, one launch (start us, length us, event | category | flops | bytes accessed | tf_op | source)
XLA Modules:
  0.0 159.5 jit_solution(7443061708636416713)
XLA Ops:
  0.0 0.7 dynamic-slice_subtract_fusion
  0.7 0.1 copy.12
  0.8 0.1 sub.12
  1.0 0.0 copy-start
  1.0 3.5 %shard_map.55 = (bf16[32,64,128]{2,1,0:T(8,128)(2,1)S(1)}, bf16[64,64,128]{2,1,0:T(8,128)(2,1)S(1)}, f32[8,64,128]{2,1,0:T(8,128)S(1)}) custom-call(s32[2,128]{1,0:T(2,128)S(1)} %pad.4.ids_vmem.ids_ref, bf16[64,3,128,128]{3,2,1,0:T(8,128)(2,1)} %bitcast.12, f32[64,8192]{1,0:T(8,128)} %bitcast.28), custom_call_target="tpu_custom_call" | custom-call | tf_op jit(solution)/shard_map/pallas_call | solution.py:108
  4.5 0.1 collective-permute-start
  4.6 0.7 copy-done
  5.3 1.2 shard_map.56
  6.5 0.0 copy-start.1
  6.5 0.0 copy-start.2
  6.6 0.0 collective-permute-done
  6.6 0.1 add_convert_fusion.1
  6.7 16.5 %all_to_all.40 = bf16[32,64,128]{2,1,0:T(8,128)(2,1)S(1)} all-to-all(bf16[32,64,128]{2,1,0:T(8,128)(2,1)S(1)} %add_convert_fusion.1), channel_id=1, replica_groups={{0,2,4,6,8,10,12,14},{1,3,5,7,9,11,13,15},{16,18,20,22,24,26,28,30},{17..., dimensions={0} | all-to-all | bytes 1048576 | tf_op jit(solution)/shard_map/all_to_all | solution.py:332
  23.2 0.0 copy-done.1
  23.2 0.0 copy-done.2
  23.2 0.1 shard_map.57
  23.4 12.1 %all_to_all.41.scaled_ref = bf16[8,272,128]{2,1,0:T(8,128)(2,1)S(1)} all-to-all(bf16[8,272,128]{2,1,0:T(8,128)(2,1)S(1)} %shard_map.57), channel_id=1, replica_groups={{0,2,4,6,8,10,12,14},{1,3,5,7,9,11,13,15},{16,18,20,22,24,26,28,30},{17..., dimensions={0} | all-to-all | bytes 1114112 | tf_op jit(solution)/shard_map/all_to_all | solution.py:332
  35.5 0.0 collective-permute-start.1
  35.5 1.6 shard_map.58
  37.1 0.4 collective-permute-done.1.scaled_ref
  37.4 1.7 %shard_map.59 = (f32[64,64,128]{2,1,0:T(8,128)S(1)}, f32[64,8,128]{2,1,0:T(8,128)S(1)}, bf16[8,528,128]{2,1,0:T(8,128)(2,1)S(1)}) custom-call(s32[2,128]{1,0:T(2,128)S(1)} %pad.4.ids_vmem.ids_ref, bf16[64,3,128,128]{3,2,1,0:T(8,128)(2,1)S(1)} %bitcast.15, ...), custom_call_target="tpu_custom_call", output_to_operand_aliasing={{0}: (3, {}), {1}: (4, {})} | custom-call | tf_op jit(solution)/shard_map/pallas_call | solution.py:247
  39.2 24.5 %all_to_all.42.parts_ref = bf16[8,528,128]{2,1,0:T(8,128)(2,1)S(1)} all-to-all(bf16[8,528,128]{2,1,0:T(8,128)(2,1)S(1)} %get-tuple-element.21), channel_id=1, replica_groups=mesh['row'=8,'feat'=16] {'row'}, dimensions={0} | all-to-all | bytes 2162688 | tf_op jit(solution)/shard_map/all_to_all | solution.py:335
  63.7 0.2 shard_map.60
  63.9 19.5 %all_to_all.43 = bf16[8,8,64,128]{3,2,1,0:T(8,128)(2,1)S(1)} all-to-all(bf16[8,8,64,128]{3,2,1,0:T(8,128)(2,1)S(1)} %get-tuple-element.23.refs_0_), channel_id=1, replica_groups=mesh['row'=8,'feat'=16] {'row'}, dimensions={0} | all-to-all | bytes 2097152 | tf_op jit(solution)/shard_map/all_to_all | solution.py:335
  83.4 1.2 shard_map.62
  84.6 0.1 collective-permute-start.2
  84.7 1.2 shard_map.61
  85.9 1.4 collective-permute-done.2
  87.3 0.2 add_convert_fusion
  87.5 12.9 %all_to_all.44 = bf16[32,64,128]{2,1,0:T(8,128)(2,1)S(1)} all-to-all(bf16[32,64,128]{2,1,0:T(8,128)(2,1)S(1)} %add_convert_fusion), channel_id=1, replica_groups={{0,2,4,6,8,10,12,14},{1,3,5,7,9,11,13,15},{16,18,20,22,24,26,28,30},{17..., dimensions={0} | all-to-all | bytes 1048576 | tf_op jit(solution)/shard_map/all_to_all | solution.py:332
  100.4 0.1 shard_map.63
  100.6 13.5 %all_to_all.45.scaled_ref = bf16[8,272,128]{2,1,0:T(8,128)(2,1)S(1)} all-to-all(bf16[8,272,128]{2,1,0:T(8,128)(2,1)S(1)} %shard_map.63), channel_id=1, replica_groups={{0,2,4,6,8,10,12,14},{1,3,5,7,9,11,13,15},{16,18,20,22,24,26,28,30},{17..., dimensions={0} | all-to-all | bytes 1114112 | tf_op jit(solution)/shard_map/all_to_all | solution.py:332
  114.1 0.0 collective-permute-start.3
  114.1 1.5 shard_map.64
  115.6 0.5 collective-permute-done.3.scaled_ref
  116.0 1.6 %shard_map.65 = (f32[64,64,128]{2,1,0:T(8,128)S(1)}, f32[64,8,128]{2,1,0:T(8,128)S(1)}, bf16[8,528,128]{2,1,0:T(8,128)(2,1)S(1)}) custom-call(s32[2,128]{1,0:T(2,128)S(1)} %pad.4.ids_vmem.ids_ref, bf16[64,3,128,128]{3,2,1,0:T(8,128)(2,1)S(1)} %bitcast.19, ...), custom_call_target="tpu_custom_call", output_to_operand_aliasing={{0}: (3, {}), {1}: (4, {})} | custom-call | tf_op jit(solution)/shard_map/pallas_call | solution.py:247
  117.7 20.7 %all_to_all.46.parts_ref = bf16[8,528,128]{2,1,0:T(8,128)(2,1)S(1)} all-to-all(bf16[8,528,128]{2,1,0:T(8,128)(2,1)S(1)} %get-tuple-element.27), channel_id=1, replica_groups=mesh['row'=8,'feat'=16] {'row'}, dimensions={0} | all-to-all | bytes 2162688 | tf_op jit(solution)/shard_map/all_to_all | solution.py:335
  138.4 0.2 shard_map.66
  138.6 19.5 %all_to_all.47 = bf16[8,8,64,128]{3,2,1,0:T(8,128)(2,1)S(1)} all-to-all(bf16[8,8,64,128]{3,2,1,0:T(8,128)(2,1)S(1)} %shard_map.66), channel_id=1, replica_groups=mesh['row'=8,'feat'=16] {'row'}, dimensions={0} | all-to-all | bytes 2097152 | tf_op jit(solution)/shard_map/all_to_all | solution.py:335
  158.1 1.4 shard_map.67
  (1 shorter events, 0.0 us)
Async XLA Ops:
  1.0 4.4 %copy-start = (bf16[1,8,8,3,128,128]{5,4,3,2,1,0:T(8,128)(2,1)S(1)}, bf16[1,8,8,3,128,128]{5,4,3,2,1,0:T(8,128)(2,1)}, u32[]{:S(2)}) copy-start(bf16[1,8,8,3,128,128]{5,4,3,2,1,0:T(8,128)(2,1)} %param.5) | copy-start | bytes 18874372
  4.5 2.0 %collective-permute-start = (bf16[32,64,128]{2,1,0:T(8,128)(2,1)S(1)}, bf16[32,64,128]{2,1,0:T(8,128)(2,1)S(1)}, u32[]{:S(2)}, u32[]{:S(2)}) collective-permute-start(bf16[32,64,128]{2,1,0:T(8,128)(2,1)S(1)} %get-tuple-element.18), channel_id=1, source_target_pairs={{0,1},{1,0},{2,3},{3,2},{4,5},{5,4},{6,7},{7,6},{8,9},{9,8},{10,11... | collective-permute-start | bytes 1572872 | tf_op jit(solution)/shard_map/ppermute | solution.py:329
  6.5 16.7 %copy-start.1 = (bf16[1,8,8,128,64]{3,4,2,1,0:T(8,128)(2,1)S(1)}, bf16[1,8,8,128,64]{3,4,2,1,0:T(8,128)(2,1)}, u32[]{:S(2)}) copy-start(bf16[1,8,8,128,64]{3,4,2,1,0:T(8,128)(2,1)} %param.7) | copy-start | bytes 3145732
  6.5 16.7 %copy-start.2 = (s32[8,8]{1,0:T(8,128)S(1)}, s32[8,8]{1,0:T(8,128)}, u32[]{:S(2)}) copy-start(s32[8,8]{1,0:T(8,128)} %live_ref.3) | copy-start | bytes 772
  35.5 2.0 %collective-permute-start.1 = (bf16[8,272,128]{2,1,0:T(8,128)(2,1)S(1)}, bf16[8,272,128]{2,1,0:T(8,128)(2,1)S(1)}, u32[]{:S(2)}, u32[]{:S(2)}) collective-permute-start(bf16[8,272,128]{2,1,0:T(8,128)(2,1)S(1)} %all_to_all.41.scaled_ref), channel_id=1, source_target_pairs={{0,1},{1,0},{2,3},{3,2},{4,5},{5,4},{6,7},{7,6},{8,9},{9,8},{10,11... | collective-permute-start | bytes 1671176 | tf_op jit(solution)/shard_map/ppermute | solution.py:329
  84.6 2.7 %collective-permute-start.2 = (f32[32,64,128]{2,1,0:T(8,128)S(1)}, f32[32,64,128]{2,1,0:T(8,128)S(1)}, u32[]{:S(2)}, u32[]{:S(2)}) collective-permute-start(f32[32,64,128]{2,1,0:T(8,128)S(1)} %shard_map.62), channel_id=1, source_target_pairs={{0,1},{1,0},{2,3},{3,2},{4,5},{5,4},{6,7},{7,6},{8,9},{9,8},{10,11... | collective-permute-start | bytes 3145736 | tf_op jit(solution)/shard_map/ppermute | solution.py:329
  114.1 2.0 %collective-permute-start.3 = (bf16[8,272,128]{2,1,0:T(8,128)(2,1)S(1)}, bf16[8,272,128]{2,1,0:T(8,128)(2,1)S(1)}, u32[]{:S(2)}, u32[]{:S(2)}) collective-permute-start(bf16[8,272,128]{2,1,0:T(8,128)(2,1)S(1)} %all_to_all.45.scaled_ref), channel_id=1, source_target_pairs={{0,1},{1,0},{2,3},{3,2},{4,5},{5,4},{6,7},{7,6},{8,9},{9,8},{10,11... | collective-permute-start | bytes 1671176 | tf_op jit(solution)/shard_map/ppermute | solution.py:329

commit v8 on v7

--- a/solution.py
+++ b/solution.py
@@ -295,16 +295,17 @@
 
 def finish(known, change):
     blocks, columns, width = known.shape
-    pieces = 8
-    step = blocks // pieces
+    step = 16
+    pieces = columns // step
 
     def kernel(known_ref, change_ref, out_hbm, held, sem):
         copies = []
         for p in range(pieces):
-            for b in range(p * step, (p + 1) * step):
-                held[:, b * width : (b + 1) * width] = known_ref[b].astype(F32) + change_ref[b].astype(F32)
-            at = pl.ds(p * step * width, step * width)
-            copies.append(pltpu.make_async_copy(held.at[:, at], out_hbm.at[:, at], sem.at[p]))
+            at = pl.ds(p * step, step)
+            for b in range(blocks):
+                value = known_ref[b, at, :].astype(F32) + change_ref[b, at, :].astype(F32)
+                held[at, b * width : (b + 1) * width] = value
+            copies.append(pltpu.make_async_copy(held.at[at], out_hbm.at[at], sem.at[p]))
             copies[p].start()
         for copy in copies:
             copy.wait()

time: 160 us -> 160 us (level)
  no operation moved by 1% of the time
where the time goes in v8:
time: 160 us
  blocking collectives  139 us (87%)
  Pallas kernels  15.7 us (10%)
  waiting for transfers between devices  2.27 us (1%)
    all_to_all x4, blocking collectives, exchange_row(): return lax.all_to_all(x, 'row', 0, 0, tiled=True)  84.3 us
    all_to_all x4, blocking collectives, exchange_feat(): return lax.all_to_all(x, 'feat', 0, 0, axis_index_groups=chips, tiled=True)  55 us
    pallas_call x4, Pallas kernels, gradient_half(): pl.pallas_call(kernel, in_specs=whole(3 + n_before, 0), out_specs=whole(l...  6.41 us
    pallas_call x3, Pallas kernels, predict_half(): pl.pallas_call(kernel, in_specs=whole(3, 0), out_specs=whole(1, 0)[0], ou...  3.64 us
    pallas_call x1, Pallas kernels, predict_first(): pl.pallas_call(kernel, in_specs=whole(1, 0) + [hbm, hbm], out_specs=whole...  3.54 us
  transfers between devices with their start and end apart: 4, of which 3 were waited for; matrix products, arithmetic and copies ran while one was open for 0% of the time, Pallas kernels for 3%

profile of v8, /device:TPU:0, one launch (start us, length us, event | category | flops | bytes accessed | tf_op | source)
XLA Modules:
  0.0 159.6 jit_solution(15224415275076520836)
XLA Ops:
  0.0 0.7 dynamic-slice_subtract_fusion
  0.7 0.1 copy.12
  0.8 0.1 sub.12
  1.0 0.0 copy-start
  1.0 3.5 %shard_map.55 = (bf16[32,64,128]{2,1,0:T(8,128)(2,1)S(1)}, bf16[64,64,128]{2,1,0:T(8,128)(2,1)S(1)}, f32[8,64,128]{2,1,0:T(8,128)S(1)}) custom-call(s32[2,128]{1,0:T(2,128)S(1)} %pad.4.ids_vmem.ids_ref, bf16[64,3,128,128]{3,2,1,0:T(8,128)(2,1)} %bitcast.12, f32[64,8192]{1,0:T(8,128)} %bitcast.28), custom_call_target="tpu_custom_call" | custom-call | tf_op jit(solution)/shard_map/pallas_call | solution.py:108
  4.5 0.1 collective-permute-start
  4.6 0.7 copy-done
  5.3 1.2 shard_map.56
  6.5 0.0 copy-start.1
  6.5 0.0 copy-start.2
  6.6 0.0 collective-permute-done
  6.6 0.1 add_convert_fusion.1
  6.7 16.5 %all_to_all.40 = bf16[32,64,128]{2,1,0:T(8,128)(2,1)S(1)} all-to-all(bf16[32,64,128]{2,1,0:T(8,128)(2,1)S(1)} %add_convert_fusion.1), channel_id=1, replica_groups={{0,2,4,6,8,10,12,14},{1,3,5,7,9,11,13,15},{16,18,20,22,24,26,28,30},{17..., dimensions={0} | all-to-all | bytes 1048576 | tf_op jit(solution)/shard_map/all_to_all | solution.py:333
  23.2 0.0 copy-done.1
  23.2 0.0 copy-done.2
  23.2 0.1 shard_map.57
  23.4 12.1 %all_to_all.41.scaled_ref = bf16[8,272,128]{2,1,0:T(8,128)(2,1)S(1)} all-to-all(bf16[8,272,128]{2,1,0:T(8,128)(2,1)S(1)} %shard_map.57), channel_id=1, replica_groups={{0,2,4,6,8,10,12,14},{1,3,5,7,9,11,13,15},{16,18,20,22,24,26,28,30},{17..., dimensions={0} | all-to-all | bytes 1114112 | tf_op jit(solution)/shard_map/all_to_all | solution.py:333
  35.5 0.0 collective-permute-start.1
  35.5 1.6 shard_map.58
  37.1 0.4 collective-permute-done.1.scaled_ref
  37.4 1.7 %shard_map.59 = (f32[64,64,128]{2,1,0:T(8,128)S(1)}, f32[64,8,128]{2,1,0:T(8,128)S(1)}, bf16[8,528,128]{2,1,0:T(8,128)(2,1)S(1)}) custom-call(s32[2,128]{1,0:T(2,128)S(1)} %pad.4.ids_vmem.ids_ref, bf16[64,3,128,128]{3,2,1,0:T(8,128)(2,1)S(1)} %bitcast.15, ...), custom_call_target="tpu_custom_call", output_to_operand_aliasing={{0}: (3, {}), {1}: (4, {})} | custom-call | tf_op jit(solution)/shard_map/pallas_call | solution.py:247
  39.2 24.5 %all_to_all.42.parts_ref = bf16[8,528,128]{2,1,0:T(8,128)(2,1)S(1)} all-to-all(bf16[8,528,128]{2,1,0:T(8,128)(2,1)S(1)} %get-tuple-element.21), channel_id=1, replica_groups=mesh['row'=8,'feat'=16] {'row'}, dimensions={0} | all-to-all | bytes 2162688 | tf_op jit(solution)/shard_map/all_to_all | solution.py:336
  63.7 0.2 shard_map.60
  63.9 19.5 %all_to_all.43 = bf16[8,8,64,128]{3,2,1,0:T(8,128)(2,1)S(1)} all-to-all(bf16[8,8,64,128]{3,2,1,0:T(8,128)(2,1)S(1)} %get-tuple-element.23.refs_0_), channel_id=1, replica_groups=mesh['row'=8,'feat'=16] {'row'}, dimensions={0} | all-to-all | bytes 2097152 | tf_op jit(solution)/shard_map/all_to_all | solution.py:336
  83.4 1.2 shard_map.62
  84.6 0.1 collective-permute-start.2
  84.7 1.2 shard_map.61
  85.9 1.4 collective-permute-done.2
  87.3 0.2 add_convert_fusion
  87.5 12.9 %all_to_all.44 = bf16[32,64,128]{2,1,0:T(8,128)(2,1)S(1)} all-to-all(bf16[32,64,128]{2,1,0:T(8,128)(2,1)S(1)} %add_convert_fusion), channel_id=1, replica_groups={{0,2,4,6,8,10,12,14},{1,3,5,7,9,11,13,15},{16,18,20,22,24,26,28,30},{17..., dimensions={0} | all-to-all | bytes 1048576 | tf_op jit(solution)/shard_map/all_to_all | solution.py:333
  100.4 0.1 shard_map.63
  100.6 13.5 %all_to_all.45.scaled_ref = bf16[8,272,128]{2,1,0:T(8,128)(2,1)S(1)} all-to-all(bf16[8,272,128]{2,1,0:T(8,128)(2,1)S(1)} %shard_map.63), channel_id=1, replica_groups={{0,2,4,6,8,10,12,14},{1,3,5,7,9,11,13,15},{16,18,20,22,24,26,28,30},{17..., dimensions={0} | all-to-all | bytes 1114112 | tf_op jit(solution)/shard_map/all_to_all | solution.py:333
  114.1 0.0 collective-permute-start.3
  114.1 1.5 shard_map.64
  115.6 0.5 collective-permute-done.3.scaled_ref
  116.1 1.6 %shard_map.65 = (f32[64,64,128]{2,1,0:T(8,128)S(1)}, f32[64,8,128]{2,1,0:T(8,128)S(1)}, bf16[8,528,128]{2,1,0:T(8,128)(2,1)S(1)}) custom-call(s32[2,128]{1,0:T(2,128)S(1)} %pad.4.ids_vmem.ids_ref, bf16[64,3,128,128]{3,2,1,0:T(8,128)(2,1)S(1)} %bitcast.19, ...), custom_call_target="tpu_custom_call", output_to_operand_aliasing={{0}: (3, {}), {1}: (4, {})} | custom-call | tf_op jit(solution)/shard_map/pallas_call | solution.py:247
  117.7 20.7 %all_to_all.46.parts_ref = bf16[8,528,128]{2,1,0:T(8,128)(2,1)S(1)} all-to-all(bf16[8,528,128]{2,1,0:T(8,128)(2,1)S(1)} %get-tuple-element.27), channel_id=1, replica_groups=mesh['row'=8,'feat'=16] {'row'}, dimensions={0} | all-to-all | bytes 2162688 | tf_op jit(solution)/shard_map/all_to_all | solution.py:336
  138.4 0.2 shard_map.66
  138.7 19.5 %all_to_all.47 = bf16[8,8,64,128]{3,2,1,0:T(8,128)(2,1)S(1)} all-to-all(bf16[8,8,64,128]{3,2,1,0:T(8,128)(2,1)S(1)} %shard_map.66), channel_id=1, replica_groups=mesh['row'=8,'feat'=16] {'row'}, dimensions={0} | all-to-all | bytes 2097152 | tf_op jit(solution)/shard_map/all_to_all | solution.py:336
  158.2 1.4 shard_map.67
  (1 shorter events, 0.0 us)
Async XLA Ops:
  1.0 4.4 %copy-start = (bf16[1,8,8,3,128,128]{5,4,3,2,1,0:T(8,128)(2,1)S(1)}, bf16[1,8,8,3,128,128]{5,4,3,2,1,0:T(8,128)(2,1)}, u32[]{:S(2)}) copy-start(bf16[1,8,8,3,128,128]{5,4,3,2,1,0:T(8,128)(2,1)} %param.5) | copy-start | bytes 18874372
  4.5 2.0 %collective-permute-start = (bf16[32,64,128]{2,1,0:T(8,128)(2,1)S(1)}, bf16[32,64,128]{2,1,0:T(8,128)(2,1)S(1)}, u32[]{:S(2)}, u32[]{:S(2)}) collective-permute-start(bf16[32,64,128]{2,1,0:T(8,128)(2,1)S(1)} %get-tuple-element.18), channel_id=1, source_target_pairs={{0,1},{1,0},{2,3},{3,2},{4,5},{5,4},{6,7},{7,6},{8,9},{9,8},{10,11... | collective-permute-start | bytes 1572872 | tf_op jit(solution)/shard_map/ppermute | solution.py:330
  6.5 16.7 %copy-start.1 = (bf16[1,8,8,128,64]{3,4,2,1,0:T(8,128)(2,1)S(1)}, bf16[1,8,8,128,64]{3,4,2,1,0:T(8,128)(2,1)}, u32[]{:S(2)}) copy-start(bf16[1,8,8,128,64]{3,4,2,1,0:T(8,128)(2,1)} %param.7) | copy-start | bytes 3145732
  6.5 16.7 %copy-start.2 = (s32[8,8]{1,0:T(8,128)S(1)}, s32[8,8]{1,0:T(8,128)}, u32[]{:S(2)}) copy-start(s32[8,8]{1,0:T(8,128)} %live_ref.3) | copy-start | bytes 772
  35.5 2.0 %collective-permute-start.1 = (bf16[8,272,128]{2,1,0:T(8,128)(2,1)S(1)}, bf16[8,272,128]{2,1,0:T(8,128)(2,1)S(1)}, u32[]{:S(2)}, u32[]{:S(2)}) collective-permute-start(bf16[8,272,128]{2,1,0:T(8,128)(2,1)S(1)} %all_to_all.41.scaled_ref), channel_id=1, source_target_pairs={{0,1},{1,0},{2,3},{3,2},{4,5},{5,4},{6,7},{7,6},{8,9},{9,8},{10,11... | collective-permute-start | bytes 1671176 | tf_op jit(solution)/shard_map/ppermute | solution.py:330
  84.6 2.7 %collective-permute-start.2 = (f32[32,64,128]{2,1,0:T(8,128)S(1)}, f32[32,64,128]{2,1,0:T(8,128)S(1)}, u32[]{:S(2)}, u32[]{:S(2)}) collective-permute-start(f32[32,64,128]{2,1,0:T(8,128)S(1)} %shard_map.62), channel_id=1, source_target_pairs={{0,1},{1,0},{2,3},{3,2},{4,5},{5,4},{6,7},{7,6},{8,9},{9,8},{10,11... | collective-permute-start | bytes 3145736 | tf_op jit(solution)/shard_map/ppermute | solution.py:330
  114.1 2.0 %collective-permute-start.3 = (bf16[8,272,128]{2,1,0:T(8,128)(2,1)S(1)}, bf16[8,272,128]{2,1,0:T(8,128)(2,1)S(1)}, u32[]{:S(2)}, u32[]{:S(2)}) collective-permute-start(bf16[8,272,128]{2,1,0:T(8,128)(2,1)S(1)} %all_to_all.45.scaled_ref), channel_id=1, source_target_pairs={{0,1},{1,0},{2,3},{3,2},{4,5},{5,4},{6,7},{7,6},{8,9},{9,8},{10,11... | collective-permute-start | bytes 1671176 | tf_op jit(solution)/shard_map/ppermute | solution.py:330

commit v9 on v8

--- a/solution.py
+++ b/solution.py
@@ -63,9 +63,9 @@
     columns, features = start_t.shape
     blocks = features // width
     half = row_blocks // 2
-    step = 8
+    step = 4
     pieces = half // step
-    coef_pieces = 4
+    coef_pieces = 8
     share = features // coef_pieces
 
     def kernel(ids_vmem, tiles_hbm, start_hbm, out_ref, coef_ref, own_ref, *scratch):

time: 160 us -> 162 us (1.012)
  transfers between devices with their start and end apart: 4 -> 4, of which waited for: 3 -> 4; matrix products, arithmetic and copies ran while one was open for 0% -> 0% of each run, Pallas kernels for 3% -> 3%
where the time goes in v9:
time: 162 us
  blocking collectives  140 us (86%)
  Pallas kernels  17 us (10%)
  waiting for transfers between devices  2.91 us (2%)
    all_to_all x4, blocking collectives, exchange_row(): return lax.all_to_all(x, 'row', 0, 0, tiled=True)  84.3 us
    all_to_all x4, blocking collectives, exchange_feat(): return lax.all_to_all(x, 'feat', 0, 0, axis_index_groups=chips, tiled=True)  55.8 us
    pallas_call x4, Pallas kernels, gradient_half(): pl.pallas_call(kernel, in_specs=whole(3 + n_before, 0), out_specs=whole(l...  6.41 us
    pallas_call x1, Pallas kernels, predict_first(): pl.pallas_call(kernel, in_specs=whole(1, 0) + [hbm, hbm], out_specs=whole...  4.82 us
    pallas_call x3, Pallas kernels, predict_half(): pl.pallas_call(kernel, in_specs=whole(3, 0), out_specs=whole(1, 0)[0], ou...  3.66 us
  transfers between devices with their start and end apart: 4, of which 4 were waited for; matrix products, arithmetic and copies ran while one was open for 0% of the time, Pallas kernels for 3%

profile of v9, /device:TPU:0, one launch (start us, length us, event | category | flops | bytes accessed | tf_op | source)
XLA Modules:
  0.0 161.5 jit_solution(6619332532799260821)
XLA Ops:
  0.0 0.7 dynamic-slice_subtract_fusion
  0.7 0.1 copy.12
  0.8 0.1 sub.12
  1.0 0.0 copy-start
  1.0 4.8 %shard_map.55 = (bf16[32,64,128]{2,1,0:T(8,128)(2,1)S(1)}, bf16[64,64,128]{2,1,0:T(8,128)(2,1)S(1)}, f32[8,64,128]{2,1,0:T(8,128)S(1)}) custom-call(s32[2,128]{1,0:T(2,128)S(1)} %pad.4.ids_vmem.ids_ref, bf16[64,3,128,128]{3,2,1,0:T(8,128)(2,1)} %bitcast.12, f32[64,8192]{1,0:T(8,128)} %bitcast.28), custom_call_target="tpu_custom_call" | custom-call | tf_op jit(solution)/shard_map/pallas_call | solution.py:108
  5.8 0.1 collective-permute-start
  5.9 0.0 copy-done
  5.9 1.2 shard_map.56
  7.1 0.0 copy-start.1
  7.1 0.0 copy-start.2
  7.2 0.6 collective-permute-done
  7.8 0.1 add_convert_fusion.1
  7.9 16.5 %all_to_all.40 = bf16[32,64,128]{2,1,0:T(8,128)(2,1)S(1)} all-to-all(bf16[32,64,128]{2,1,0:T(8,128)(2,1)S(1)} %add_convert_fusion.1), channel_id=1, replica_groups={{0,2,4,6,8,10,12,14},{1,3,5,7,9,11,13,15},{16,18,20,22,24,26,28,30},{17..., dimensions={0} | all-to-all | bytes 1048576 | tf_op jit(solution)/shard_map/all_to_all | solution.py:333
  24.5 0.0 copy-done.1
  24.5 0.0 copy-done.2
  24.5 0.1 shard_map.57
  24.6 12.8 %all_to_all.41.scaled_ref = bf16[8,272,128]{2,1,0:T(8,128)(2,1)S(1)} all-to-all(bf16[8,272,128]{2,1,0:T(8,128)(2,1)S(1)} %shard_map.57), channel_id=1, replica_groups={{0,2,4,6,8,10,12,14},{1,3,5,7,9,11,13,15},{16,18,20,22,24,26,28,30},{17..., dimensions={0} | all-to-all | bytes 1114112 | tf_op jit(solution)/shard_map/all_to_all | solution.py:333
  37.4 0.0 collective-permute-start.1
  37.4 1.6 shard_map.58
  39.0 0.4 collective-permute-done.1.scaled_ref
  39.4 1.7 %shard_map.59 = (f32[64,64,128]{2,1,0:T(8,128)S(1)}, f32[64,8,128]{2,1,0:T(8,128)S(1)}, bf16[8,528,128]{2,1,0:T(8,128)(2,1)S(1)}) custom-call(s32[2,128]{1,0:T(2,128)S(1)} %pad.4.ids_vmem.ids_ref, bf16[64,3,128,128]{3,2,1,0:T(8,128)(2,1)S(1)} %bitcast.15, ...), custom_call_target="tpu_custom_call", output_to_operand_aliasing={{0}: (3, {}), {1}: (4, {})} | custom-call | tf_op jit(solution)/shard_map/pallas_call | solution.py:247
  41.1 24.5 %all_to_all.42.parts_ref = bf16[8,528,128]{2,1,0:T(8,128)(2,1)S(1)} all-to-all(bf16[8,528,128]{2,1,0:T(8,128)(2,1)S(1)} %get-tuple-element.21), channel_id=1, replica_groups=mesh['row'=8,'feat'=16] {'row'}, dimensions={0} | all-to-all | bytes 2162688 | tf_op jit(solution)/shard_map/all_to_all | solution.py:336
  65.7 0.2 shard_map.60
  65.9 19.5 %all_to_all.43 = bf16[8,8,64,128]{3,2,1,0:T(8,128)(2,1)S(1)} all-to-all(bf16[8,8,64,128]{3,2,1,0:T(8,128)(2,1)S(1)} %get-tuple-element.23.refs_0_), channel_id=1, replica_groups=mesh['row'=8,'feat'=16] {'row'}, dimensions={0} | all-to-all | bytes 2097152 | tf_op jit(solution)/shard_map/all_to_all | solution.py:336
  85.3 1.2 shard_map.62
  86.6 0.1 collective-permute-start.2
  86.7 1.2 shard_map.61
  87.9 1.4 collective-permute-done.2
  89.3 0.2 add_convert_fusion
  89.5 12.9 %all_to_all.44 = bf16[32,64,128]{2,1,0:T(8,128)(2,1)S(1)} all-to-all(bf16[32,64,128]{2,1,0:T(8,128)(2,1)S(1)} %add_convert_fusion), channel_id=1, replica_groups={{0,2,4,6,8,10,12,14},{1,3,5,7,9,11,13,15},{16,18,20,22,24,26,28,30},{17..., dimensions={0} | all-to-all | bytes 1048576 | tf_op jit(solution)/shard_map/all_to_all | solution.py:333
  102.4 0.1 shard_map.63
  102.6 13.5 %all_to_all.45.scaled_ref = bf16[8,272,128]{2,1,0:T(8,128)(2,1)S(1)} all-to-all(bf16[8,272,128]{2,1,0:T(8,128)(2,1)S(1)} %shard_map.63), channel_id=1, replica_groups={{0,2,4,6,8,10,12,14},{1,3,5,7,9,11,13,15},{16,18,20,22,24,26,28,30},{17..., dimensions={0} | all-to-all | bytes 1114112 | tf_op jit(solution)/shard_map/all_to_all | solution.py:333
  116.1 0.0 collective-permute-start.3
  116.1 1.5 shard_map.64
  117.5 0.5 collective-permute-done.3.scaled_ref
  118.0 1.6 %shard_map.65 = (f32[64,64,128]{2,1,0:T(8,128)S(1)}, f32[64,8,128]{2,1,0:T(8,128)S(1)}, bf16[8,528,128]{2,1,0:T(8,128)(2,1)S(1)}) custom-call(s32[2,128]{1,0:T(2,128)S(1)} %pad.4.ids_vmem.ids_ref, bf16[64,3,128,128]{3,2,1,0:T(8,128)(2,1)S(1)} %bitcast.19, ...), custom_call_target="tpu_custom_call", output_to_operand_aliasing={{0}: (3, {}), {1}: (4, {})} | custom-call | tf_op jit(solution)/shard_map/pallas_call | solution.py:247
  119.7 20.7 %all_to_all.46.parts_ref = bf16[8,528,128]{2,1,0:T(8,128)(2,1)S(1)} all-to-all(bf16[8,528,128]{2,1,0:T(8,128)(2,1)S(1)} %get-tuple-element.27), channel_id=1, replica_groups=mesh['row'=8,'feat'=16] {'row'}, dimensions={0} | all-to-all | bytes 2162688 | tf_op jit(solution)/shard_map/all_to_all | solution.py:336
  140.4 0.2 shard_map.66
  140.6 19.5 %all_to_all.47 = bf16[8,8,64,128]{3,2,1,0:T(8,128)(2,1)S(1)} all-to-all(bf16[8,8,64,128]{3,2,1,0:T(8,128)(2,1)S(1)} %shard_map.66), channel_id=1, replica_groups=mesh['row'=8,'feat'=16] {'row'}, dimensions={0} | all-to-all | bytes 2097152 | tf_op jit(solution)/shard_map/all_to_all | solution.py:336
  160.1 1.4 shard_map.67
  (1 shorter events, 0.0 us)
Async XLA Ops:
  1.0 4.9 %copy-start = (bf16[1,8,8,3,128,128]{5,4,3,2,1,0:T(8,128)(2,1)S(1)}, bf16[1,8,8,3,128,128]{5,4,3,2,1,0:T(8,128)(2,1)}, u32[]{:S(2)}) copy-start(bf16[1,8,8,3,128,128]{5,4,3,2,1,0:T(8,128)(2,1)} %param.5) | copy-start | bytes 18874372
  5.8 2.0 %collective-permute-start = (bf16[32,64,128]{2,1,0:T(8,128)(2,1)S(1)}, bf16[32,64,128]{2,1,0:T(8,128)(2,1)S(1)}, u32[]{:S(2)}, u32[]{:S(2)}) collective-permute-start(bf16[32,64,128]{2,1,0:T(8,128)(2,1)S(1)} %get-tuple-element.18), channel_id=1, source_target_pairs={{0,1},{1,0},{2,3},{3,2},{4,5},{5,4},{6,7},{7,6},{8,9},{9,8},{10,11... | collective-permute-start | bytes 1572872 | tf_op jit(solution)/shard_map/ppermute | solution.py:330
  7.1 17.4 %copy-start.1 = (bf16[1,8,8,128,64]{3,4,2,1,0:T(8,128)(2,1)S(1)}, bf16[1,8,8,128,64]{3,4,2,1,0:T(8,128)(2,1)}, u32[]{:S(2)}) copy-start(bf16[1,8,8,128,64]{3,4,2,1,0:T(8,128)(2,1)} %param.7) | copy-start | bytes 3145732
  7.1 17.3 %copy-start.2 = (s32[8,8]{1,0:T(8,128)S(1)}, s32[8,8]{1,0:T(8,128)}, u32[]{:S(2)}) copy-start(s32[8,8]{1,0:T(8,128)} %live_ref.3) | copy-start | bytes 772
  37.4 2.0 %collective-permute-start.1 = (bf16[8,272,128]{2,1,0:T(8,128)(2,1)S(1)}, bf16[8,272,128]{2,1,0:T(8,128)(2,1)S(1)}, u32[]{:S(2)}, u32[]{:S(2)}) collective-permute-start(bf16[8,272,128]{2,1,0:T(8,128)(2,1)S(1)} %all_to_all.41.scaled_ref), channel_id=1, source_target_pairs={{0,1},{1,0},{2,3},{3,2},{4,5},{5,4},{6,7},{7,6},{8,9},{9,8},{10,11... | collective-permute-start | bytes 1671176 | tf_op jit(solution)/shard_map/ppermute | solution.py:330
  86.6 2.7 %collective-permute-start.2 = (f32[32,64,128]{2,1,0:T(8,128)S(1)}, f32[32,64,128]{2,1,0:T(8,128)S(1)}, u32[]{:S(2)}, u32[]{:S(2)}) collective-permute-start(f32[32,64,128]{2,1,0:T(8,128)S(1)} %shard_map.62), channel_id=1, source_target_pairs={{0,1},{1,0},{2,3},{3,2},{4,5},{5,4},{6,7},{7,6},{8,9},{9,8},{10,11... | collective-permute-start | bytes 3145736 | tf_op jit(solution)/shard_map/ppermute | solution.py:330
  116.1 2.0 %collective-permute-start.3 = (bf16[8,272,128]{2,1,0:T(8,128)(2,1)S(1)}, bf16[8,272,128]{2,1,0:T(8,128)(2,1)S(1)}, u32[]{:S(2)}, u32[]{:S(2)}) collective-permute-start(bf16[8,272,128]{2,1,0:T(8,128)(2,1)S(1)} %all_to_all.45.scaled_ref), channel_id=1, source_target_pairs={{0,1},{1,0},{2,3},{3,2},{4,5},{5,4},{6,7},{7,6},{8,9},{9,8},{10,11... | collective-permute-start | bytes 1671176 | tf_op jit(solution)/shard_map/ppermute | solution.py:330
